TPU v7x, 128 devices: a whole 4x4x4 slice. The times are simulated.
128 devices in a mesh: grp: 2 (over core), ep: 32 (over z_lo, x, y), mp: 2 (over z_hi).
Axes of the slice: x: 4, y: 4, z: 4 (z_hi: 2, z_lo: 2; z = z_hi * 2 + z_lo), core: 2. Of those that a mesh axis runs over, the one named last changes fastest.
Arguments:
- teacher_rows: bfloat16 [16384, 2048], P(('grp', 'ep')), may hold values from -6 to 6
- expert_ids: int32 [16384, 2], P(('grp', 'ep')), may hold values from 0 to 31, all different within a row; in each aligned block of 256 rows (0 to 255, 256 to 511, ...) at most 32 rows name the same one
- router: bfloat16 [2048, 32], replicated, may hold values from -0.5 to 0.5
- teacher_up: bfloat16 [32, 2048, 4096], P('ep', None, 'mp'), may hold values from -0.125 to 0.125
- teacher_down: bfloat16 [32, 4096, 2048], P('ep', 'mp'), may hold values from -0.1875 to 0.1875
- student_experts: bfloat16 [2048, 1024], replicated, may hold values from -0.25 to 0.25
- student_gates: bfloat16 [2048, 48], replicated, may hold values from -0.5 to 0.5
- tower_in: bfloat16 [6, 128, 256], replicated, may hold values from -1 to 1
- tower_out: bfloat16 [6, 256], replicated, may hold values from -0.75 to 0.75
- soft_labels: float32 [16384, 6], P(('grp', 'ep', 'mp')), may hold values from 0.02 to 0.98
- label_masks: int32 [16384, 6], P(('grp', 'ep', 'mp')), may hold values 0 or 1
Outputs:
- grad_experts: float32 [2048, 1024], replicated
- grad_gates: float32 [2048, 48], replicated
- grad_tower_in: float32 [6, 128, 256], replicated
- grad_tower_out: float32 [6, 256], replicated
Inputs may be any that keep to these rules, and one draw needn't show every extreme that they name: `expert_ids`: each sample names 2 different experts. Within each block of 256 consecutive samples no expert is named by more than 32 samples, and in every draw some block names some expert exactly 32 times.
All inputs are finite; a program needn't handle non-finite values. No bound on the sum of `label_masks` on one device may be relied on, other than what follows from the above.
Results may differ from a plain program's by a relative error of at most 0.023.
The roundings to bfloat16 on the way count: a program that leaves them out, or rounds other values in their place, can miss the bound.
Values may be sent and summed in bfloat16 or wider, within the bound.
No kernel may reach another device: no remote copies, remote signals or barrier semaphores. Data moves between devices by JAX's collectives and lax.ppermute only.
A program may use at most 128 MiB of HBM per device.

v0:
```python
import math

import jax
import jax.numpy as jnp
from jax import lax
from jax.sharding import PartitionSpec as P


def partner(shard, axis, apart):
    return lax.ppermute(shard, axis, [(i, i ^ 1 << apart) for i in range(lax.axis_size(axis))])


def student_grads(
    rows_in, experts_w, gates_w, tower_w, tower_v, soft_labels, label_masks, loss_scale
):
    count_rows = rows_in.shape[0]
    task_count, expert_width, tower_width = tower_w.shape
    expert_count = gates_w.shape[1] // task_count
    pre_act = jnp.dot(rows_in, experts_w, preferred_element_type=jnp.float32)
    activation, gelu_back = jax.vjp(jax.nn.gelu, pre_act)
    act_three = activation.reshape(count_rows, expert_count, expert_width)
    gate_logit = jnp.dot(rows_in, gates_w, preferred_element_type=jnp.float32).reshape(
        count_rows, task_count, expert_count
    )
    gate_sig = jax.nn.sigmoid(gate_logit)
    gate_sum = jnp.sum(gate_sig, -1, keepdims=True)
    gate_share = gate_sig / gate_sum
    mixture = jnp.einsum("ntk,nks->nts", gate_share, act_three).astype(jnp.bfloat16)
    tower_pre = jnp.einsum("nts,tsh->nth", mixture, tower_w, preferred_element_type=jnp.float32)
    tower_sig = jax.nn.sigmoid(tower_pre)
    tower_hid = tower_pre * tower_sig
    tower_vec = tower_v.astype(jnp.float32)
    task_logit = jnp.einsum("nth,th->nt", tower_hid, tower_vec)
    logit_grad = (
        label_masks.astype(jnp.float32) * (jax.nn.sigmoid(task_logit) - soft_labels) * loss_scale
    )
    grad_tower_out = jnp.einsum("nt,nth->th", logit_grad, tower_hid)
    hid_grad = logit_grad[:, :, None] * tower_vec[None, :, :]
    tower_grad = (hid_grad * tower_sig * (1.0 + tower_pre * (1.0 - tower_sig))).astype(jnp.bfloat16)
    grad_tower_in = jnp.einsum(
        "nts,nth->tsh", mixture, tower_grad, preferred_element_type=jnp.float32
    )
    mixture_grad = jnp.einsum(
        "nth,tsh->nts", tower_grad, tower_w, preferred_element_type=jnp.float32
    )
    act_grad = jnp.einsum("ntk,nts->nks", gate_share, mixture_grad)
    share_grad = jnp.einsum("nts,nks->ntk", mixture_grad, act_three)
    sig_grad = (share_grad - jnp.sum(gate_share * share_grad, -1, keepdims=True)) / gate_sum
    gate_grad = (
        (sig_grad * gate_sig * (1.0 - gate_sig))
        .astype(jnp.bfloat16)
        .reshape(count_rows, task_count * expert_count)
    )
    grad_gates = jnp.einsum("nd,ng->dg", rows_in, gate_grad, preferred_element_type=jnp.float32)
    pre_grad = gelu_back(act_grad.reshape(count_rows, expert_count * expert_width))[0].astype(
        jnp.bfloat16
    )
    grad_experts = jnp.einsum("nd,nf->df", rows_in, pre_grad, preferred_element_type=jnp.float32)
    return (grad_experts, grad_gates, grad_tower_in, grad_tower_out)


def on_device(
    teacher_rows,
    expert_ids,
    router,
    teacher_up,
    teacher_down,
    student_experts,
    student_gates,
    tower_in,
    tower_out,
    soft_labels,
    label_masks,
):
    rows_dev, feature_dim = teacher_rows.shape
    expert_total = lax.axis_size("ep")
    width_parts = lax.axis_size("mp")
    capacity = 4 * rows_dev // expert_total
    choices_each = expert_ids.shape[1]
    logits = jnp.dot(teacher_rows, router, preferred_element_type=jnp.float32)
    onehot = (
        expert_ids[:, :, None] == jnp.arange(expert_total, dtype=jnp.int32)[None, None, :]
    ).astype(jnp.int32)
    chosen = jnp.sum(logits[:, None, :] * onehot.astype(jnp.float32), -1)
    route_sig = jax.nn.sigmoid(chosen)
    route_weight = route_sig / jnp.sum(route_sig, -1, keepdims=True)
    flat_hot = onehot.reshape(choices_each * rows_dev, expert_total)
    earlier = jnp.cumsum(flat_hot, axis=0) - flat_hot
    slot_index = jnp.sum(earlier * flat_hot, -1)
    target = expert_ids.reshape(-1) * capacity + slot_index
    sample_index = jnp.arange(choices_each * rows_dev, dtype=jnp.int32) // choices_each
    slot_table = (
        jnp.full((expert_total * capacity,), rows_dev, jnp.int32).at[target].set(sample_index)
    )
    padded = jnp.concatenate([teacher_rows, jnp.zeros((1, feature_dim), teacher_rows.dtype)], 0)
    outgoing = padded[slot_table].reshape(expert_total, capacity, feature_dim)
    up_proj = teacher_up[0]
    down_proj = teacher_down[0]
    received = lax.all_to_all(outgoing, "ep", split_axis=0, concat_axis=0, tiled=True)
    sources, items, _ = received.shape
    rows_in = received.reshape(sources * items, feature_dim)
    inner_act = jax.nn.gelu(jnp.dot(rows_in, up_proj, preferred_element_type=jnp.float32)).astype(
        jnp.bfloat16
    )
    partial_value = jnp.dot(inner_act, down_proj, preferred_element_type=jnp.float32)
    summed = lax.psum(partial_value.astype(jnp.bfloat16), "mp").astype(jnp.float32)
    expert_result = summed.astype(jnp.bfloat16).reshape(sources, items, summed.shape[1])
    returned = lax.all_to_all(expert_result, "ep", split_axis=0, concat_axis=0, tiled=True)
    picked = returned.reshape(expert_total * capacity, returned.shape[2])[target].reshape(
        rows_dev, choices_each, returned.shape[2]
    )
    mixture_rows = jnp.sum(route_weight[:, :, None] * picked.astype(jnp.float32), 1).astype(
        jnp.bfloat16
    )
    relayed = partner(mixture_rows, "grp", 0)
    half_rows = rows_dev // width_parts
    own_rows = lax.dynamic_slice_in_dim(relayed, lax.axis_index("mp") * half_rows, half_rows, 0)
    sample_total = rows_dev * lax.axis_size("grp") * expert_total
    loss_scale = 1.0 / math.sqrt(sample_total)
    grad_parts = student_grads(
        own_rows,
        student_experts,
        student_gates,
        tower_in,
        tower_out,
        soft_labels,
        label_masks,
        loss_scale,
    )
    summed_grads = lax.psum(
        (grad_parts[0], grad_parts[1], grad_parts[2], grad_parts[3]), ("grp", "ep", "mp")
    )
    return (summed_grads[0], summed_grads[1], summed_grads[2], summed_grads[3])


def solution(mesh):
    return jax.shard_map(
        on_device,
        mesh=mesh,
        in_specs=(
            P(("grp", "ep"), None),
            P(("grp", "ep"), None),
            P(),
            P("ep", None, "mp"),
            P("ep", "mp", None),
            P(),
            P(),
            P(),
            P(),
            P(("grp", "ep", "mp"), None),
            P(("grp", "ep", "mp"), None),
        ),
        out_specs=(P(), P(), P(), P()),
        check_vma=False,
    )
```

profile of v0, /device:TPU:1, one launch (start us, length us, event | category | flops | bytes accessed | tf_op | source)
XLA Modules:
  0.0 503.0 jit_solution(3441356995214056869)
XLA Ops:
  7.2 0.7 broadcast_multiply_fusion
  8.0 0.8 copy.53
  9.4 1.2 reduce-window.6
  10.9 2.4 scatter_custom_fusion
  13.4 1.3 concatenate.3
  14.7 6.0 %gather_fusion = bf16[1024,2048]{1,0:T(8,128)(2,1)} fusion(bf16[257,2048]{1,0:T(8,128)(2,1)S(1)} %concatenate.3, s32[1024]{0:T(1024)S(1)} %fusion.72), kind=kCustom, calls=%fused_computation | custom fusion | bytes 8392704 | tf_op jit(solution)/shard_map/gather | solution.py:96
  20.7 58.3 %all_to_all.10 = bf16[32,32,2048]{2,1,0:T(8,128)(2,1)} all-to-all(bf16[32,32,2048]{2,1,0:T(8,128)(2,1)} %bitcast.105), channel_id=1, replica_groups=mesh['grp'=2,'ep'=32,'mp'=2] {'ep'}, dimensions={0} | all-to-all | bytes 8388608 | tf_op jit(solution)/shard_map/all_to_all | solution.py:99
  79.0 25.4 %fusion.15 = bf16[1024,2048]{1,0:T(8,128)(2,1)} fusion(bf16[1,2048,2048]{2,1,0:T(8,128)(2,1)} %param.15, bf16[1024,2048]{1,0:T(8,128)(2,1)} %bitcast.107, bf16[1,2048,2048]{2,1,0:T(8,128)(2,1)} %param.14), kind=kOutput, calls=%fused_computation.18 | convolution fusion | flops 17200840704 | bytes 25165824 | tf_op jit(solution)/shard_map/dot_general | solution.py:105
  104.5 117.0 %all-reduce.5.cloned.1.call-done = bf16[32,32,2048]{2,1,0:T(8,128)(2,1)} async-done(((bf16[32,32,2048]{2,1,0:T(8,128)(2,1)}), bf16[32,32,2048]{2,1,0:T(8,128)(2,1)}) %all-reduce.5.cloned.1.call-update) | async-done | bytes 4194320 | tf_op jit(solution)/shard_map/psum | solution.py:106
  221.5 7.0 %all-to-all-start.1 = ((bf16[32,32,2048]{2,1,0:T(8,128)(2,1)}), bf16[32,32,2048]{2,1,0:T(8,128)(2,1)}, u32[]{:S(2)}, u32[]{:S(2)}) async-start(bf16[32,32,2048]{2,1,0:T(8,128)(2,1)} %all-reduce.5.cloned.1.call-done), calls=%async_computation.1 | async-start | bytes 8388608 | tf_op jit(solution)/shard_map/all_to_all | solution.py:108
  228.8 0.4 fusion.98
  229.5 52.0 %all-to-all-done.1 = bf16[32,32,2048]{2,1,0:T(8,128)(2,1)} async-done(((bf16[32,32,2048]{2,1,0:T(8,128)(2,1)}), bf16[32,32,2048]{2,1,0:T(8,128)(2,1)}, u32[]{:S(2)}, u32[]{:S(2)}) %all-to-all-start.1) | async-done | bytes 4194336 | tf_op jit(solution)/shard_map/all_to_all | solution.py:108
  281.4 7.1 %gather_fusion.1 = bf16[512,2048]{1,0:T(8,128)(2,1)S(1)} fusion(bf16[1024,2048]{1,0:T(8,128)(2,1)} %bitcast.8, s32[1024]{0:T(1024)S(1)} %pad_clamp_fusion), kind=kCustom, calls=%fused_computation.1 | custom fusion | bytes 4196352 | tf_op jit(solution)/shard_map/gather | solution.py:109
  288.6 3.9 reshape.118
  292.5 8.9 %multiply_reduce_fusion = bf16[256,2048]{1,0:T(8,128)(2,1)S(1)} fusion(f32[256,2,2048]{2,1,0:T(2,128)} %reshape.118, f32[256,2]{1,0:T(8,128)S(1)} %copy.51), kind=kLoop, calls=%fused_computation.17 | loop fusion | flops 1572864 | bytes 5244928 | tf_op jit(solution)/shard_map/reduce_sum | solution.py:112
  301.4 3.1 collective-permute-start
  304.5 2.3 collective-permute-done
  306.8 0.3 fusion.69
  307.3 2.9 fusion.46
  310.5 0.4 fusion.99
  311.1 0.3 fusion.58
  311.5 0.5 convolution_bitcast_fusion.1
  312.0 1.4 fusion.70
  314.1 1.0 fusion.28
  315.1 4.8 fusion.44
  319.9 1.1 copy-done.4
  321.0 0.3 fusion.56
  321.4 68.8 %psum.39 = f32[6,256]{1,0:T(8,128)} all-reduce(f32[6,256]{1,0:T(8,128)S(1)} %bitcast.111), channel_id=1, replica_groups=mesh['grp'=2,'ep'=32,'mp'=2] {'grp','ep','mp'}, use_global_device_ids=true, to_apply=%region_13.14 | all-reduce | flops 1536 | bytes 12288 | tf_op jit(solution)/shard_map/psum | solution.py:130
  390.2 95.8 %all-reduce.7.cloned.1.call-done = (f32[2048,1024]{1,0:T(8,128)}, f32[2048,48]{0,1:T(8,128)}, f32[6,128,256]{2,1,0:T(8,128)}) async-done(((f32[2048,1024]{1,0:T(8,128)}, f32[2048,48]{0,1:T(8,128)}, f32[6,128,256]{2,1,0:T(8,128)}), (f32[2048,1024]{1,0:T(8,128)}, f32[2048,48]{0,1:T(8,128)}, f32[6,128,256]{2,1,0:T(8,128)})) %all-reduce.7.cloned.1.call-update) | async-done | bytes 9568272 | tf_op jit(solution)/shard_map/psum | solution.py:130
  486.0 8.5 %copy.93 = f32[2048,1024]{1,0:T(8,128)} copy(f32[2048,1024]{1,0:T(8,128)} %get-tuple-element.9) | data formatting | bytes 16777216
  494.6 0.7 copy.94
  495.3 0.9 copy.95
  (55 shorter events, 3.0 us)
Async XLA Ops:
  7.2 303.7 %copy-start = (bf16[6,128,256]{2,1,0:T(8,128)(2,1)S(1)}, bf16[6,128,256]{2,1,0:T(8,128)(2,1)}, u32[]{:S(2)}) copy-start(bf16[6,128,256]{2,1,0:T(8,128)(2,1)} %param.18) | copy-start | bytes 1179652
  7.2 214.3 %all-reduce.5.cloned.1.call-start = ((), (), s32[]{:S(2)}) async-start(), calls=%async_computation.2 | async-start | bytes 8388608 | tf_op jit(solution)/shard_map/psum | solution.py:106
  104.4 124.4 %copy-start.1 = (bf16[256,2048]{1,0:T(8,128)(2,1)S(1)}, bf16[256,2048]{1,0:T(8,128)(2,1)}, u32[]{:S(2)}) copy-start(bf16[256,2048]{1,0:T(8,128)(2,1)} %param.11) | copy-start | bytes 3145732
  104.4 124.4 %copy-start.7 = (bf16[2048,32]{0,1:T(8,128)(2,1)S(1)}, bf16[2048,32]{0,1:T(8,128)(2,1)}, u32[]{:S(2)}) copy-start(bf16[2048,32]{0,1:T(8,128)(2,1)} %param.13) | copy-start | bytes 393220
  104.4 124.8 %copy-start.8 = (s32[256,2]{0,1:T(2,128)S(1)}, s32[256,2]{0,1:T(2,128)}, u32[]{:S(2)}) copy-start(s32[256,2]{0,1:T(2,128)} %param.12) | copy-start | bytes 6148
  221.5 59.9 %all-to-all-start.1 = ((bf16[32,32,2048]{2,1,0:T(8,128)(2,1)}), bf16[32,32,2048]{2,1,0:T(8,128)(2,1)}, u32[]{:S(2)}, u32[]{:S(2)}) async-start(bf16[32,32,2048]{2,1,0:T(8,128)(2,1)} %all-reduce.5.cloned.1.call-done), calls=%async_computation.1 | async-start | bytes 8388608 | tf_op jit(solution)/shard_map/all_to_all | solution.py:108
  228.5 257.5 %all-reduce.7.cloned.1.call-start = ((), (), s32[]{:S(2)}) async-start(), calls=%async_computation.3 | async-start | bytes 19136512 | tf_op jit(solution)/shard_map/psum | solution.py:130
  292.5 12.0 %copy-start.9 = (bf16[6,256]{1,0:T(8,128)(2,1)S(1)}, bf16[6,256]{1,0:T(8,128)(2,1)}, u32[]{:S(2)}) copy-start(bf16[6,256]{1,0:T(8,128)(2,1)} %param.19) | copy-start | bytes 9220
  292.5 14.2 %copy-start.6 = (bf16[2048,48]{0,1:T(8,128)(2,1)S(1)}, bf16[2048,48]{0,1:T(8,128)(2,1)}, u32[]{:S(2)}) copy-start(bf16[2048,48]{0,1:T(8,128)(2,1)} %param.17) | copy-start | bytes 589828
  301.4 5.3 %collective-permute-start = (bf16[256,2048]{1,0:T(8,128)(2,1)S(1)}, bf16[256,2048]{1,0:T(8,128)(2,1)S(1)}, u32[]{:S(2)}, u32[]{:S(2)}) collective-permute-start(bf16[256,2048]{1,0:T(8,128)(2,1)S(1)} %multiply_reduce_fusion), channel_id=1, source_target_pairs={{0,64},{64,0},{1,65},{65,1},{2,66},{66,2},{3,67},{67,3},{4,68},{68... | collective-permute-start | bytes 3145736 | tf_op jit(solution)/shard_map/ppermute | solution.py:10
  310.2 1.2 copy-start.10
  310.2 1.2 copy-start.11
  311.1 0.9 copy-start.3
  319.9 1.1 copy-start.4
  486.0 8.5 %copy-start.5 = (f32[2048,48]{0,1:T(8,128)S(1)}, f32[2048,48]{0,1:T(8,128)}, u32[]{:S(2)}) copy-start(f32[2048,48]{0,1:T(8,128)} %get-tuple-element.10) | copy-start | bytes 1179652
  486.0 9.3 %copy-start.2 = (f32[6,128,256]{2,1,0:T(8,128)S(1)}, f32[6,128,256]{2,1,0:T(8,128)}, u32[]{:S(2)}) copy-start(f32[6,128,256]{2,1,0:T(8,128)} %get-tuple-element.11) | copy-start | bytes 2359300
Sparse Core Ops, SparseCore 0:
  104.5 116.9 all-reduce.4
  320.1 165.9 all-reduce.6
where the time goes:
time: 504 us; the launch traced here: 503 us
  waiting for transfers between devices  267 us (53%)
  blocking collectives  127 us (25%)
  matrix products  38.5 us (8%)
  local copies, waits for them, and re-layouts  34.3 us (7%)
  between operations  14.3 us (3%)
  other arithmetic  11.2 us (2%)
  starting transfers between devices  10.3 us (2%)
    psum x1, waiting for transfers between devices, on_device(): lax.psum(partial_value.astype(jnp.bfloat16), 'mp').astype(jnp.float32)  117 us
    psum x1, waiting for transfers between devices, on_device(): lax.psum((grad_parts[0], grad_parts[1], grad_parts[2], grad_parts[3]), ('...  95.8 us
    psum x1, blocking collectives, on_device(): lax.psum((grad_parts[0], grad_parts[1], grad_parts[2], grad_parts[3]), ('...  68.8 us
    all_to_all x1, blocking collectives, on_device(): lax.all_to_all(outgoing, 'ep', split_axis=0, concat_axis=0, tiled=True)  58.3 us
    all_to_all x1, waiting for transfers between devices, on_device(): lax.all_to_all(expert_result, 'ep', split_axis=0, concat_axis=0, tiled=True)  52 us
    dot_general x1, matrix products, on_device(): jnp.dot(inner_act, down_proj, preferred_element_type=jnp.float32)  25.4 us
    unnamed x29, local copies, waits for them, and re-layouts  12.2 us
  transfers between devices with their start and end apart: 4, of which 4 were waited for; matrix products, arithmetic and copies ran while one was open for 0% of the time, Pallas kernels for 0%

commit v1 on v0

v1 whole, which is shorter than its diff:
```python
import math

import jax
import jax.numpy as jnp
from jax import lax
from jax.sharding import PartitionSpec as P

F32 = jnp.float32
BF16 = jnp.bfloat16
SLOT_CHUNKS = 2
CHIPS = ("ep", "mp")


def swap(shard, axis):
    return lax.ppermute(shard, axis, [(0, 1), (1, 0)])


def student_grads(rows_in, experts_w, gates_w, tower_w, tower_v, soft_labels, masks, loss_scale):
    count_rows = rows_in.shape[0]
    task_count, expert_width, tower_width = tower_w.shape
    expert_count = gates_w.shape[1] // task_count
    pre_act = jnp.dot(rows_in, experts_w, preferred_element_type=F32)
    activation, gelu_back = jax.vjp(jax.nn.gelu, pre_act)
    act_three = activation.reshape(count_rows, expert_count, expert_width)
    gate_logit = jnp.dot(rows_in, gates_w, preferred_element_type=F32).reshape(
        count_rows, task_count, expert_count
    )
    gate_sig = jax.nn.sigmoid(gate_logit)
    gate_sum = jnp.sum(gate_sig, -1, keepdims=True)
    gate_share = gate_sig / gate_sum
    mixture = jnp.einsum("ntk,nks->nts", gate_share, act_three).astype(BF16)
    tower_pre = jnp.einsum("nts,tsh->nth", mixture, tower_w, preferred_element_type=F32)
    tower_sig = jax.nn.sigmoid(tower_pre)
    tower_hid = tower_pre * tower_sig
    tower_vec = tower_v.astype(F32)
    task_logit = jnp.einsum("nth,th->nt", tower_hid, tower_vec)
    logit_grad = masks * (jax.nn.sigmoid(task_logit) - soft_labels) * loss_scale
    grad_tower_out = jnp.einsum("nt,nth->th", logit_grad, tower_hid)
    hid_grad = logit_grad[:, :, None] * tower_vec[None, :, :]
    tower_grad = (hid_grad * tower_sig * (1.0 + tower_pre * (1.0 - tower_sig))).astype(BF16)
    grad_tower_in = jnp.einsum("nts,nth->tsh", mixture, tower_grad, preferred_element_type=F32)
    mixture_grad = jnp.einsum("nth,tsh->nts", tower_grad, tower_w, preferred_element_type=F32)
    act_grad = jnp.einsum("ntk,nts->nks", gate_share, mixture_grad)
    share_grad = jnp.einsum("nts,nks->ntk", mixture_grad, act_three)
    sig_grad = (share_grad - jnp.sum(gate_share * share_grad, -1, keepdims=True)) / gate_sum
    gate_grad = (
        (sig_grad * gate_sig * (1.0 - gate_sig))
        .astype(BF16)
        .reshape(count_rows, task_count * expert_count)
    )
    pre_grad = gelu_back(act_grad.reshape(count_rows, expert_count * expert_width))[0].astype(BF16)
    return pre_grad, gate_grad, grad_tower_in, grad_tower_out


def on_device(
    teacher_rows,
    expert_ids,
    router,
    teacher_up,
    teacher_down,
    student_experts,
    student_gates,
    tower_in,
    tower_out,
    soft_labels,
    label_masks,
):
    rows_dev, feature_dim = teacher_rows.shape
    expert_total = lax.axis_size("ep")
    width_parts = lax.axis_size("mp")
    group_index = lax.axis_index("grp")
    chips = expert_total * width_parts
    capacity = 4 * rows_dev // expert_total
    chunk_slots = capacity // SLOT_CHUNKS

    labels = swap(jnp.concatenate([soft_labels, label_masks.astype(F32)], 1), "grp")
    task_count = soft_labels.shape[1]

    experts = jnp.arange(expert_total, dtype=jnp.int32)
    hot = [(expert_ids[:, c : c + 1] == experts[None, :]) for c in range(2)]
    named = (hot[0] | hot[1]).astype(BF16)
    sample = jnp.arange(rows_dev, dtype=jnp.int32)
    before = (sample[None, :] < sample[:, None]).astype(BF16)
    earlier = jnp.dot(before, named, preferred_element_type=F32)
    slots = [jnp.sum(jnp.where(h, earlier, 0.0), 1, keepdims=True).astype(jnp.int32) for h in hot]

    def places(chunk):
        found = []
        for c in range(2):
            local = slots[c] - chunk * chunk_slots
            inside = (local >= 0) & (local < chunk_slots)
            found.append(jnp.where(inside, expert_ids[:, c : c + 1] * chunk_slots + local, -1))
        return found

    lane = jnp.arange(expert_total * chunk_slots, dtype=jnp.int32)[None, :]
    targets = [places(chunk) for chunk in range(SLOT_CHUNKS)]

    received = []
    for first, second in targets:
        pick = ((lane == first) | (lane == second)).astype(BF16)
        outgoing = lax.dot_general(
            pick, teacher_rows, (((0,), (0,)), ((), ())), preferred_element_type=F32
        ).astype(BF16)
        outgoing = outgoing.reshape(expert_total, chunk_slots, feature_dim)
        received.append(lax.all_to_all(outgoing, "ep", split_axis=0, concat_axis=0, tiled=True))

    logits = jnp.dot(teacher_rows, router, preferred_element_type=F32)
    chosen = [jnp.sum(jnp.where(h, logits, 0.0), 1, keepdims=True) for h in hot]
    sigs = [jax.nn.sigmoid(v) for v in chosen]
    weights = [v / (sigs[0] + sigs[1]) for v in sigs]

    up_proj = teacher_up[0]
    down_proj = teacher_down[0]
    mixed = jnp.zeros((rows_dev, feature_dim), F32)
    for chunk in range(SLOT_CHUNKS):
        rows_in = received[chunk].reshape(expert_total * chunk_slots, feature_dim)
        inner = jax.nn.gelu(jnp.dot(rows_in, up_proj, preferred_element_type=F32)).astype(BF16)
        partial = jnp.dot(inner, down_proj, preferred_element_type=F32).astype(BF16)
        returned = lax.all_to_all(
            partial.reshape(expert_total, chunk_slots, feature_dim),
            "ep",
            split_axis=0,
            concat_axis=0,
            tiled=True,
        ).reshape(expert_total * chunk_slots, feature_dim)
        first, second = targets[chunk]
        share = jnp.where(lane == first, weights[0], 0.0) + jnp.where(
            lane == second, weights[1], 0.0
        )
        high = share.astype(BF16)
        low = (share - high.astype(F32)).astype(BF16)
        mixed = mixed + jnp.dot(high, returned, preferred_element_type=F32)
        mixed = mixed + jnp.dot(low, returned, preferred_element_type=F32)
    mixed = mixed.astype(BF16)

    half_rows = rows_dev // width_parts
    part = lax.axis_index("mp")
    kept = lax.dynamic_slice_in_dim(mixed, part * half_rows, half_rows, 0)
    given = lax.dynamic_slice_in_dim(mixed, (1 - part) * half_rows, half_rows, 0)
    own_rows = (kept.astype(F32) + swap(given, "mp").astype(F32)).astype(BF16)
    other_rows = swap(own_rows, "grp")

    sample_total = rows_dev * lax.axis_size("grp") * expert_total
    pre_grad, gate_grad, grad_tower_in, grad_tower_out = student_grads(
        own_rows,
        student_experts,
        student_gates,
        tower_in,
        tower_out,
        labels[:, :task_count],
        labels[:, task_count:],
        1.0 / math.sqrt(sample_total),
    )

    def halves(array, axis):
        size = array.shape[axis] // 2
        mine = lax.dynamic_slice_in_dim(array, group_index * size, size, axis)
        theirs = lax.dynamic_slice_in_dim(array, (1 - group_index) * size, size, axis)
        return mine, theirs

    both_rows = jnp.concatenate([own_rows, other_rows], 0)
    mine, theirs = halves(pre_grad, 1)
    pre_both = jnp.concatenate([mine, swap(theirs, "grp")], 0)
    mine, theirs = halves(gate_grad, 1)
    gate_both = jnp.concatenate([mine, swap(theirs, "grp")], 0)
    contract = (((0,), (0,)), ((), ()))
    main = lax.dot_general(both_rows, pre_both, contract, preferred_element_type=F32).astype(BF16)
    gates = lax.dot_general(gate_both, both_rows, contract, preferred_element_type=F32)
    mine, theirs = halves(grad_tower_in.astype(BF16), 0)
    tower = mine.astype(F32) + swap(theirs, "grp").astype(F32)
    mine, theirs = halves(grad_tower_out.astype(BF16), 0)
    vector = mine.astype(F32) + swap(theirs, "grp").astype(F32)

    width = main.shape[1]
    tower_rows = tower.reshape(-1, tower.shape[2])
    tower_half = tower_rows.shape[0] // 2
    tower_block = jnp.concatenate([tower_rows[:tower_half], tower_rows[tower_half:]], 1)
    gate_block = gates.reshape(-1, width)
    vector_flat = vector.reshape(-1)
    vector_rows = -(-vector_flat.shape[0] // width)
    vector_block = jnp.pad(vector_flat, (0, vector_rows * width - vector_flat.shape[0]))
    small = jnp.concatenate(
        [tower_block, gate_block, vector_block.reshape(vector_rows, width)], 0
    ).astype(BF16)
    small_each = -(-small.shape[0] // (8 * chips)) * 8
    small = jnp.pad(small, ((0, small_each * chips - small.shape[0]), (0, 0)))
    main_each = main.shape[0] // chips
    packed = jnp.concatenate(
        [main.reshape(chips, main_each, width), small.reshape(chips, small_each, width)], 1
    )

    parts = lax.all_to_all(packed, CHIPS, split_axis=0, concat_axis=0, tiled=True)
    total = jnp.sum(parts.astype(F32), 0).astype(BF16)
    spread = jnp.broadcast_to(total[None], packed.shape)
    own_half = lax.all_to_all(spread, CHIPS, split_axis=0, concat_axis=0, tiled=True)
    other_half = swap(own_half, "grp")
    low_half = jnp.where(group_index == 0, own_half, other_half)
    high_half = jnp.where(group_index == 0, other_half, own_half)

    main_halves, tower_halves, gate_halves, vector_halves = [], [], [], []
    for half in (low_half, high_half):
        main_halves.append(half[:, :main_each].reshape(-1, width))
        rest = half[:, main_each:].reshape(-1, width)
        block = rest[:tower_half]
        tower_width = tower.shape[2]
        tower_halves.append(
            jnp.concatenate([block[:, :tower_width], block[:, tower_width:]], 0).reshape(
                tower.shape
            )
        )
        at = tower_half
        gate_halves.append(rest[at : at + gate_block.shape[0]].reshape(gates.shape))
        at += gate_block.shape[0]
        vector_halves.append(
            rest[at : at + vector_rows].reshape(-1)[: vector_flat.shape[0]].reshape(vector.shape)
        )
    return (
        jnp.concatenate(main_halves, 1).astype(F32),
        jnp.concatenate(gate_halves, 0).astype(F32).T,
        jnp.concatenate(tower_halves, 0).astype(F32),
        jnp.concatenate(vector_halves, 0).astype(F32),
    )


def solution(mesh):
    return jax.shard_map(
        on_device,
        mesh=mesh,
        in_specs=(
            P(("grp", "ep"), None),
            P(("grp", "ep"), None),
            P(),
            P("ep", None, "mp"),
            P("ep", "mp", None),
            P(),
            P(),
            P(),
            P(),
            P(("grp", "ep", "mp"), None),
            P(("grp", "ep", "mp"), None),
        ),
        out_specs=(P(), P(), P(), P()),
        check_vma=False,
    )
```

time: 504 us -> 278 us (0.55)
  waiting for transfers between devices: 267 us -> 76.2 us
  blocking collectives: 127 us -> 82.7 us
  starting transfers between devices: 10.3 us -> 44.3 us
  local copies, waits for them, and re-layouts: 34.3 us -> 5.77 us
  matrix products: 38.5 us -> 55.6 us
  between operations: 14.3 us -> 1.11 us
    psum x2 -> x0, waiting for transfers between devices: 213 us -> none  [the longest x1 117 us: on_device(): lax.psum(partial_value.astype(jnp.bfloat16), 'mp').astype(jnp.float32)]
    psum x1 -> x0, blocking collectives: 68.8 us -> none  [on_device(): lax.psum((grad_parts[0], grad_parts[1], grad_parts[2], grad_parts[3]), ('...]
    all_to_all x1 -> x2, blocking collectives: 58.3 us -> 82.7 us  [the longest x1 43.3 us: on_device(): lax.all_to_all(packed, CHIPS, split_axis=0, concat_axis=0, tiled=True)]
    all_to_all x1 -> x4, starting transfers between devices: 7.03 us -> 30.7 us  [the longest x2 15.9 us: on_device(): lax.all_to_all(outgoing, 'ep', split_axis=0, concat_axis=0, tiled=True)]
    dot_general x10 -> x18, matrix products: 37.3 us -> 54.4 us  [the longest x2 32.5 us: on_device(): partial = jnp.dot(inner, down_proj, preferred_element_type=F32).astype(BF16)]
    gather x2 -> x0, local copies, waits for them, and re-layouts: 13.1 us -> none  [the longest x1 7.13 us: on_device(): returned.reshape(expert_total * capacity, returned.shape[2])[target]]
    all_to_all x1 -> x4, waiting for transfers between devices: 52 us -> 64.7 us  [the longest x2 33.9 us: on_device(): lax.all_to_all(outgoing, 'ep', split_axis=0, concat_axis=0, tiled=True)]
    unnamed x29 -> x17, local copies, waits for them, and re-layouts: 12.2 us -> 0.55 us
  transfers between devices with their start and end apart: 4 -> 12, of which waited for: 4 -> 6; matrix products, arithmetic and copies ran while one was open for 0% -> 17% of each run, Pallas kernels for 0% -> 0%
where the time goes in v1:
time: 278 us; the launch traced here: 277 us
  blocking collectives  82.7 us (30%)
  waiting for transfers between devices  76.2 us (27%)
  matrix products  55.6 us (20%)
  starting transfers between devices  44.3 us (16%)
  other arithmetic  11.6 us (4%)
  local copies, waits for them, and re-layouts  5.77 us (2%)
    all_to_all x1, blocking collectives, on_device(): lax.all_to_all(packed, CHIPS, split_axis=0, concat_axis=0, tiled=True)  43.3 us
    all_to_all x1, blocking collectives, on_device(): lax.all_to_all(spread, CHIPS, split_axis=0, concat_axis=0, tiled=True)  39.5 us
    all_to_all x2, waiting for transfers between devices, on_device(): lax.all_to_all(outgoing, 'ep', split_axis=0, concat_axis=0, tiled=True)  33.9 us
    dot_general x2, matrix products, on_device(): partial = jnp.dot(inner, down_proj, preferred_element_type=F32).astype(BF16)  32.5 us
    all_to_all x2, waiting for transfers between devices, on_device(): lax.all_to_all(partial.reshape(expert_total, chunk_slots, feature_dim), '...  30.8 us
    all_to_all x2, starting transfers between devices, on_device(): lax.all_to_all(outgoing, 'ep', split_axis=0, concat_axis=0, tiled=True)  15.9 us
    all_to_all x2, starting transfers between devices, on_device(): lax.all_to_all(partial.reshape(expert_total, chunk_slots, feature_dim), '...  14.9 us
    ppermute x8, starting transfers between devices, swap(): return lax.ppermute(shard, axis, [(0, 1), (1, 0)])  13.5 us
  transfers between devices with their start and end apart: 12, of which 6 were waited for; matrix products, arithmetic and copies ran while one was open for 17% of the time, Pallas kernels for 0%

profile of v1, /device:TPU:1, one launch (start us, length us, event | category | flops | bytes accessed | tf_op | source)
XLA Modules:
  0.0 277.3 jit_solution(16641592192123862863)
XLA Ops:
  1.9 1.3 fusion.149
  4.2 2.2 convolution_convert_fusion.2
  6.4 9.2 %all-to-all-start = ((bf16[32,16,2048]{2,1,0:T(8,128)(2,1)}), bf16[32,16,2048]{2,1,0:T(8,128)(2,1)S(1)}, u32[]{:S(2)}, u32[]{:S(2)}) async-start(bf16[32,16,2048]{2,1,0:T(8,128)(2,1)} %bitcast.6), calls=%async_computation | async-start | bytes 4194304 | tf_op jit(solution)/shard_map/all_to_all | solution.py:105
  15.6 2.2 convolution_convert_fusion.1
  17.9 24.3 %all-to-all-done = bf16[32,16,2048]{2,1,0:T(8,128)(2,1)S(1)} async-done(((bf16[32,16,2048]{2,1,0:T(8,128)(2,1)}), bf16[32,16,2048]{2,1,0:T(8,128)(2,1)S(1)}, u32[]{:S(2)}, u32[]{:S(2)}) %all-to-all-start) | async-done | bytes 2097184 | tf_op jit(solution)/shard_map/all_to_all | solution.py:105
  42.2 6.6 %all-to-all-start.2 = ((bf16[32,16,2048]{2,1,0:T(8,128)(2,1)}), bf16[32,16,2048]{2,1,0:T(8,128)(2,1)}, u32[]{:S(2)}, u32[]{:S(2)}) async-start(bf16[32,16,2048]{2,1,0:T(8,128)(2,1)} %bitcast.14), calls=%async_computation.2 | async-start | bytes 4194304 | tf_op jit(solution)/shard_map/all_to_all | solution.py:105
  48.8 15.9 %fusion.25 = bf16[512,2048]{1,0:T(8,128)(2,1)} fusion(bf16[1,2048,2048]{2,1,0:T(8,128)(2,1)} %param.15, bf16[512,2048]{1,0:T(8,128)(2,1)S(1)} %bitcast.129, bf16[1,2048,2048]{2,1,0:T(8,128)(2,1)} %param.14), kind=kOutput, calls=%fused_computation.31 | convolution fusion | flops 8600420352 | bytes 20971520 | tf_op jit(solution)/shard_map/dot_general | solution.py:118
  64.8 9.6 %all-to-all-done.2 = bf16[32,16,2048]{2,1,0:T(8,128)(2,1)} async-done(((bf16[32,16,2048]{2,1,0:T(8,128)(2,1)}), bf16[32,16,2048]{2,1,0:T(8,128)(2,1)}, u32[]{:S(2)}, u32[]{:S(2)}) %all-to-all-start.2) | async-done | bytes 2097184 | tf_op jit(solution)/shard_map/all_to_all | solution.py:105
  74.3 5.8 %all-to-all-start.1 = ((bf16[32,16,2048]{2,1,0:T(8,128)(2,1)}), bf16[32,16,2048]{2,1,0:T(8,128)(2,1)S(1)}, u32[]{:S(2)}, u32[]{:S(2)}) async-start(bf16[32,16,2048]{2,1,0:T(8,128)(2,1)} %bitcast.130), calls=%async_computation.1 | async-start | bytes 4194304 | tf_op jit(solution)/shard_map/all_to_all | solution.py:119
  80.2 16.5 %fusion.28 = bf16[512,2048]{1,0:T(8,128)(2,1)} fusion(bf16[1,2048,2048]{2,1,0:T(8,128)(2,1)} %param.15, bf16[512,2048]{1,0:T(8,128)(2,1)} %bitcast.15, bf16[1,2048,2048]{2,1,0:T(8,128)(2,1)} %param.14), kind=kOutput, calls=%fused_computation.32 | convolution fusion | flops 8600420352 | bytes 20971520 | tf_op jit(solution)/shard_map/dot_general | solution.py:118
  96.7 6.8 %all-to-all-done.1 = bf16[32,16,2048]{2,1,0:T(8,128)(2,1)S(1)} async-done(((bf16[32,16,2048]{2,1,0:T(8,128)(2,1)}), bf16[32,16,2048]{2,1,0:T(8,128)(2,1)S(1)}, u32[]{:S(2)}, u32[]{:S(2)}) %all-to-all-start.1) | async-done | bytes 2097184 | tf_op jit(solution)/shard_map/all_to_all | solution.py:119
  103.5 9.1 %all-to-all-start.3 = ((bf16[32,16,2048]{2,1,0:T(8,128)(2,1)}), bf16[32,16,2048]{2,1,0:T(8,128)(2,1)}, u32[]{:S(2)}, u32[]{:S(2)}) async-start(bf16[32,16,2048]{2,1,0:T(8,128)(2,1)} %bitcast.128), calls=%async_computation.3 | async-start | bytes 4194304 | tf_op jit(solution)/shard_map/all_to_all | solution.py:119
  113.5 2.2 convolution_add_fusion.2
  115.6 24.0 %all-to-all-done.3 = bf16[32,16,2048]{2,1,0:T(8,128)(2,1)} async-done(((bf16[32,16,2048]{2,1,0:T(8,128)(2,1)}), bf16[32,16,2048]{2,1,0:T(8,128)(2,1)}, u32[]{:S(2)}, u32[]{:S(2)}) %all-to-all-start.3) | async-done | bytes 2097184 | tf_op jit(solution)/shard_map/all_to_all | solution.py:119
  139.7 3.0 %convolution_add_fusion.1 = f32[256,2048]{1,0:T(8,128)S(1)} fusion(f32[256,2048]{1,0:T(8,128)} %convolution_add_fusion.2, bf16[512,2048]{1,0:T(8,128)(2,1)} %bitcast.17, s32[256]{0:T(256)S(1)} %bitcast.146, s32[256]{0:T(256)S(1)} %bitcast.143, f32[256]{0:T(256)S(1)} %multiply_divide_fusion.1, f32[256]{0:T(256)S(1)} %get-tuple-element.10), kind=kOutput, calls=%fused_computation.34 | convolution fusion | flops 538181632 | bytes 6295552 | tf_op jit(solution)/shard_map/dot_general | solution.py:132
  142.7 2.5 fusion.35
  145.3 3.3 %collective-permute-start = (bf16[128,2048]{1,0:T(8,128)(2,1)S(1)}, bf16[128,2048]{1,0:T(8,128)(2,1)S(1)}, u32[]{:S(2)}, u32[]{:S(2)}) collective-permute-start(bf16[128,2048]{1,0:T(8,128)(2,1)S(1)} %constant_dynamic-slice_fusion.7), channel_id=1, source_target_pairs={{0,1},{1,0},{2,3},{3,2},{4,5},{5,4},{6,7},{7,6},{8,9},{9,8},{10,11... | collective-permute-start | bytes 1572872 | tf_op jit(solution)/shard_map/ppermute | solution.py:15
  148.6 2.9 %collective-permute-start.2 = (f32[128,12]{0,1:T(8,128)S(1)}, f32[128,12]{0,1:T(8,128)S(1)}, u32[]{:S(2)}, u32[]{:S(2)}) collective-permute-start(f32[128,12]{0,1:T(8,128)S(1)} %pad_maximum_fusion.6), channel_id=1, source_target_pairs={{0,64},{64,0},{1,65},{65,1},{2,66},{66,2},{3,67},{67,3},{4,68},{68... | collective-permute-start | bytes 18440 | tf_op jit(solution)/shard_map/ppermute | solution.py:15
  151.5 6.7 %collective-permute-done = bf16[128,2048]{1,0:T(8,128)(2,1)S(1)} collective-permute-done((bf16[128,2048]{1,0:T(8,128)(2,1)S(1)}, bf16[128,2048]{1,0:T(8,128)(2,1)S(1)}, u32[]{:S(2)}, u32[]{:S(2)}) %collective-permute-start) | collective-permute-done | bytes 524320 | tf_op jit(solution)/shard_map/ppermute | solution.py:15
  158.3 3.5 %collective-permute-start.1 = (bf16[128,2048]{1,0:T(8,128)(2,1)S(1)}, bf16[128,2048]{1,0:T(8,128)(2,1)}, u32[]{:S(2)}, u32[]{:S(2)}) collective-permute-start(bf16[128,2048]{1,0:T(8,128)(2,1)S(1)} %add_convert_fusion), channel_id=1, source_target_pairs={{0,64},{64,0},{1,65},{65,1},{2,66},{66,2},{3,67},{67,3},{4,68},{68... | collective-permute-start | bytes 1572872 | tf_op jit(solution)/shard_map/ppermute | solution.py:15
  162.4 2.9 %fusion.150 = f32[128,1024]{1,0:T(8,128)S(1)} fusion(bf16[128,2048]{1,0:T(8,128)(2,1)S(1)} %add_convert_fusion, bf16[2048,1024]{1,0:T(8,128)(2,1)} %param.16), kind=kOutput, calls=%fused_computation.207 | convolution fusion | flops 536870912 | bytes 5242880 | tf_op jit(solution)/shard_map/dot_general | solution.py:22
  170.6 1.3 convolution_convert_fusion.3
  172.1 1.8 convolution_convert_fusion
  174.1 43.3 %all_to_all.30 = bf16[64,40,512]{2,1,0:T(8,128)(2,1)S(1)} all-to-all(bf16[64,40,512]{2,1,0:T(8,128)(2,1)S(1)} %pad_maximum_fusion), channel_id=1, replica_groups=mesh['grp'=2,'ep'=32,'mp'=2] {'ep','mp'}, dimensions={0} | all-to-all | bytes 5242880 | tf_op jit(solution)/shard_map/all_to_all | solution.py:192
  217.9 39.5 %all_to_all.31 = bf16[64,40,512]{2,1,0:T(8,128)(2,1)S(1)} all-to-all(bf16[64,40,512]{2,1,0:T(8,128)(2,1)S(1)} %broadcast_in_dim.64), channel_id=1, replica_groups=mesh['grp'=2,'ep'=32,'mp'=2] {'ep','mp'}, dimensions={0} | all-to-all | bytes 5242880 | tf_op jit(solution)/shard_map/all_to_all | solution.py:195
  257.4 2.5 collective-permute-start.7
  259.9 4.7 %collective-permute-done.7 = bf16[64,40,512]{2,1,0:T(8,128)(2,1)} collective-permute-done((bf16[64,40,512]{2,1,0:T(8,128)(2,1)S(1)}, bf16[64,40,512]{2,1,0:T(8,128)(2,1)}, u32[]{:S(2)}, u32[]{:S(2)}) %collective-permute-start.7) | collective-permute-done | bytes 2621472 | tf_op jit(solution)/shard_map/ppermute | solution.py:15
  264.6 2.1 broadcast_select_fusion.1
  266.7 0.9 slice_bitcast_fusion
  267.8 1.6 slice.121
  271.2 0.9 maximum_convert_fusion.1
  272.7 4.6 %maximum_convert_fusion = f32[2048,1024]{1,0:T(8,128)} fusion(bf16[2048,512]{1,0:T(8,128)(2,1)S(1)} %bitcast.125, bf16[2048,512]{1,0:T(8,128)(2,1)S(1)} %bitcast.124), kind=kLoop, calls=%fused_computation.27 | loop fusion | flops 8388608 | bytes 12582912 | tf_op jit(solution)/shard_map/convert_element_type | solution.py:218
  (89 shorter events, 12.4 us)
Async XLA Ops:
  0.6 1.3 copy-start
  6.4 35.7 %all-to-all-start = ((bf16[32,16,2048]{2,1,0:T(8,128)(2,1)}), bf16[32,16,2048]{2,1,0:T(8,128)(2,1)S(1)}, u32[]{:S(2)}, u32[]{:S(2)}) async-start(bf16[32,16,2048]{2,1,0:T(8,128)(2,1)} %bitcast.6), calls=%async_computation | async-start | bytes 4194304 | tf_op jit(solution)/shard_map/all_to_all | solution.py:105
  42.2 32.2 %all-to-all-start.2 = ((bf16[32,16,2048]{2,1,0:T(8,128)(2,1)}), bf16[32,16,2048]{2,1,0:T(8,128)(2,1)}, u32[]{:S(2)}, u32[]{:S(2)}) async-start(bf16[32,16,2048]{2,1,0:T(8,128)(2,1)} %bitcast.14), calls=%async_computation.2 | async-start | bytes 4194304 | tf_op jit(solution)/shard_map/all_to_all | solution.py:105
  74.3 29.2 %all-to-all-start.1 = ((bf16[32,16,2048]{2,1,0:T(8,128)(2,1)}), bf16[32,16,2048]{2,1,0:T(8,128)(2,1)S(1)}, u32[]{:S(2)}, u32[]{:S(2)}) async-start(bf16[32,16,2048]{2,1,0:T(8,128)(2,1)} %bitcast.130), calls=%async_computation.1 | async-start | bytes 4194304 | tf_op jit(solution)/shard_map/all_to_all | solution.py:119
  103.5 36.2 %all-to-all-start.3 = ((bf16[32,16,2048]{2,1,0:T(8,128)(2,1)}), bf16[32,16,2048]{2,1,0:T(8,128)(2,1)}, u32[]{:S(2)}, u32[]{:S(2)}) async-start(bf16[32,16,2048]{2,1,0:T(8,128)(2,1)} %bitcast.128), calls=%async_computation.3 | async-start | bytes 4194304 | tf_op jit(solution)/shard_map/all_to_all | solution.py:119
  142.7 5.8 %copy-start.6 = (s32[128,6]{0,1:T(8,128)S(1)}, s32[128,6]{0,1:T(8,128)}, u32[]{:S(2)}) copy-start(s32[128,6]{0,1:T(8,128)} %param.21) | copy-start | bytes 9220
  142.7 5.8 %copy-start.7 = (f32[128,6]{0,1:T(8,128)S(1)}, f32[128,6]{0,1:T(8,128)}, u32[]{:S(2)}) copy-start(f32[128,6]{0,1:T(8,128)} %param.20) | copy-start | bytes 9220
  142.7 8.7 %copy-start.5 = (bf16[6,256]{1,0:T(8,128)(2,1)S(1)}, bf16[6,256]{1,0:T(8,128)(2,1)}, u32[]{:S(2)}) copy-start(bf16[6,256]{1,0:T(8,128)(2,1)} %param.19) | copy-start | bytes 9220
  145.2 16.7 %copy-start.4 = (bf16[2048,48]{0,1:T(8,128)(2,1)S(1)}, bf16[2048,48]{0,1:T(8,128)(2,1)}, u32[]{:S(2)}) copy-start(bf16[2048,48]{0,1:T(8,128)(2,1)} %param.17) | copy-start | bytes 589828
  145.3 12.9 %collective-permute-start = (bf16[128,2048]{1,0:T(8,128)(2,1)S(1)}, bf16[128,2048]{1,0:T(8,128)(2,1)S(1)}, u32[]{:S(2)}, u32[]{:S(2)}) collective-permute-start(bf16[128,2048]{1,0:T(8,128)(2,1)S(1)} %constant_dynamic-slice_fusion.7), channel_id=1, source_target_pairs={{0,1},{1,0},{2,3},{3,2},{4,5},{5,4},{6,7},{7,6},{8,9},{9,8},{10,11... | collective-permute-start | bytes 1572872 | tf_op jit(solution)/shard_map/ppermute | solution.py:15
  148.6 18.0 %collective-permute-start.2 = (f32[128,12]{0,1:T(8,128)S(1)}, f32[128,12]{0,1:T(8,128)S(1)}, u32[]{:S(2)}, u32[]{:S(2)}) collective-permute-start(f32[128,12]{0,1:T(8,128)S(1)} %pad_maximum_fusion.6), channel_id=1, source_target_pairs={{0,64},{64,0},{1,65},{65,1},{2,66},{66,2},{3,67},{67,3},{4,68},{68... | collective-permute-start | bytes 18440 | tf_op jit(solution)/shard_map/ppermute | solution.py:15
  158.3 12.3 %collective-permute-start.1 = (bf16[128,2048]{1,0:T(8,128)(2,1)S(1)}, bf16[128,2048]{1,0:T(8,128)(2,1)}, u32[]{:S(2)}, u32[]{:S(2)}) collective-permute-start(bf16[128,2048]{1,0:T(8,128)(2,1)S(1)} %add_convert_fusion), channel_id=1, source_target_pairs={{0,64},{64,0},{1,65},{65,1},{2,66},{66,2},{3,67},{67,3},{4,68},{68... | collective-permute-start | bytes 1572872 | tf_op jit(solution)/shard_map/ppermute | solution.py:15
  162.4 3.6 %copy-start.3 = (bf16[6,128,256]{2,1,0:T(8,128)(2,1)S(1)}, bf16[6,128,256]{2,1,0:T(8,128)(2,1)}, u32[]{:S(2)}) copy-start(bf16[6,128,256]{2,1,0:T(8,128)(2,1)} %param.18) | copy-start | bytes 1179652
  168.5 2.0 collective-permute-start.6
  168.6 1.9 collective-permute-start.4
  169.4 1.2 collective-permute-start.5
  169.9 2.2 collective-permute-start.3
  257.4 7.2 %collective-permute-start.7 = (bf16[64,40,512]{2,1,0:T(8,128)(2,1)S(1)}, bf16[64,40,512]{2,1,0:T(8,128)(2,1)}, u32[]{:S(2)}, u32[]{:S(2)}) collective-permute-start(bf16[64,40,512]{2,1,0:T(8,128)(2,1)S(1)} %all_to_all.31), channel_id=1, source_target_pairs={{0,64},{64,0},{1,65},{65,1},{2,66},{66,2},{3,67},{67,3},{4,68},{68... | collective-permute-start | bytes 7864328 | tf_op jit(solution)/shard_map/ppermute | solution.py:15
  270.4 2.4 copy-start.2
  272.7 4.6 %copy-start.1 = (bf16[256,2048]{1,0:T(8,128)(2,1)S(1)}, bf16[256,2048]{1,0:T(8,128)(2,1)}, u32[]{:S(2)}) copy-start(bf16[256,2048]{1,0:T(8,128)(2,1)} %param.11) | copy-start | bytes 3145732

commit v2 on v1

--- a/solution.py
+++ b/solution.py
@@ -3,16 +3,105 @@
 import jax
 import jax.numpy as jnp
 from jax import lax
+from jax.experimental import pallas as pl
+from jax.experimental.pallas import tpu as pltpu
 from jax.sharding import PartitionSpec as P
 
 F32 = jnp.float32
 BF16 = jnp.bfloat16
 SLOT_CHUNKS = 2
 CHIPS = ("ep", "mp")
+GATE_STEPS = 3
 
 
 def swap(shard, axis):
     return lax.ppermute(shard, axis, [(0, 1), (1, 0)])
+
+
+def unpack_kernel(group_ref, own_ref, other_ref, main_ref, tower_ref, gate_ref, vector_ref):
+    blocks, parts, _, width = own_ref.shape
+    main_rows = main_ref.shape[1] // blocks
+    tower_rows = tower_ref.shape[2] // blocks
+    tower_width = tower_ref.shape[3]
+    gate_steps = gate_ref.shape[1] // blocks
+    first = group_ref[0] == 0
+    step = pl.program_id(0)
+
+    def both(block, part):
+        own = own_ref[block, part].astype(F32)
+        other = other_ref[block, part].astype(F32)
+        return jnp.where(first, own, other), jnp.where(first, other, own)
+
+    for block in range(blocks):
+        tower_sum = [0.0, 0.0]
+        vector_sum = [0.0, 0.0]
+        for part in range(parts):
+            for half, value in enumerate(both(block, part)):
+                main_ref[
+                    part,
+                    block * main_rows : (block + 1) * main_rows,
+                    half * width : (half + 1) * width,
+                ] = value[:main_rows]
+                rest = value[main_rows : main_rows + 2]
+                tower_sum[half] += value[main_rows + 2 : main_rows + 2 + tower_rows]
+                vector_sum[half] += rest
+
+                @pl.when(step < GATE_STEPS)
+                def _(rest=rest, part=part, half=half):
+                    for row in range(2):
+                        at = (part * 2 + row) * width
+                        gate_ref[half, block : block + 1, at : at + width] = rest[row : row + 1]
+
+        for half in range(2):
+            rows = slice(block * tower_rows, (block + 1) * tower_rows)
+            tower_ref[half, 0, rows, :] = tower_sum[half][:, :tower_width]
+            tower_ref[half, 1, rows, :] = tower_sum[half][:, tower_width:]
+            if block == 0:
+
+                @pl.when(step == GATE_STEPS)
+                def _(half=half, vector=vector_sum[half]):
+                    vector_ref[half] = vector
+
+
+def unpack(own_half, other_half, group_index, chips, parts):
+    _, each, width = own_half.shape
+    outer = chips // parts
+    step_blocks = 8
+    steps = outer // step_blocks
+    main_rows, tower_rows = each - 8, 6
+    tower_width = width // 2
+    shape = (outer, parts, each, width)
+    block = pl.BlockSpec((step_blocks, parts, each, width), lambda i, g: (i, 0, 0, 0))
+    return pl.pallas_call(
+        unpack_kernel,
+        grid_spec=pltpu.PrefetchScalarGridSpec(
+            num_scalar_prefetch=1,
+            grid=(steps,),
+            in_specs=[block, block],
+            out_specs=[
+                pl.BlockSpec((parts, step_blocks * main_rows, 2 * width), lambda i, g: (0, i, 0)),
+                pl.BlockSpec(
+                    (2, 2, step_blocks * tower_rows, tower_width), lambda i, g: (0, 0, i, 0)
+                ),
+                pl.BlockSpec(
+                    (2, step_blocks, 2 * parts * width),
+                    lambda i, g: (0, jnp.minimum(i, GATE_STEPS - 1), 0),
+                ),
+                pl.BlockSpec((2, 2, width), lambda i, g: (0, 0, 0)),
+            ],
+        ),
+        out_shape=[
+            jax.ShapeDtypeStruct((parts, outer * main_rows, 2 * width), F32),
+            jax.ShapeDtypeStruct((2, 2, outer * tower_rows, tower_width), F32),
+            jax.ShapeDtypeStruct((2, GATE_STEPS * step_blocks, 2 * parts * width), F32),
+            jax.ShapeDtypeStruct((2, 2, width), F32),
+        ],
+        compiler_params=pltpu.CompilerParams(vmem_limit_bytes=32 * 1024 * 1024),
+    )(
+        group_index.astype(jnp.int32).reshape(1),
+        own_half.reshape(shape),
+        other_half.reshape(shape),
+    )
 
 
 def student_grads(rows_in, experts_w, gates_w, tower_w, tower_v, soft_labels, masks, loss_scale):
@@ -111,21 +200,23 @@
 
     up_proj = teacher_up[0]
     down_proj = teacher_down[0]
-    mixed = jnp.zeros((rows_dev, feature_dim), F32)
+    part = lax.axis_index("mp")
+    half_width = feature_dim // width_parts
+    mixed = jnp.zeros((rows_dev, half_width), F32)
+    wide_lane = jnp.arange(chips * chunk_slots, dtype=jnp.int32)[None, :]
+    wide_expert = wide_lane // (width_parts * chunk_slots)
+    wide_place = wide_expert * chunk_slots + wide_lane % chunk_slots
     for chunk in range(SLOT_CHUNKS):
         rows_in = received[chunk].reshape(expert_total * chunk_slots, feature_dim)
         inner = jax.nn.gelu(jnp.dot(rows_in, up_proj, preferred_element_type=F32)).astype(BF16)
         partial = jnp.dot(inner, down_proj, preferred_element_type=F32).astype(BF16)
-        returned = lax.all_to_all(
-            partial.reshape(expert_total, chunk_slots, feature_dim),
-            "ep",
-            split_axis=0,
-            concat_axis=0,
-            tiled=True,
-        ).reshape(expert_total * chunk_slots, feature_dim)
+        outgoing = partial.reshape(expert_total, chunk_slots, width_parts, half_width)
+        outgoing = outgoing.transpose(0, 2, 1, 3).reshape(chips, chunk_slots, half_width)
+        returned = lax.all_to_all(outgoing, CHIPS, split_axis=0, concat_axis=0, tiled=True)
+        returned = returned.reshape(chips * chunk_slots, half_width)
         first, second = targets[chunk]
-        share = jnp.where(lane == first, weights[0], 0.0) + jnp.where(
-            lane == second, weights[1], 0.0
+        share = jnp.where(wide_place == first, weights[0], 0.0) + jnp.where(
+            wide_place == second, weights[1], 0.0
         )
         high = share.astype(BF16)
         low = (share - high.astype(F32)).astype(BF16)
@@ -134,11 +225,14 @@
     mixed = mixed.astype(BF16)
 
     half_rows = rows_dev // width_parts
-    part = lax.axis_index("mp")
     kept = lax.dynamic_slice_in_dim(mixed, part * half_rows, half_rows, 0)
     given = lax.dynamic_slice_in_dim(mixed, (1 - part) * half_rows, half_rows, 0)
-    own_rows = (kept.astype(F32) + swap(given, "mp").astype(F32)).astype(BF16)
-    other_rows = swap(own_rows, "grp")
+    taken = swap(given, "mp")
+    own_rows = jnp.concatenate(
+        [jnp.where(part == 0, kept, taken), jnp.where(part == 0, taken, kept)], 1
+    )
+    kept_both = jnp.concatenate([kept, given], 0)
+    all_rows = jnp.concatenate([kept_both, swap(kept_both, "grp")], 0)
 
     sample_total = rows_dev * lax.axis_size("grp") * expert_total
     pre_grad, gate_grad, grad_tower_in, grad_tower_out = student_grads(
@@ -158,67 +252,50 @@
         theirs = lax.dynamic_slice_in_dim(array, (1 - group_index) * size, size, axis)
         return mine, theirs
 
-    both_rows = jnp.concatenate([own_rows, other_rows], 0)
     mine, theirs = halves(pre_grad, 1)
-    pre_both = jnp.concatenate([mine, swap(theirs, "grp")], 0)
-    mine, theirs = halves(gate_grad, 1)
-    gate_both = jnp.concatenate([mine, swap(theirs, "grp")], 0)
+    gate_mine, gate_theirs = halves(gate_grad, 1)
+    width, gate_width = mine.shape[1], gate_mine.shape[1]
+    mine = jnp.concatenate([mine, gate_mine], 1)
+    theirs = swap(jnp.concatenate([theirs, gate_theirs], 1), "grp")
+    from_other = swap(jnp.concatenate([mine, theirs], 0), "mp")
+    factors = jnp.concatenate([mine, from_other[:half_rows], theirs, from_other[half_rows:]], 0)
     contract = (((0,), (0,)), ((), ()))
-    main = lax.dot_general(both_rows, pre_both, contract, preferred_element_type=F32).astype(BF16)
-    gates = lax.dot_general(gate_both, both_rows, contract, preferred_element_type=F32)
+    main = lax.dot_general(all_rows, factors[:, :width], contract, preferred_element_type=F32)
+    gates = lax.dot_general(factors[:, width:], all_rows, contract, preferred_element_type=F32)
     mine, theirs = halves(grad_tower_in.astype(BF16), 0)
-    tower = mine.astype(F32) + swap(theirs, "grp").astype(F32)
+    tower = (mine.astype(F32) + swap(theirs, "grp").astype(F32)).reshape(-1, grad_tower_in.shape[2])
     mine, theirs = halves(grad_tower_out.astype(BF16), 0)
-    vector = mine.astype(F32) + swap(theirs, "grp").astype(F32)
-
-    width = main.shape[1]
-    tower_rows = tower.reshape(-1, tower.shape[2])
-    tower_half = tower_rows.shape[0] // 2
-    tower_block = jnp.concatenate([tower_rows[:tower_half], tower_rows[tower_half:]], 1)
-    gate_block = gates.reshape(-1, width)
-    vector_flat = vector.reshape(-1)
-    vector_rows = -(-vector_flat.shape[0] // width)
-    vector_block = jnp.pad(vector_flat, (0, vector_rows * width - vector_flat.shape[0]))
-    small = jnp.concatenate(
-        [tower_block, gate_block, vector_block.reshape(vector_rows, width)], 0
-    ).astype(BF16)
-    small_each = -(-small.shape[0] // (8 * chips)) * 8
-    small = jnp.pad(small, ((0, small_each * chips - small.shape[0]), (0, 0)))
-    main_each = main.shape[0] // chips
+    vector = (mine.astype(F32) + swap(theirs, "grp").astype(F32)).reshape(-1)
+
+    tower_half = tower.shape[0] // 2
+    tower = jnp.concatenate([tower[:tower_half], tower[tower_half:]], 1)
+    rest = jnp.concatenate(
+        [
+            gates.reshape(-1),
+            vector,
+            jnp.zeros((2 * expert_total * width - gates.size - vector.size,), F32),
+        ]
+    )
     packed = jnp.concatenate(
-        [main.reshape(chips, main_each, width), small.reshape(chips, small_each, width)], 1
-    )
-
-    parts = lax.all_to_all(packed, CHIPS, split_axis=0, concat_axis=0, tiled=True)
+        [
+            main.astype(BF16).reshape(expert_total, -1, width),
+            rest.astype(BF16).reshape(expert_total, -1, width),
+            tower.astype(BF16).reshape(expert_total, -1, width),
+        ],
+        1,
+    )
+
+    parts = lax.all_to_all(packed, "ep", split_axis=0, concat_axis=0, tiled=True)
     total = jnp.sum(parts.astype(F32), 0).astype(BF16)
-    spread = jnp.broadcast_to(total[None], packed.shape)
+    spread = jnp.broadcast_to(total[None], (chips,) + total.shape)
     own_half = lax.all_to_all(spread, CHIPS, split_axis=0, concat_axis=0, tiled=True)
     other_half = swap(own_half, "grp")
-    low_half = jnp.where(group_index == 0, own_half, other_half)
-    high_half = jnp.where(group_index == 0, other_half, own_half)
-
-    main_halves, tower_halves, gate_halves, vector_halves = [], [], [], []
-    for half in (low_half, high_half):
-        main_halves.append(half[:, :main_each].reshape(-1, width))
-        rest = half[:, main_each:].reshape(-1, width)
-        block = rest[:tower_half]
-        tower_width = tower.shape[2]
-        tower_halves.append(
-            jnp.concatenate([block[:, :tower_width], block[:, tower_width:]], 0).reshape(
-                tower.shape
-            )
-        )
-        at = tower_half
-        gate_halves.append(rest[at : at + gate_block.shape[0]].reshape(gates.shape))
-        at += gate_block.shape[0]
-        vector_halves.append(
-            rest[at : at + vector_rows].reshape(-1)[: vector_flat.shape[0]].reshape(vector.shape)
-        )
+    main, tower, gates, vector = unpack(own_half, other_half, group_index, chips, width_parts)
     return (
-        jnp.concatenate(main_halves, 1).astype(F32),
-        jnp.concatenate(gate_halves, 0).astype(F32).T,
-        jnp.concatenate(tower_halves, 0).astype(F32),
-        jnp.concatenate(vector_halves, 0).astype(F32),
+        main.reshape(student_experts.shape),
+        gates.reshape(2 * gate_width, feature_dim).T,
+        tower.reshape(tower_in.shape),
+        vector.reshape(2, -1)[:, : tower_out.size // 2].reshape(tower_out.shape),
     )
 
 

time: 278 us -> 261 us (0.939)
  blocking collectives: 82.7 us -> 61.7 us
  local copies, waits for them, and re-layouts: 5.77 us -> 14.5 us
  waiting for transfers between devices: 76.2 us -> 67.7 us
  other arithmetic: 11.6 us -> 4.33 us
  starting transfers between devices: 44.3 us -> 50 us
  Pallas kernels: 0 us -> 4.3 us
    all_to_all x1, blocking collectives: 43.3 us -> 23.3 us  [on_device(): lax.all_to_all(packed, 'ep', split_axis=0, concat_axis=0, tiled=True)]
    reshape x6, local copies, waits for them, and re-layouts: 1.11 us -> 11.2 us  [the longest x4 10.6 us: on_device(): partial.reshape(expert_total, chunk_slots, width_parts, half_width)]
    all_to_all x2, waiting for transfers between devices: 30.8 us -> 23.9 us  [on_device(): lax.all_to_all(outgoing, CHIPS, split_axis=0, concat_axis=0, tiled=True)]
    convert_element_type x4 -> x0, other arithmetic: 6.25 us -> none  [the longest x1 4.59 us: on_device(): jnp.concatenate(main_halves, 1).astype(F32)]
    all_to_all x2, waiting for transfers between devices: 33.9 us -> 28.6 us  [on_device(): lax.all_to_all(outgoing, 'ep', split_axis=0, concat_axis=0, tiled=True)]
    pallas_call x0 -> x1, Pallas kernels: none -> 4.3 us  [unpack(): pl.pallas_call(unpack_kernel, grid_spec=pltpu.PrefetchScalarGridSpec(num_...]
    ppermute x8, waiting for transfers between devices: 11.4 us -> 15.1 us  [swap(): return lax.ppermute(shard, axis, [(0, 1), (1, 0)])]
    ppermute x8, starting transfers between devices: 13.5 us -> 17.1 us  [swap(): return lax.ppermute(shard, axis, [(0, 1), (1, 0)])]
  transfers between devices with their start and end apart: 12 -> 12, of which waited for: 6 -> 8; matrix products, arithmetic and copies ran while one was open for 17% -> 23% of each run, Pallas kernels for 0% -> 0%
where the time goes in v2:
time: 261 us; the launch traced here: 259 us
  waiting for transfers between devices  67.7 us (26%)
  blocking collectives  61.7 us (24%)
  matrix products  55.8 us (21%)
  starting transfers between devices  50 us (19%)
  local copies, waits for them, and re-layouts  14.5 us (6%)
  other arithmetic  4.33 us (2%)
  Pallas kernels  4.3 us (2%)
    all_to_all x1, blocking collectives, on_device(): lax.all_to_all(spread, CHIPS, split_axis=0, concat_axis=0, tiled=True)  38.4 us
    dot_general x2, matrix products, on_device(): partial = jnp.dot(inner, down_proj, preferred_element_type=F32).astype(BF16)  32.5 us
    all_to_all x2, waiting for transfers between devices, on_device(): lax.all_to_all(outgoing, 'ep', split_axis=0, concat_axis=0, tiled=True)  28.6 us
    all_to_all x2, waiting for transfers between devices, on_device(): lax.all_to_all(outgoing, CHIPS, split_axis=0, concat_axis=0, tiled=True)  23.9 us
    all_to_all x1, blocking collectives, on_device(): lax.all_to_all(packed, 'ep', split_axis=0, concat_axis=0, tiled=True)  23.3 us
    ppermute x8, starting transfers between devices, swap(): return lax.ppermute(shard, axis, [(0, 1), (1, 0)])  17.1 us
    all_to_all x2, starting transfers between devices, on_device(): lax.all_to_all(outgoing, CHIPS, split_axis=0, concat_axis=0, tiled=True)  17 us
    all_to_all x2, starting transfers between devices, on_device(): lax.all_to_all(outgoing, 'ep', split_axis=0, concat_axis=0, tiled=True)  15.9 us
  transfers between devices with their start and end apart: 12, of which 8 were waited for; matrix products, arithmetic and copies ran while one was open for 23% of the time, Pallas kernels for 0%

profile of v2, /device:TPU:1, one launch (start us, length us, event | category | flops | bytes accessed | tf_op | source)
XLA Modules:
  0.0 259.5 jit_solution(4153395264811569980)
XLA Ops:
  4.2 2.2 convolution_convert_fusion.1
  6.4 9.2 %all-to-all-start = ((bf16[32,16,2048]{2,1,0:T(8,128)(2,1)}), bf16[32,16,2048]{2,1,0:T(8,128)(2,1)S(1)}, u32[]{:S(2)}, u32[]{:S(2)}) async-start(bf16[32,16,2048]{2,1,0:T(8,128)(2,1)} %bitcast.7), calls=%async_computation | async-start | bytes 4194304 | tf_op jit(solution)/shard_map/all_to_all | solution.py:194
  15.7 2.2 convolution_convert_fusion
  17.9 24.3 %all-to-all-done = bf16[32,16,2048]{2,1,0:T(8,128)(2,1)S(1)} async-done(((bf16[32,16,2048]{2,1,0:T(8,128)(2,1)}), bf16[32,16,2048]{2,1,0:T(8,128)(2,1)S(1)}, u32[]{:S(2)}, u32[]{:S(2)}) %all-to-all-start) | async-done | bytes 2097184 | tf_op jit(solution)/shard_map/all_to_all | solution.py:194
  42.2 6.6 %all-to-all-start.2 = ((bf16[32,16,2048]{2,1,0:T(8,128)(2,1)}), bf16[32,16,2048]{2,1,0:T(8,128)(2,1)}, u32[]{:S(2)}, u32[]{:S(2)}) async-start(bf16[32,16,2048]{2,1,0:T(8,128)(2,1)} %bitcast.16), calls=%async_computation.2 | async-start | bytes 4194304 | tf_op jit(solution)/shard_map/all_to_all | solution.py:194
  48.8 15.9 %fusion.25 = bf16[512,2048]{1,0:T(8,128)(2,1)} fusion(bf16[1,2048,2048]{2,1,0:T(8,128)(2,1)} %param.15, bf16[512,2048]{1,0:T(8,128)(2,1)S(1)} %bitcast.126, bf16[1,2048,2048]{2,1,0:T(8,128)(2,1)} %param.14), kind=kOutput, calls=%fused_computation.29 | convolution fusion | flops 8600420352 | bytes 20971520 | tf_op jit(solution)/shard_map/dot_general | solution.py:212
  64.8 3.3 %reshape.293 = bf16[32,16,2,1024]{3,2,1,0:T(2,128)(2,1)S(1)} reshape(bf16[512,2048]{1,0:T(8,128)(2,1)} %fusion.25) | data formatting | bytes 4194304 | tf_op jit(solution)/shard_map/reshape | solution.py:213
  68.1 2.0 copy.34
  70.0 4.3 %all-to-all-done.2 = bf16[32,16,2048]{2,1,0:T(8,128)(2,1)} async-done(((bf16[32,16,2048]{2,1,0:T(8,128)(2,1)}), bf16[32,16,2048]{2,1,0:T(8,128)(2,1)}, u32[]{:S(2)}, u32[]{:S(2)}) %all-to-all-start.2) | async-done | bytes 2097184 | tf_op jit(solution)/shard_map/all_to_all | solution.py:194
  74.3 9.0 %all-to-all-start.1 = ((bf16[64,16,1024]{2,1,0:T(8,128)(2,1)}), bf16[64,16,1024]{2,1,0:T(8,128)(2,1)}, u32[]{:S(2)}, u32[]{:S(2)}) async-start(bf16[64,16,1024]{2,1,0:T(8,128)(2,1)} %bitcast.12), calls=%async_computation.1 | async-start | bytes 4194304 | tf_op jit(solution)/shard_map/all_to_all | solution.py:215
  83.3 16.6 %fusion.28 = bf16[512,2048]{1,0:T(8,128)(2,1)} fusion(bf16[1,2048,2048]{2,1,0:T(8,128)(2,1)} %param.15, bf16[512,2048]{1,0:T(8,128)(2,1)} %bitcast.17, bf16[1,2048,2048]{2,1,0:T(8,128)(2,1)} %param.14), kind=kOutput, calls=%fused_computation.30 | convolution fusion | flops 8600420352 | bytes 20971520 | tf_op jit(solution)/shard_map/dot_general | solution.py:212
  99.9 3.3 %reshape.298 = bf16[32,16,2,1024]{3,2,1,0:T(2,128)(2,1)S(1)} reshape(bf16[512,2048]{1,0:T(8,128)(2,1)} %fusion.28) | data formatting | bytes 4194304 | tf_op jit(solution)/shard_map/reshape | solution.py:213
  103.2 2.0 copy.35
  105.2 3.6 %all-to-all-done.1 = bf16[64,16,1024]{2,1,0:T(8,128)(2,1)} async-done(((bf16[64,16,1024]{2,1,0:T(8,128)(2,1)}), bf16[64,16,1024]{2,1,0:T(8,128)(2,1)}, u32[]{:S(2)}, u32[]{:S(2)}) %all-to-all-start.1) | async-done | bytes 2097184 | tf_op jit(solution)/shard_map/all_to_all | solution.py:215
  108.8 8.0 %all-to-all-start.3 = ((bf16[64,16,1024]{2,1,0:T(8,128)(2,1)}), bf16[64,16,1024]{2,1,0:T(8,128)(2,1)S(1)}, u32[]{:S(2)}, u32[]{:S(2)}) async-start(bf16[64,16,1024]{2,1,0:T(8,128)(2,1)} %bitcast.19), calls=%async_computation.3 | async-start | bytes 4194304 | tf_op jit(solution)/shard_map/all_to_all | solution.py:215
  116.9 2.4 fusion.93
  119.3 3.4 %convolution_add_fusion.2 = f32[256,1024]{1,0:T(8,128)} fusion(f32[256,1024]{1,0:T(8,128)S(1)} %fusion.93, bf16[1024,1024]{1,0:T(8,128)(2,1)} %bitcast.13, f32[256]{0:T(256)S(1)} %multiply_divide_fusion.1, f32[256]{0:T(256)S(1)} %get-tuple-element.20, s32[1024]{0:T(1024)S(1)} %fusion.128, s32[256]{0:T(256)S(1)} %bitcast.146, s32[256]{0:T(256)S(1)} %bitcast.143), kind=kOutput, calls=%fused_computation.42 | convolution fusion | flops 539492352 | bytes 4202496 | tf_op jit(solution)/shard_map/dot_general | solution.py:224
  122.7 20.4 %all-to-all-done.3 = bf16[64,16,1024]{2,1,0:T(8,128)(2,1)S(1)} async-done(((bf16[64,16,1024]{2,1,0:T(8,128)(2,1)}), bf16[64,16,1024]{2,1,0:T(8,128)(2,1)S(1)}, u32[]{:S(2)}, u32[]{:S(2)}) %all-to-all-start.3) | async-done | bytes 2097184 | tf_op jit(solution)/shard_map/all_to_all | solution.py:215
  143.1 2.1 convolution_add_fusion.1
  146.8 2.6 %collective-permute-start.1 = (bf16[128,1024]{1,0:T(8,128)(2,1)S(1)}, bf16[128,1024]{1,0:T(8,128)(2,1)S(1)}, u32[]{:S(2)}, u32[]{:S(2)}) collective-permute-start(bf16[128,1024]{1,0:T(8,128)(2,1)S(1)} %constant_dynamic-slice_fusion.7), channel_id=1, source_target_pairs={{0,1},{1,0},{2,3},{3,2},{4,5},{5,4},{6,7},{7,6},{8,9},{9,8},{10,11... | collective-permute-start | bytes 786440 | tf_op jit(solution)/shard_map/ppermute | solution.py:18
  149.4 3.4 %collective-permute-start.2 = (f32[128,12]{0,1:T(8,128)S(1)}, f32[128,12]{0,1:T(8,128)S(1)}, u32[]{:S(2)}, u32[]{:S(2)}) collective-permute-start(f32[128,12]{0,1:T(8,128)S(1)} %pad_maximum_fusion.11), channel_id=1, source_target_pairs={{0,64},{64,0},{1,65},{65,1},{2,66},{66,2},{3,67},{67,3},{4,68},{68... | collective-permute-start | bytes 18440 | tf_op jit(solution)/shard_map/ppermute | solution.py:18
  155.0 2.9 %fusion.97 = f32[128,1024]{1,0:T(8,128)S(1)} fusion(bf16[2048,1024]{1,0:T(8,128)(2,1)} %param.16, bf16[128,1024]{1,0:T(8,128)(2,1)S(1)} %broadcast_select_fusion, bf16[128,1024]{1,0:T(8,128)(2,1)S(1)} %get-tuple-element.18), kind=kOutput, calls=%fused_computation.114 | convolution fusion | flops 537919488 | bytes 5242880 | tf_op jit(solution)/shard_map/dot_general | solution.py:111
  161.1 5.5 %collective-permute-start = (bf16[256,1024]{1,0:T(8,128)(2,1)S(1)}, bf16[256,1024]{1,0:T(8,128)(2,1)}, u32[]{:S(2)}, u32[]{:S(2)}) collective-permute-start(bf16[256,1024]{1,0:T(8,128)(2,1)S(1)} %pad_maximum_fusion.2), channel_id=1, source_target_pairs={{0,64},{64,0},{1,65},{65,1},{2,66},{66,2},{3,67},{67,3},{4,68},{68... | collective-permute-start | bytes 1572872 | tf_op jit(solution)/shard_map/ppermute | solution.py:18
  168.6 1.3 collective-permute-done.3
  172.3 8.5 %collective-permute-done.4 = bf16[256,536]{1,0:T(8,128)(2,1)S(1)} collective-permute-done((bf16[256,536]{1,0:T(8,128)(2,1)S(1)}, bf16[256,536]{1,0:T(8,128)(2,1)S(1)}, u32[]{:S(2)}, u32[]{:S(2)}) %collective-permute-start.4) | collective-permute-done | bytes 274464 | tf_op jit(solution)/shard_map/ppermute | solution.py:18
  180.9 1.3 fusion.48
  182.3 1.8 convolution_convert_fusion.2
  184.2 23.3 %all_to_all.30 = bf16[32,40,512]{2,1,0:T(8,128)(2,1)S(1)} all-to-all(bf16[32,40,512]{2,1,0:T(8,128)(2,1)S(1)} %maximum_maximum_fusion), channel_id=1, replica_groups=mesh['grp'=2,'ep'=32,'mp'=2] {'ep'}, dimensions={0} | all-to-all | bytes 2621440 | tf_op jit(solution)/shard_map/all_to_all | solution.py:288
  207.9 38.4 %all_to_all.31 = bf16[64,40,512]{2,1,0:T(8,128)(2,1)S(1)} all-to-all(bf16[64,40,512]{2,1,0:T(8,128)(2,1)S(1)} %broadcast_in_dim.69), channel_id=1, replica_groups=mesh['grp'=2,'ep'=32,'mp'=2] {'ep','mp'}, dimensions={0} | all-to-all | bytes 5242880 | tf_op jit(solution)/shard_map/all_to_all | solution.py:291
  246.3 3.8 %collective-permute-start.7 = (bf16[64,40,512]{2,1,0:T(8,128)(2,1)S(1)}, bf16[64,40,512]{2,1,0:T(8,128)(2,1)S(1)}, u32[]{:S(2)}, u32[]{:S(2)}) collective-permute-start(bf16[64,40,512]{2,1,0:T(8,128)(2,1)S(1)} %all_to_all.31), channel_id=1, source_target_pairs={{0,64},{64,0},{1,65},{65,1},{2,66},{66,2},{3,67},{67,3},{4,68},{68... | collective-permute-start | bytes 7864328 | tf_op jit(solution)/shard_map/ppermute | solution.py:18
  250.0 4.5 %collective-permute-done.7 = bf16[64,40,512]{2,1,0:T(8,128)(2,1)S(1)} collective-permute-done((bf16[64,40,512]{2,1,0:T(8,128)(2,1)S(1)}, bf16[64,40,512]{2,1,0:T(8,128)(2,1)S(1)}, u32[]{:S(2)}, u32[]{:S(2)}) %collective-permute-start.7) | collective-permute-done | bytes 2621472 | tf_op jit(solution)/shard_map/ppermute | solution.py:18
  254.6 4.3 %shard_map.138 = (f32[2,1024,1024]{2,1,0:T(8,128)}, f32[2,2,192,256]{3,2,1,0:T(8,128)}, f32[2,24,2048]{2,1,0:T(8,128)}, f32[2,2,512]{2,1,0:T(2,128)S(1)}) custom-call(s32[1]{0:T(128)} %bitcast.group_ref, bf16[32,2,40,512]{3,2,1,0:T(8,128)(2,1)S(1)} %bitcast.119, bf16[32,2,40,512]{3,2,1,0:T(8,128)(2,1)S(1)} %bitcast.120), custom_call_target="tpu_custom_call" | custom-call | tf_op jit(solution)/shard_map/pallas_call | solution.py:75
  (87 shorter events, 16.1 us)
Async XLA Ops:
  0.6 1.3 copy-start
  6.4 35.7 %all-to-all-start = ((bf16[32,16,2048]{2,1,0:T(8,128)(2,1)}), bf16[32,16,2048]{2,1,0:T(8,128)(2,1)S(1)}, u32[]{:S(2)}, u32[]{:S(2)}) async-start(bf16[32,16,2048]{2,1,0:T(8,128)(2,1)} %bitcast.7), calls=%async_computation | async-start | bytes 4194304 | tf_op jit(solution)/shard_map/all_to_all | solution.py:194
  42.2 32.2 %all-to-all-start.2 = ((bf16[32,16,2048]{2,1,0:T(8,128)(2,1)}), bf16[32,16,2048]{2,1,0:T(8,128)(2,1)}, u32[]{:S(2)}, u32[]{:S(2)}) async-start(bf16[32,16,2048]{2,1,0:T(8,128)(2,1)} %bitcast.16), calls=%async_computation.2 | async-start | bytes 4194304 | tf_op jit(solution)/shard_map/all_to_all | solution.py:194
  74.3 34.4 %all-to-all-start.1 = ((bf16[64,16,1024]{2,1,0:T(8,128)(2,1)}), bf16[64,16,1024]{2,1,0:T(8,128)(2,1)}, u32[]{:S(2)}, u32[]{:S(2)}) async-start(bf16[64,16,1024]{2,1,0:T(8,128)(2,1)} %bitcast.12), calls=%async_computation.1 | async-start | bytes 4194304 | tf_op jit(solution)/shard_map/all_to_all | solution.py:215
  108.8 34.3 %all-to-all-start.3 = ((bf16[64,16,1024]{2,1,0:T(8,128)(2,1)}), bf16[64,16,1024]{2,1,0:T(8,128)(2,1)S(1)}, u32[]{:S(2)}, u32[]{:S(2)}) async-start(bf16[64,16,1024]{2,1,0:T(8,128)(2,1)} %bitcast.19), calls=%async_computation.3 | async-start | bytes 4194304 | tf_op jit(solution)/shard_map/all_to_all | solution.py:215
  145.1 4.3 %copy-start.5 = (s32[128,6]{0,1:T(8,128)S(1)}, s32[128,6]{0,1:T(8,128)}, u32[]{:S(2)}) copy-start(s32[128,6]{0,1:T(8,128)} %param.21) | copy-start | bytes 9220
  145.1 4.3 %copy-start.6 = (f32[128,6]{0,1:T(8,128)S(1)}, f32[128,6]{0,1:T(8,128)}, u32[]{:S(2)}) copy-start(f32[128,6]{0,1:T(8,128)} %param.20) | copy-start | bytes 9220
  145.1 7.7 %copy-start.4 = (bf16[6,256]{1,0:T(8,128)(2,1)S(1)}, bf16[6,256]{1,0:T(8,128)(2,1)}, u32[]{:S(2)}) copy-start(bf16[6,256]{1,0:T(8,128)(2,1)} %param.19) | copy-start | bytes 9220
  146.0 0.8 copy-start.3
  146.8 7.9 %copy-start.7 = (bf16[2048,48]{0,1:T(8,128)(2,1)S(1)}, bf16[2048,48]{0,1:T(8,128)(2,1)}, u32[]{:S(2)}) copy-start(bf16[2048,48]{0,1:T(8,128)(2,1)} %param.17) | copy-start | bytes 589828
  146.8 6.8 %collective-permute-start.1 = (bf16[128,1024]{1,0:T(8,128)(2,1)S(1)}, bf16[128,1024]{1,0:T(8,128)(2,1)S(1)}, u32[]{:S(2)}, u32[]{:S(2)}) collective-permute-start(bf16[128,1024]{1,0:T(8,128)(2,1)S(1)} %constant_dynamic-slice_fusion.7), channel_id=1, source_target_pairs={{0,1},{1,0},{2,3},{3,2},{4,5},{5,4},{6,7},{7,6},{8,9},{9,8},{10,11... | collective-permute-start | bytes 786440 | tf_op jit(solution)/shard_map/ppermute | solution.py:18
  149.4 10.1 %collective-permute-start.2 = (f32[128,12]{0,1:T(8,128)S(1)}, f32[128,12]{0,1:T(8,128)S(1)}, u32[]{:S(2)}, u32[]{:S(2)}) collective-permute-start(f32[128,12]{0,1:T(8,128)S(1)} %pad_maximum_fusion.11), channel_id=1, source_target_pairs={{0,64},{64,0},{1,65},{65,1},{2,66},{66,2},{3,67},{67,3},{4,68},{68... | collective-permute-start | bytes 18440 | tf_op jit(solution)/shard_map/ppermute | solution.py:18
  158.0 1.0 copy-start.2
  161.1 19.8 %collective-permute-start = (bf16[256,1024]{1,0:T(8,128)(2,1)S(1)}, bf16[256,1024]{1,0:T(8,128)(2,1)}, u32[]{:S(2)}, u32[]{:S(2)}) collective-permute-start(bf16[256,1024]{1,0:T(8,128)(2,1)S(1)} %pad_maximum_fusion.2), channel_id=1, source_target_pairs={{0,64},{64,0},{1,65},{65,1},{2,66},{66,2},{3,67},{67,3},{4,68},{68... | collective-permute-start | bytes 1572872 | tf_op jit(solution)/shard_map/ppermute | solution.py:18
  166.9 1.7 collective-permute-start.5
  167.0 4.2 %collective-permute-start.6 = (bf16[3,128,256]{2,1,0:T(8,128)(2,1)S(1)}, bf16[3,128,256]{2,1,0:T(8,128)(2,1)}, u32[]{:S(2)}, u32[]{:S(2)}) collective-permute-start(bf16[3,128,256]{2,1,0:T(8,128)(2,1)S(1)} %constant_dynamic-slice_fusion), channel_id=1, source_target_pairs={{0,64},{64,0},{1,65},{65,1},{2,66},{66,2},{3,67},{67,3},{4,68},{68... | collective-permute-start | bytes 589832 | tf_op jit(solution)/shard_map/ppermute | solution.py:18
  168.5 1.5 collective-permute-start.3
  170.0 10.8 %collective-permute-start.4 = (bf16[256,536]{1,0:T(8,128)(2,1)S(1)}, bf16[256,536]{1,0:T(8,128)(2,1)S(1)}, u32[]{:S(2)}, u32[]{:S(2)}) collective-permute-start(bf16[256,536]{1,0:T(8,128)(2,1)S(1)} %pad_maximum_fusion.8), channel_id=1, source_target_pairs={{0,1},{1,0},{2,3},{3,2},{4,5},{5,4},{6,7},{7,6},{8,9},{9,8},{10,11... | collective-permute-start | bytes 823304 | tf_op jit(solution)/shard_map/ppermute | solution.py:18
  246.3 8.3 %collective-permute-start.7 = (bf16[64,40,512]{2,1,0:T(8,128)(2,1)S(1)}, bf16[64,40,512]{2,1,0:T(8,128)(2,1)S(1)}, u32[]{:S(2)}, u32[]{:S(2)}) collective-permute-start(bf16[64,40,512]{2,1,0:T(8,128)(2,1)S(1)} %all_to_all.31), channel_id=1, source_target_pairs={{0,64},{64,0},{1,65},{65,1},{2,66},{66,2},{3,67},{67,3},{4,68},{68... | collective-permute-start | bytes 7864328 | tf_op jit(solution)/shard_map/ppermute | solution.py:18
  254.6 4.9 %copy-start.1 = (bf16[256,2048]{1,0:T(8,128)(2,1)S(1)}, bf16[256,2048]{1,0:T(8,128)(2,1)}, u32[]{:S(2)}) copy-start(bf16[256,2048]{1,0:T(8,128)(2,1)} %param.11) | copy-start | bytes 3145732

commit v3 on v2

v3 whole, which is shorter than its diff:
```python
import functools
import math

import jax
import jax.numpy as jnp
from jax import lax
from jax.experimental import pallas as pl
from jax.experimental.pallas import tpu as pltpu
from jax.sharding import PartitionSpec as P

F32 = jnp.float32
BF16 = jnp.bfloat16
SLOT_CHUNKS = 2
CHIPS = ("ep", "mp")
GATE_STEPS = 3


def swap(shard, axis):
    return lax.ppermute(shard, axis, [(0, 1), (1, 0)])


def unpack_kernel(place_ref, half_ref, *refs):
    main_ref, tower_ref, gate_ref, vector_ref = refs[-4:]
    blocks, parts, _, width = half_ref.shape
    main_rows = main_ref.shape[1] // blocks
    tower_rows = tower_ref.shape[2] // blocks
    tower_width = tower_ref.shape[3]
    step = pl.program_id(0)
    for block in range(blocks):
        values = [half_ref[block, part].astype(F32) for part in range(parts)]
        for part in range(parts):
            main_ref[part, block * main_rows : (block + 1) * main_rows, :] = values[part][
                :main_rows
            ]
        tower = sum(value[main_rows + 2 : main_rows + 2 + tower_rows] for value in values)
        rows = slice(block * tower_rows, (block + 1) * tower_rows)
        tower_ref[0, 0, rows, :] = tower[:, :tower_width]
        tower_ref[0, 1, rows, :] = tower[:, tower_width:]
        rests = [value[main_rows : main_rows + 2] for value in values]

        @pl.when(step < GATE_STEPS)
        def _(rests=rests, block=block):
            for part in range(parts):
                for row in range(2):
                    at = (part * 2 + row) * width
                    gate_ref[0, block : block + 1, at : at + width] = rests[part][row : row + 1]

        if block == 0:

            @pl.when(step == GATE_STEPS)
            def _(rests=rests):
                vector_ref[0] = sum(rests)


def unpack(half, place, chips, parts, filled):
    _, each, width = half.shape
    outer = chips // parts
    step_blocks = 8
    main_rows, tower_rows = each - 8, 6
    tower_width = width // 2
    out_shape = [
        jax.ShapeDtypeStruct((parts, outer * main_rows, 2 * width), F32),
        jax.ShapeDtypeStruct((2, 2, outer * tower_rows, tower_width), F32),
        jax.ShapeDtypeStruct((2, GATE_STEPS * step_blocks, 2 * parts * width), F32),
        jax.ShapeDtypeStruct((2, 2, width), F32),
    ]
    size = sum(4 * math.prod(shape.shape) for shape in out_shape) // 2 + 2 * half.size
    return pl.pallas_call(
        unpack_kernel,
        grid_spec=pltpu.PrefetchScalarGridSpec(
            num_scalar_prefetch=1,
            grid=(outer // step_blocks,),
            in_specs=[pl.BlockSpec((step_blocks, parts, each, width), lambda i, g: (i, 0, 0, 0))]
            + [pl.BlockSpec(memory_space=pl.ANY)] * len(filled),
            out_specs=[
                pl.BlockSpec((parts, step_blocks * main_rows, width), lambda i, g: (0, i, g[0])),
                pl.BlockSpec(
                    (1, 2, step_blocks * tower_rows, tower_width), lambda i, g: (g[0], 0, i, 0)
                ),
                pl.BlockSpec(
                    (1, step_blocks, 2 * parts * width),
                    lambda i, g: (g[0], jnp.minimum(i, GATE_STEPS - 1), 0),
                ),
                pl.BlockSpec((1, 2, width), lambda i, g: (g[0], 0, 0)),
            ],
        ),
        out_shape=out_shape,
        input_output_aliases={2 + i: i for i in range(len(filled))},
        cost_estimate=pl.CostEstimate(flops=half.size, bytes_accessed=size, transcendentals=0),
        compiler_params=pltpu.CompilerParams(vmem_limit_bytes=32 * 1024 * 1024),
    )(place.astype(jnp.int32).reshape(1), half.reshape(outer, parts, each, width), *filled)


def student_kernel(
    part_ref,
    kept_ref,
    taken_ref,
    experts_ref,
    gates_ref,
    tower_in_ref,
    tower_out_ref,
    labels_ref,
    pre_grad_ref,
    gate_grad_ref,
    tower_in_grad_ref,
    tower_out_grad_ref,
    act_ref,
    slope_ref,
    *,
    loss_scale,
):
    tasks, width, _ = tower_in_ref.shape
    columns = gates_ref.shape[0]
    experts = columns // tasks
    half = kept_ref.shape[1]
    first = part_ref[0] == 0
    left = jnp.where(first, kept_ref[...], taken_ref[...])
    right = jnp.where(first, taken_ref[...], kept_ref[...])
    across = (((1,), (1,)), ((), ()))
    down = (((0,), (0,)), ((), ()))

    logit = lax.dot_general(left, gates_ref[:, :half], across, preferred_element_type=F32)
    logit += lax.dot_general(right, gates_ref[:, half:], across, preferred_element_type=F32)
    sig = jax.nn.sigmoid(logit)
    task_of = [lax.broadcasted_iota(jnp.int32, (columns, columns), d) // experts for d in (0, 1)]
    same_task = jnp.where(task_of[0] == task_of[1], 1.0, 0.0)

    def task_sum(value):
        return jnp.dot(
            value, same_task, precision=lax.Precision.HIGHEST, preferred_element_type=F32
        )

    gate_sum = task_sum(sig)
    share = sig / gate_sum

    scale = math.sqrt(2.0 / math.pi)
    for k in range(experts):
        at = slice(k * width, (k + 1) * width)
        pre = jnp.dot(left, experts_ref[:half, at], preferred_element_type=F32)
        pre += jnp.dot(right, experts_ref[half:, at], preferred_element_type=F32)
        square = pre * pre
        tanh = jnp.tanh(scale * (pre + 0.044715 * (square * pre)))
        cdf = 0.5 * (1.0 + tanh)
        act_ref[k] = pre * cdf
        slope_ref[k] = cdf + (0.5 * scale) * pre * (1.0 - tanh * tanh) * (
            1.0 + (3 * 0.044715) * square
        )

    mix_grads = []
    lane = lax.broadcasted_iota(jnp.int32, share.shape, 1)
    share_grad = jnp.zeros(share.shape, F32)
    for t in range(tasks):
        mixture = jnp.zeros(act_ref.shape[1:], F32)
        for k in range(experts):
            column = t * experts + k
            mixture += share[:, column : column + 1] * act_ref[k]
        mixture = mixture.astype(BF16)
        tower_w = tower_in_ref[t]
        tower_pre = jnp.dot(mixture, tower_w, preferred_element_type=F32)
        tower_sig = jax.nn.sigmoid(tower_pre)
        tower_hid = tower_pre * tower_sig
        tower_vec = tower_out_ref[t : t + 1, :].astype(F32)
        task_logit = jnp.sum(tower_hid * tower_vec, 1, keepdims=True)
        mask = labels_ref[:, tasks + t : tasks + t + 1]
        error = jax.nn.sigmoid(task_logit) - labels_ref[:, t : t + 1]
        logit_grad = mask * error * loss_scale
        tower_out_grad_ref[t : t + 1, :] = jnp.sum(logit_grad * tower_hid, 0, keepdims=True)
        tower_grad = (
            (logit_grad * tower_vec) * tower_sig * (1.0 + tower_pre * (1.0 - tower_sig))
        ).astype(BF16)
        tower_in_grad_ref[t] = lax.dot_general(
            mixture, tower_grad, down, preferred_element_type=F32
        ).astype(BF16)
        mix_grad = lax.dot_general(tower_grad, tower_w, across, preferred_element_type=F32)
        mix_grads.append(mix_grad)
        for k in range(experts):
            value = jnp.sum(mix_grad * act_ref[k], 1, keepdims=True)
            share_grad = jnp.where(lane == t * experts + k, value, share_grad)

    for k in range(experts):
        act_grad = jnp.zeros(act_ref.shape[1:], F32)
        for t in range(tasks):
            column = t * experts + k
            act_grad += share[:, column : column + 1] * mix_grads[t]
        pre_grad_ref[:, k * width : (k + 1) * width] = (act_grad * slope_ref[k]).astype(BF16)

    sig_grad = (share_grad - task_sum(share * share_grad)) / gate_sum
    gate_grad_ref[...] = (sig_grad * sig * (1.0 - sig)).astype(BF16)


def student_grads(part, kept, taken, experts_w, gates_w, tower_w, tower_v, labels, loss_scale):
    rows = kept.shape[0]
    width = tower_w.shape[1]
    experts = experts_w.shape[1] // width
    vmem = pl.BlockSpec(memory_space=pltpu.VMEM)
    return pl.pallas_call(
        functools.partial(student_kernel, loss_scale=loss_scale),
        in_specs=[pl.BlockSpec(memory_space=pltpu.SMEM)] + [vmem] * 7,
        out_specs=[vmem] * 4,
        out_shape=[
            jax.ShapeDtypeStruct((rows, experts_w.shape[1]), BF16),
            jax.ShapeDtypeStruct((rows, gates_w.shape[1]), BF16),
            jax.ShapeDtypeStruct(tower_w.shape, BF16),
            jax.ShapeDtypeStruct(tower_v.shape, F32),
        ],
        scratch_shapes=[pltpu.VMEM((experts, rows, width), F32)] * 2,
        cost_estimate=pl.CostEstimate(
            flops=2 * rows * experts_w.size, bytes_accessed=2 * experts_w.size, transcendentals=0
        ),
        compiler_params=pltpu.CompilerParams(vmem_limit_bytes=32 * 1024 * 1024),
    )(part.reshape(1), kept, taken, experts_w, gates_w.T, tower_w, tower_v, labels)


def on_device(
    teacher_rows,
    expert_ids,
    router,
    teacher_up,
    teacher_down,
    student_experts,
    student_gates,
    tower_in,
    tower_out,
    soft_labels,
    label_masks,
):
    rows_dev, feature_dim = teacher_rows.shape
    expert_total = lax.axis_size("ep")
    width_parts = lax.axis_size("mp")
    group_index = lax.axis_index("grp")
    chips = expert_total * width_parts
    capacity = 4 * rows_dev // expert_total
    chunk_slots = capacity // SLOT_CHUNKS

    labels = swap(jnp.concatenate([soft_labels, label_masks.astype(F32)], 1), "grp")

    experts = jnp.arange(expert_total, dtype=jnp.int32)
    hot = [(expert_ids[:, c : c + 1] == experts[None, :]) for c in range(2)]
    named = (hot[0] | hot[1]).astype(BF16)
    sample = jnp.arange(rows_dev, dtype=jnp.int32)
    before = (sample[None, :] < sample[:, None]).astype(BF16)
    earlier = jnp.dot(before, named, preferred_element_type=F32)
    slots = [jnp.sum(jnp.where(h, earlier, 0.0), 1, keepdims=True).astype(jnp.int32) for h in hot]

    def places(chunk):
        found = []
        for c in range(2):
            local = slots[c] - chunk * chunk_slots
            inside = (local >= 0) & (local < chunk_slots)
            found.append(jnp.where(inside, expert_ids[:, c : c + 1] * chunk_slots + local, -1))
        return found

    lane = jnp.arange(expert_total * chunk_slots, dtype=jnp.int32)[None, :]
    targets = [places(chunk) for chunk in range(SLOT_CHUNKS)]

    received = []
    for first, second in targets:
        pick = ((lane == first) | (lane == second)).astype(BF16)
        outgoing = lax.dot_general(
            pick, teacher_rows, (((0,), (0,)), ((), ())), preferred_element_type=F32
        ).astype(BF16)
        outgoing = outgoing.reshape(expert_total, chunk_slots, feature_dim)
        received.append(lax.all_to_all(outgoing, "ep", split_axis=0, concat_axis=0, tiled=True))

    logits = jnp.dot(teacher_rows, router, preferred_element_type=F32)
    chosen = [jnp.sum(jnp.where(h, logits, 0.0), 1, keepdims=True) for h in hot]
    sigs = [jax.nn.sigmoid(v) for v in chosen]
    weights = [v / (sigs[0] + sigs[1]) for v in sigs]

    up_proj = teacher_up[0]
    down_proj = teacher_down[0]
    part = lax.axis_index("mp")
    half_width = feature_dim // width_parts
    mixed = jnp.zeros((rows_dev, half_width), F32)
    wide_lane = jnp.arange(chips * chunk_slots, dtype=jnp.int32)[None, :]
    wide_expert = wide_lane // (width_parts * chunk_slots)
    wide_place = wide_expert * chunk_slots + wide_lane % chunk_slots
    for chunk in range(SLOT_CHUNKS):
        rows_in = received[chunk].reshape(expert_total * chunk_slots, feature_dim)
        inner = jax.nn.gelu(jnp.dot(rows_in, up_proj, preferred_element_type=F32)).astype(BF16)
        partial = jnp.dot(inner, down_proj, preferred_element_type=F32).astype(BF16)
        outgoing = partial.reshape(expert_total, chunk_slots, width_parts, half_width)
        outgoing = outgoing.transpose(0, 2, 1, 3).reshape(chips, chunk_slots, half_width)
        returned = lax.all_to_all(outgoing, CHIPS, split_axis=0, concat_axis=0, tiled=True)
        returned = returned.reshape(chips * chunk_slots, half_width)
        first, second = targets[chunk]
        share = jnp.where(wide_place == first, weights[0], 0.0) + jnp.where(
            wide_place == second, weights[1], 0.0
        )
        high = share.astype(BF16)
        low = (share - high.astype(F32)).astype(BF16)
        mixed = mixed + jnp.dot(high, returned, preferred_element_type=F32)
        mixed = mixed + jnp.dot(low, returned, preferred_element_type=F32)
    mixed = mixed.astype(BF16)

    half_rows = rows_dev // width_parts
    kept = lax.dynamic_slice_in_dim(mixed, part * half_rows, half_rows, 0)
    given = lax.dynamic_slice_in_dim(mixed, (1 - part) * half_rows, half_rows, 0)
    taken = swap(given, "mp")
    kept_both = jnp.concatenate([kept, given], 0)
    all_rows = jnp.concatenate([kept_both, swap(kept_both, "grp")], 0)

    sample_total = rows_dev * lax.axis_size("grp") * expert_total
    pre_grad, gate_grad, grad_tower_in, grad_tower_out = student_grads(
        part,
        kept,
        taken,
        student_experts,
        student_gates,
        tower_in,
        tower_out,
        labels,
        1.0 / math.sqrt(sample_total),
    )

    def halves(array, axis):
        size = array.shape[axis] // 2
        mine = lax.dynamic_slice_in_dim(array, group_index * size, size, axis)
        theirs = lax.dynamic_slice_in_dim(array, (1 - group_index) * size, size, axis)
        return mine, theirs

    mine, theirs = halves(pre_grad, 1)
    gate_mine, gate_theirs = halves(gate_grad, 1)
    width, gate_width = mine.shape[1], gate_mine.shape[1]
    mine = jnp.concatenate([mine, gate_mine], 1)
    theirs = swap(jnp.concatenate([theirs, gate_theirs], 1), "grp")
    from_other = swap(jnp.concatenate([mine, theirs], 0), "mp")
    factors = jnp.concatenate([mine, from_other[:half_rows], theirs, from_other[half_rows:]], 0)
    contract = (((0,), (0,)), ((), ()))
    main = lax.dot_general(all_rows, factors[:, :width], contract, preferred_element_type=F32)
    gates = lax.dot_general(factors[:, width:], all_rows, contract, preferred_element_type=F32)
    mine, theirs = halves(grad_tower_in, 0)
    tower = (mine.astype(F32) + swap(theirs, "grp").astype(F32)).reshape(-1, grad_tower_in.shape[2])
    mine, theirs = halves(grad_tower_out.astype(BF16), 0)
    vector = (mine.astype(F32) + swap(theirs, "grp").astype(F32)).reshape(-1)

    tower_half = tower.shape[0] // 2
    tower = jnp.concatenate([tower[:tower_half], tower[tower_half:]], 1)
    rest = jnp.concatenate(
        [
            gates.reshape(-1),
            vector,
            jnp.zeros((2 * expert_total * width - gates.size - vector.size,), F32),
        ]
    )
    packed = jnp.concatenate(
        [
            main.astype(BF16).reshape(expert_total, -1, width),
            rest.astype(BF16).reshape(expert_total, -1, width),
            tower.astype(BF16).reshape(expert_total, -1, width),
        ],
        1,
    )

    parts = lax.all_to_all(packed, "ep", split_axis=0, concat_axis=0, tiled=True)
    total = jnp.sum(parts.astype(F32), 0).astype(BF16)
    spread = jnp.broadcast_to(total[None], (chips,) + total.shape)
    own_half = lax.all_to_all(spread, CHIPS, split_axis=0, concat_axis=0, tiled=True)
    other_half = swap(own_half, "grp")
    filled = unpack(own_half, group_index, chips, width_parts, ())
    main, tower, gates, vector = unpack(other_half, 1 - group_index, chips, width_parts, filled)
    return (
        main.reshape(student_experts.shape),
        gates.reshape(2 * gate_width, feature_dim).T,
        tower.reshape(tower_in.shape),
        vector.reshape(2, -1)[:, : tower_out.size // 2].reshape(tower_out.shape),
    )


def solution(mesh):
    return jax.shard_map(
        on_device,
        mesh=mesh,
        in_specs=(
            P(("grp", "ep"), None),
            P(("grp", "ep"), None),
            P(),
            P("ep", None, "mp"),
            P("ep", "mp", None),
            P(),
            P(),
            P(),
            P(),
            P(("grp", "ep", "mp"), None),
            P(("grp", "ep", "mp"), None),
        ),
        out_specs=(P(), P(), P(), P()),
        check_vma=False,
    )
```

time: 261 us -> 257 us (0.985)
  Pallas kernels: 4.3 us -> 11 us
  matrix products: 55.8 us -> 50.3 us
  other arithmetic: 4.33 us -> 1.41 us
    pallas_call x0 -> x1, Pallas kernels: none -> 5.74 us  [student_grads(): pl.pallas_call(functools.partial(student_kernel, loss_scale=loss_scale),...]
    dot_general x10 -> x0, matrix products: 5.64 us -> none  [the longest x1 2.94 us: student_grads(): pre_act = jnp.dot(rows_in, experts_w, preferred_element_type=F32)]
    pallas_call x1 -> x2, Pallas kernels: 4.3 us -> 5.24 us  [unpack(): pl.pallas_call(unpack_kernel, grid_spec=pltpu.PrefetchScalarGridSpec(num_...]
  transfers between devices with their start and end apart: 12 -> 12, of which waited for: 8 -> 8; matrix products, arithmetic and copies ran while one was open for 23% -> 20% of each run, Pallas kernels for 0% -> 3%
where the time goes in v3:
time: 257 us; the launch traced here: 256 us
  waiting for transfers between devices  65.1 us (25%)
  blocking collectives  61.7 us (24%)
  matrix products  50.3 us (20%)
  starting transfers between devices  50 us (19%)
  local copies, waits for them, and re-layouts  15.3 us (6%)
  Pallas kernels  11 us (4%)
    all_to_all x1, blocking collectives, on_device(): lax.all_to_all(spread, CHIPS, split_axis=0, concat_axis=0, tiled=True)  38.4 us
    dot_general x2, matrix products, on_device(): partial = jnp.dot(inner, down_proj, preferred_element_type=F32).astype(BF16)  32.5 us
    all_to_all x2, waiting for transfers between devices, on_device(): lax.all_to_all(outgoing, 'ep', split_axis=0, concat_axis=0, tiled=True)  28.6 us
    all_to_all x2, waiting for transfers between devices, on_device(): lax.all_to_all(outgoing, CHIPS, split_axis=0, concat_axis=0, tiled=True)  23.9 us
    all_to_all x1, blocking collectives, on_device(): lax.all_to_all(packed, 'ep', split_axis=0, concat_axis=0, tiled=True)  23.3 us
    ppermute x8, starting transfers between devices, swap(): return lax.ppermute(shard, axis, [(0, 1), (1, 0)])  17.2 us
    all_to_all x2, starting transfers between devices, on_device(): lax.all_to_all(outgoing, CHIPS, split_axis=0, concat_axis=0, tiled=True)  17 us
    all_to_all x2, starting transfers between devices, on_device(): lax.all_to_all(outgoing, 'ep', split_axis=0, concat_axis=0, tiled=True)  15.9 us
  transfers between devices with their start and end apart: 12, of which 8 were waited for; matrix products, arithmetic and copies ran while one was open for 20% of the time, Pallas kernels for 3%

profile of v3, /device:TPU:1, one launch (start us, length us, event | category | flops | bytes accessed | tf_op | source)
XLA Modules:
  0.0 255.8 jit_solution(301121168261489436)
XLA Ops:
  4.2 2.2 convolution_convert_fusion.1
  6.4 9.2 %all-to-all-start = ((bf16[32,16,2048]{2,1,0:T(8,128)(2,1)}), bf16[32,16,2048]{2,1,0:T(8,128)(2,1)S(1)}, u32[]{:S(2)}, u32[]{:S(2)}) async-start(bf16[32,16,2048]{2,1,0:T(8,128)(2,1)} %bitcast.7), calls=%async_computation | async-start | bytes 4194304 | tf_op jit(solution)/shard_map/all_to_all | solution.py:263
  15.7 2.2 convolution_convert_fusion
  17.9 24.3 %all-to-all-done = bf16[32,16,2048]{2,1,0:T(8,128)(2,1)S(1)} async-done(((bf16[32,16,2048]{2,1,0:T(8,128)(2,1)}), bf16[32,16,2048]{2,1,0:T(8,128)(2,1)S(1)}, u32[]{:S(2)}, u32[]{:S(2)}) %all-to-all-start) | async-done | bytes 2097184 | tf_op jit(solution)/shard_map/all_to_all | solution.py:263
  42.2 6.6 %all-to-all-start.2 = ((bf16[32,16,2048]{2,1,0:T(8,128)(2,1)}), bf16[32,16,2048]{2,1,0:T(8,128)(2,1)}, u32[]{:S(2)}, u32[]{:S(2)}) async-start(bf16[32,16,2048]{2,1,0:T(8,128)(2,1)} %bitcast.16), calls=%async_computation.2 | async-start | bytes 4194304 | tf_op jit(solution)/shard_map/all_to_all | solution.py:263
  48.8 16.0 %fusion.24 = bf16[512,2048]{1,0:T(8,128)(2,1)} fusion(bf16[1,2048,2048]{2,1,0:T(8,128)(2,1)} %param.15, bf16[512,2048]{1,0:T(8,128)(2,1)S(1)} %bitcast.77, bf16[1,2048,2048]{2,1,0:T(8,128)(2,1)} %param.14), kind=kOutput, calls=%fused_computation.28 | convolution fusion | flops 8600420352 | bytes 20971520 | tf_op jit(solution)/shard_map/dot_general | solution.py:281
  64.8 3.3 %reshape.281 = bf16[32,16,2,1024]{3,2,1,0:T(2,128)(2,1)S(1)} reshape(bf16[512,2048]{1,0:T(8,128)(2,1)} %fusion.24) | data formatting | bytes 4194304 | tf_op jit(solution)/shard_map/reshape | solution.py:282
  68.1 2.0 copy.25
  70.1 4.3 %all-to-all-done.2 = bf16[32,16,2048]{2,1,0:T(8,128)(2,1)} async-done(((bf16[32,16,2048]{2,1,0:T(8,128)(2,1)}), bf16[32,16,2048]{2,1,0:T(8,128)(2,1)}, u32[]{:S(2)}, u32[]{:S(2)}) %all-to-all-start.2) | async-done | bytes 2097184 | tf_op jit(solution)/shard_map/all_to_all | solution.py:263
  74.4 9.0 %all-to-all-start.1 = ((bf16[64,16,1024]{2,1,0:T(8,128)(2,1)}), bf16[64,16,1024]{2,1,0:T(8,128)(2,1)}, u32[]{:S(2)}, u32[]{:S(2)}) async-start(bf16[64,16,1024]{2,1,0:T(8,128)(2,1)} %bitcast.12), calls=%async_computation.1 | async-start | bytes 4194304 | tf_op jit(solution)/shard_map/all_to_all | solution.py:284
  83.3 16.6 %fusion.27 = bf16[512,2048]{1,0:T(8,128)(2,1)} fusion(bf16[1,2048,2048]{2,1,0:T(8,128)(2,1)} %param.15, bf16[512,2048]{1,0:T(8,128)(2,1)} %bitcast.17, bf16[1,2048,2048]{2,1,0:T(8,128)(2,1)} %param.14), kind=kOutput, calls=%fused_computation.29 | convolution fusion | flops 8600420352 | bytes 20971520 | tf_op jit(solution)/shard_map/dot_general | solution.py:281
  99.9 3.3 %reshape.286 = bf16[32,16,2,1024]{3,2,1,0:T(2,128)(2,1)S(1)} reshape(bf16[512,2048]{1,0:T(8,128)(2,1)} %fusion.27) | data formatting | bytes 4194304 | tf_op jit(solution)/shard_map/reshape | solution.py:282
  103.2 2.0 copy.26
  105.2 3.6 %all-to-all-done.1 = bf16[64,16,1024]{2,1,0:T(8,128)(2,1)} async-done(((bf16[64,16,1024]{2,1,0:T(8,128)(2,1)}), bf16[64,16,1024]{2,1,0:T(8,128)(2,1)}, u32[]{:S(2)}, u32[]{:S(2)}) %all-to-all-start.1) | async-done | bytes 2097184 | tf_op jit(solution)/shard_map/all_to_all | solution.py:284
  108.8 8.0 %all-to-all-start.3 = ((bf16[64,16,1024]{2,1,0:T(8,128)(2,1)}), bf16[64,16,1024]{2,1,0:T(8,128)(2,1)S(1)}, u32[]{:S(2)}, u32[]{:S(2)}) async-start(bf16[64,16,1024]{2,1,0:T(8,128)(2,1)} %bitcast.19), calls=%async_computation.3 | async-start | bytes 4194304 | tf_op jit(solution)/shard_map/all_to_all | solution.py:284
  116.9 2.4 fusion.68
  119.3 3.4 %convolution_add_fusion.2 = f32[256,1024]{1,0:T(8,128)} fusion(f32[256,1024]{1,0:T(8,128)S(1)} %fusion.68, bf16[1024,1024]{1,0:T(8,128)(2,1)} %bitcast.13, f32[256]{0:T(256)S(1)} %multiply_divide_fusion, f32[256]{0:T(256)S(1)} %get-tuple-element.34, s32[1024]{0:T(1024)S(1)} %fusion.95, s32[256]{0:T(256)S(1)} %bitcast.95, s32[256]{0:T(256)S(1)} %bitcast.92), kind=kOutput, calls=%fused_computation.41 | convolution fusion | flops 539492352 | bytes 4202496 | tf_op jit(solution)/shard_map/dot_general | solution.py:293
  122.7 20.4 %all-to-all-done.3 = bf16[64,16,1024]{2,1,0:T(8,128)(2,1)S(1)} async-done(((bf16[64,16,1024]{2,1,0:T(8,128)(2,1)}), bf16[64,16,1024]{2,1,0:T(8,128)(2,1)S(1)}, u32[]{:S(2)}, u32[]{:S(2)}) %all-to-all-start.3) | async-done | bytes 2097184 | tf_op jit(solution)/shard_map/all_to_all | solution.py:284
  143.1 2.1 convolution_add_fusion.1
  146.1 2.6 %collective-permute-start.1 = (bf16[128,1024]{1,0:T(8,128)(2,1)S(1)}, bf16[128,1024]{1,0:T(8,128)(2,1)S(1)}, u32[]{:S(2)}, u32[]{:S(2)}) collective-permute-start(bf16[128,1024]{1,0:T(8,128)(2,1)S(1)} %get-tuple-element.36), channel_id=1, source_target_pairs={{0,1},{1,0},{2,3},{3,2},{4,5},{5,4},{6,7},{7,6},{8,9},{9,8},{10,11... | collective-permute-start | bytes 786440 | tf_op jit(solution)/shard_map/ppermute | solution.py:19
  148.9 3.2 %collective-permute-start.2 = (f32[128,12]{1,0:T(8,128)S(1)}, f32[128,12]{1,0:T(8,128)S(1)}, u32[]{:S(2)}, u32[]{:S(2)}) collective-permute-start(f32[128,12]{1,0:T(8,128)S(1)} %copy.27), channel_id=1, source_target_pairs={{0,64},{64,0},{1,65},{65,1},{2,66},{66,2},{3,67},{67,3},{4,68},{68... | collective-permute-start | bytes 18440 | tf_op jit(solution)/shard_map/ppermute | solution.py:19
  152.9 2.2 copy-done.2
  155.1 5.7 %shard_map.138 = (bf16[128,1024]{1,0:T(8,128)(2,1)S(1)}, bf16[128,48]{1,0:T(8,128)(2,1)S(1)}, bf16[6,128,256]{2,1,0:T(8,128)(2,1)S(1)}, f32[6,256]{1,0:T(8,128)S(1)}) custom-call(s32[1]{0:T(128)} %bitcast.21.part_ref, bf16[128,1024]{1,0:T(8,128)(2,1)S(1)} %get-tuple-element.37.kept_ref, bf16[128,1024]{1,0:T(8,128)(2,1)S(1)} %collective-permute-done.1.taken_ref, ...), custom_call_target="tpu_custom_call" | custom-call | flops 536870912 | bytes 4194304 | tf_op jit(solution)/shard_map/pallas_call | solution.py:196
  160.9 5.5 %collective-permute-start.5 = (bf16[3,256]{1,0:T(4,128)(2,1)S(1)}, bf16[3,256]{1,0:T(4,128)(2,1)S(1)}, u32[]{:S(2)}, u32[]{:S(2)}) collective-permute-start(bf16[3,256]{1,0:T(4,128)(2,1)S(1)} %constant_dynamic-slice_fusion.1), channel_id=1, source_target_pairs={{0,64},{64,0},{1,65},{65,1},{2,66},{66,2},{3,67},{67,3},{4,68},{68... | collective-permute-start | bytes 4616 | tf_op jit(solution)/shard_map/ppermute | solution.py:19
  169.4 9.4 %collective-permute-done.4 = bf16[256,536]{1,0:T(8,128)(2,1)S(1)} collective-permute-done((bf16[256,536]{1,0:T(8,128)(2,1)S(1)}, bf16[256,536]{1,0:T(8,128)(2,1)S(1)}, u32[]{:S(2)}, u32[]{:S(2)}) %collective-permute-start.4) | collective-permute-done | bytes 274464 | tf_op jit(solution)/shard_map/ppermute | solution.py:19
  180.3 1.8 convolution_convert_fusion.2
  182.3 23.3 %all_to_all.30 = bf16[32,40,512]{2,1,0:T(8,128)(2,1)S(1)} all-to-all(bf16[32,40,512]{2,1,0:T(8,128)(2,1)S(1)} %maximum_maximum_fusion), channel_id=1, replica_groups=mesh['grp'=2,'ep'=32,'mp'=2] {'ep'}, dimensions={0} | all-to-all | bytes 2621440 | tf_op jit(solution)/shard_map/all_to_all | solution.py:355
  205.9 38.4 %all_to_all.31 = bf16[64,40,512]{2,1,0:T(8,128)(2,1)S(1)} all-to-all(bf16[64,40,512]{2,1,0:T(8,128)(2,1)S(1)} %broadcast_in_dim.65), channel_id=1, replica_groups=mesh['grp'=2,'ep'=32,'mp'=2] {'ep','mp'}, dimensions={0} | all-to-all | bytes 5242880 | tf_op jit(solution)/shard_map/all_to_all | solution.py:358
  244.3 3.8 %collective-permute-start.7 = (bf16[64,40,512]{2,1,0:T(8,128)(2,1)S(1)}, bf16[64,40,512]{2,1,0:T(8,128)(2,1)S(1)}, u32[]{:S(2)}, u32[]{:S(2)}) collective-permute-start(bf16[64,40,512]{2,1,0:T(8,128)(2,1)S(1)} %all_to_all.31), channel_id=1, source_target_pairs={{0,64},{64,0},{1,65},{65,1},{2,66},{66,2},{3,67},{67,3},{4,68},{68... | collective-permute-start | bytes 7864328 | tf_op jit(solution)/shard_map/ppermute | solution.py:19
  248.1 2.6 %shard_map.139 = (f32[2,1024,1024]{2,1,0:T(8,128)}, f32[2,2,192,256]{3,2,1,0:T(8,128)}, f32[2,24,2048]{2,1,0:T(8,128)}, f32[2,2,512]{2,1,0:T(2,128)S(1)}) custom-call(s32[1]{0:T(128)} %bitcast.26.place_ref, bf16[32,2,40,512]{3,2,1,0:T(8,128)(2,1)S(1)} %bitcast.70), custom_call_target="tpu_custom_call" | custom-call | flops 1310720 | bytes 7409664 | tf_op jit(solution)/shard_map/pallas_call | solution.py:68
  250.7 1.9 collective-permute-done.7
  252.6 2.6 %shard_map.140 = (f32[2,1024,1024]{2,1,0:T(8,128)}, f32[2,2,192,256]{3,2,1,0:T(8,128)}, f32[2,24,2048]{2,1,0:T(8,128)}, f32[2,2,512]{2,1,0:T(2,128)S(1)}) custom-call(s32[1]{0:T(128)} %bitcast.place_ref, bf16[32,2,40,512]{3,2,1,0:T(8,128)(2,1)S(1)} %bitcast.71, ...), custom_call_target="tpu_custom_call", output_to_operand_aliasing={{0}: (2, {}), {1}: (3, {}), {2}: (4, {}), {3}: (5, {})} | custom-call | flops 1310720 | bytes 7409664 | tf_op jit(solution)/shard_map/pallas_call | solution.py:68
  (66 shorter events, 11.1 us)
Async XLA Ops:
  0.6 1.3 copy-start
  6.4 35.7 %all-to-all-start = ((bf16[32,16,2048]{2,1,0:T(8,128)(2,1)}), bf16[32,16,2048]{2,1,0:T(8,128)(2,1)S(1)}, u32[]{:S(2)}, u32[]{:S(2)}) async-start(bf16[32,16,2048]{2,1,0:T(8,128)(2,1)} %bitcast.7), calls=%async_computation | async-start | bytes 4194304 | tf_op jit(solution)/shard_map/all_to_all | solution.py:263
  42.2 32.2 %all-to-all-start.2 = ((bf16[32,16,2048]{2,1,0:T(8,128)(2,1)}), bf16[32,16,2048]{2,1,0:T(8,128)(2,1)}, u32[]{:S(2)}, u32[]{:S(2)}) async-start(bf16[32,16,2048]{2,1,0:T(8,128)(2,1)} %bitcast.16), calls=%async_computation.2 | async-start | bytes 4194304 | tf_op jit(solution)/shard_map/all_to_all | solution.py:263
  74.4 34.4 %all-to-all-start.1 = ((bf16[64,16,1024]{2,1,0:T(8,128)(2,1)}), bf16[64,16,1024]{2,1,0:T(8,128)(2,1)}, u32[]{:S(2)}, u32[]{:S(2)}) async-start(bf16[64,16,1024]{2,1,0:T(8,128)(2,1)} %bitcast.12), calls=%async_computation.1 | async-start | bytes 4194304 | tf_op jit(solution)/shard_map/all_to_all | solution.py:284
  108.8 34.3 %all-to-all-start.3 = ((bf16[64,16,1024]{2,1,0:T(8,128)(2,1)}), bf16[64,16,1024]{2,1,0:T(8,128)(2,1)S(1)}, u32[]{:S(2)}, u32[]{:S(2)}) async-start(bf16[64,16,1024]{2,1,0:T(8,128)(2,1)} %bitcast.19), calls=%async_computation.3 | async-start | bytes 4194304 | tf_op jit(solution)/shard_map/all_to_all | solution.py:284
  145.1 3.6 %copy-start.6 = (s32[128,6]{0,1:T(8,128)S(1)}, s32[128,6]{0,1:T(8,128)}, u32[]{:S(2)}) copy-start(s32[128,6]{0,1:T(8,128)} %param.21) | copy-start | bytes 9220
  145.1 3.6 %copy-start.7 = (f32[128,6]{0,1:T(8,128)S(1)}, f32[128,6]{0,1:T(8,128)}, u32[]{:S(2)}) copy-start(f32[128,6]{0,1:T(8,128)} %param.20) | copy-start | bytes 9220
  146.0 6.9 %copy-start.3 = (bf16[6,128,256]{2,1,0:T(8,128)(2,1)S(1)}, bf16[6,128,256]{2,1,0:T(8,128)(2,1)}, u32[]{:S(2)}) copy-start(bf16[6,128,256]{2,1,0:T(8,128)(2,1)} %tower_in_ref.1) | copy-start | bytes 1179652
  146.0 6.9 %copy-start.4 = (bf16[2048,48]{0,1:T(8,128)(2,1)S(1)}, bf16[2048,48]{0,1:T(8,128)(2,1)}, u32[]{:S(2)}) copy-start(bf16[2048,48]{0,1:T(8,128)(2,1)} %param.17) | copy-start | bytes 589828
  146.0 6.9 %copy-start.5 = (bf16[6,256]{1,0:T(8,128)(2,1)S(1)}, bf16[6,256]{1,0:T(8,128)(2,1)}, u32[]{:S(2)}) copy-start(bf16[6,256]{1,0:T(8,128)(2,1)} %tower_out_ref.1) | copy-start | bytes 9220
  146.1 6.8 %collective-permute-start.1 = (bf16[128,1024]{1,0:T(8,128)(2,1)S(1)}, bf16[128,1024]{1,0:T(8,128)(2,1)S(1)}, u32[]{:S(2)}, u32[]{:S(2)}) collective-permute-start(bf16[128,1024]{1,0:T(8,128)(2,1)S(1)} %get-tuple-element.36), channel_id=1, source_target_pairs={{0,1},{1,0},{2,3},{3,2},{4,5},{5,4},{6,7},{7,6},{8,9},{9,8},{10,11... | collective-permute-start | bytes 786440 | tf_op jit(solution)/shard_map/ppermute | solution.py:19
  148.9 4.1 %collective-permute-start.2 = (f32[128,12]{1,0:T(8,128)S(1)}, f32[128,12]{1,0:T(8,128)S(1)}, u32[]{:S(2)}, u32[]{:S(2)}) collective-permute-start(f32[128,12]{1,0:T(8,128)S(1)} %copy.27), channel_id=1, source_target_pairs={{0,64},{64,0},{1,65},{65,1},{2,66},{66,2},{3,67},{67,3},{4,68},{68... | collective-permute-start | bytes 18440 | tf_op jit(solution)/shard_map/ppermute | solution.py:19
  152.0 26.8 %collective-permute-start = (bf16[256,1024]{1,0:T(8,128)(2,1)S(1)}, bf16[256,1024]{1,0:T(8,128)(2,1)}, u32[]{:S(2)}, u32[]{:S(2)}) collective-permute-start(bf16[256,1024]{1,0:T(8,128)(2,1)S(1)} %pad_maximum_fusion.2), channel_id=1, source_target_pairs={{0,64},{64,0},{1,65},{65,1},{2,66},{66,2},{3,67},{67,3},{4,68},{68... | collective-permute-start | bytes 1572872 | tf_op jit(solution)/shard_map/ppermute | solution.py:19
  152.9 2.2 copy-start.2
  160.9 6.3 %collective-permute-start.5 = (bf16[3,256]{1,0:T(4,128)(2,1)S(1)}, bf16[3,256]{1,0:T(4,128)(2,1)S(1)}, u32[]{:S(2)}, u32[]{:S(2)}) collective-permute-start(bf16[3,256]{1,0:T(4,128)(2,1)S(1)} %constant_dynamic-slice_fusion.1), channel_id=1, source_target_pairs={{0,64},{64,0},{1,65},{65,1},{2,66},{66,2},{3,67},{67,3},{4,68},{68... | collective-permute-start | bytes 4616 | tf_op jit(solution)/shard_map/ppermute | solution.py:19
  166.5 1.5 collective-permute-start.3
  166.6 2.6 %collective-permute-start.6 = (bf16[3,128,256]{2,1,0:T(8,128)(2,1)S(1)}, bf16[3,128,256]{2,1,0:T(8,128)(2,1)S(1)}, u32[]{:S(2)}, u32[]{:S(2)}) collective-permute-start(bf16[3,128,256]{2,1,0:T(8,128)(2,1)S(1)} %constant_dynamic-slice_fusion), channel_id=1, source_target_pairs={{0,64},{64,0},{1,65},{65,1},{2,66},{66,2},{3,67},{67,3},{4,68},{68... | collective-permute-start | bytes 589832 | tf_op jit(solution)/shard_map/ppermute | solution.py:19
  168.0 10.8 %collective-permute-start.4 = (bf16[256,536]{1,0:T(8,128)(2,1)S(1)}, bf16[256,536]{1,0:T(8,128)(2,1)S(1)}, u32[]{:S(2)}, u32[]{:S(2)}) collective-permute-start(bf16[256,536]{1,0:T(8,128)(2,1)S(1)} %pad_maximum_fusion.5), channel_id=1, source_target_pairs={{0,1},{1,0},{2,3},{3,2},{4,5},{5,4},{6,7},{7,6},{8,9},{9,8},{10,11... | collective-permute-start | bytes 823304 | tf_op jit(solution)/shard_map/ppermute | solution.py:19
  244.3 8.3 %collective-permute-start.7 = (bf16[64,40,512]{2,1,0:T(8,128)(2,1)S(1)}, bf16[64,40,512]{2,1,0:T(8,128)(2,1)S(1)}, u32[]{:S(2)}, u32[]{:S(2)}) collective-permute-start(bf16[64,40,512]{2,1,0:T(8,128)(2,1)S(1)} %all_to_all.31), channel_id=1, source_target_pairs={{0,64},{64,0},{1,65},{65,1},{2,66},{66,2},{3,67},{67,3},{4,68},{68... | collective-permute-start | bytes 7864328 | tf_op jit(solution)/shard_map/ppermute | solution.py:19
  252.6 3.2 %copy-start.1 = (bf16[256,2048]{1,0:T(8,128)(2,1)S(1)}, bf16[256,2048]{1,0:T(8,128)(2,1)}, u32[]{:S(2)}) copy-start(bf16[256,2048]{1,0:T(8,128)(2,1)} %param.11) | copy-start | bytes 3145732

commit v4 on v3

--- a/solution.py
+++ b/solution.py
@@ -12,6 +12,7 @@
 BF16 = jnp.bfloat16
 SLOT_CHUNKS = 2
 CHIPS = ("ep", "mp")
+PIECE = 2
 GATE_STEPS = 3
 
 
@@ -91,8 +92,102 @@
     )(place.astype(jnp.int32).reshape(1), half.reshape(outer, parts, each, width), *filled)
 
 
+def dispatch_kernel(ids_ref, rows_ref, out_ref, target_ref, *, experts, first_slot):
+    step = pl.program_id(0)
+    count = rows_ref.shape[0]
+    block_experts, slots, _ = out_ref.shape
+
+    @pl.when(step == 0)
+    def _():
+        ids = ids_ref[...]
+        expert = lax.broadcasted_iota(jnp.int32, (experts, count), 0)
+        hot = [expert == ids[c : c + 1] for c in range(2)]
+        named = jnp.where(hot[0] | hot[1], 1.0, 0.0).astype(BF16)
+        order = [lax.broadcasted_iota(jnp.int32, (count, count), d) for d in (0, 1)]
+        before = jnp.where(order[0] < order[1], 1.0, 0.0).astype(BF16)
+        earlier = jnp.dot(named, before, preferred_element_type=F32)
+        for c in range(2):
+            slot = jnp.sum(jnp.where(hot[c], earlier, 0.0), 0, keepdims=True).astype(jnp.int32)
+            local = slot - first_slot
+            inside = (local >= 0) & (local < slots)
+            target_ref[c : c + 1, :] = jnp.where(inside, ids[c : c + 1] * slots + local, -1)
+
+    block = block_experts * slots
+    place = step * block + lax.broadcasted_iota(jnp.int32, (block, count), 0)
+    chosen = (place == target_ref[0:1, :]) | (place == target_ref[1:2, :])
+    pick = jnp.where(chosen, 1.0, 0.0).astype(BF16)
+    rows = jnp.dot(pick, rows_ref[...], preferred_element_type=F32).astype(BF16)
+    out_ref[...] = rows.reshape(out_ref.shape)
+
+
+def dispatch(ids_by_choice, rows, experts, slots, first_slot):
+    count, feature_dim = rows.shape
+    block_experts = experts // 2
+    return pl.pallas_call(
+        functools.partial(dispatch_kernel, experts=experts, first_slot=first_slot),
+        grid=(2,),
+        in_specs=[
+            pl.BlockSpec((2, count), lambda i: (0, 0)),
+            pl.BlockSpec((count, feature_dim), lambda i: (0, 0)),
+        ],
+        out_specs=pl.BlockSpec((block_experts, slots, feature_dim), lambda i: (i, 0, 0)),
+        out_shape=jax.ShapeDtypeStruct((experts, slots, feature_dim), BF16),
+        scratch_shapes=[pltpu.VMEM((2, count), jnp.int32)],
+        cost_estimate=pl.CostEstimate(
+            flops=2 * experts * slots * rows.size,
+            bytes_accessed=2 * rows.size + 2 * experts * slots * feature_dim,
+            transcendentals=0,
+        ),
+        compiler_params=pltpu.CompilerParams(vmem_limit_bytes=48 * 1024 * 1024),
+    )(ids_by_choice, rows)
+
+
+def combine_kernel(part_ref, high_ref, low_ref, back_ref, so_far_ref, kept_ref, given_ref, both_ref):
+    back = back_ref[...]
+    mixed = so_far_ref[...] + jnp.dot(high_ref[...], back, preferred_element_type=F32)
+    mixed += jnp.dot(low_ref[...], back, preferred_element_type=F32)
+    half = kept_ref.shape[0]
+    first = part_ref[0] == 0
+    top, bottom = mixed[:half], mixed[half:]
+    kept = jnp.where(first, top, bottom).astype(BF16)
+    given = jnp.where(first, bottom, top).astype(BF16)
+    kept_ref[...] = kept
+    given_ref[...] = given
+    both_ref[:half] = kept
+    both_ref[half:] = given
+
+
+def combine(part, high, low, back, so_far):
+    rows, width = so_far.shape
+    slots = back.shape[0]
+    block = width // 2
+    whole = pl.BlockSpec((rows, slots), lambda i: (0, 0))
+    half = pl.BlockSpec((rows // 2, block), lambda i: (0, i))
+    return pl.pallas_call(
+        combine_kernel,
+        grid=(width // block,),
+        in_specs=[
+            pl.BlockSpec(memory_space=pltpu.SMEM),
+            whole,
+            whole,
+            pl.BlockSpec((slots, block), lambda i: (0, i)),
+            pl.BlockSpec((rows, block), lambda i: (0, i)),
+        ],
+        out_specs=[half, half, pl.BlockSpec((rows, block), lambda i: (0, i))],
+        out_shape=[
+            jax.ShapeDtypeStruct((rows // 2, width), BF16),
+            jax.ShapeDtypeStruct((rows // 2, width), BF16),
+            jax.ShapeDtypeStruct((rows, width), BF16),
+        ],
+        cost_estimate=pl.CostEstimate(
+            flops=4 * rows * back.size, bytes_accessed=2 * back.size, transcendentals=0
+        ),
+        compiler_params=pltpu.CompilerParams(vmem_limit_bytes=24 * 1024 * 1024),
+    )(part.reshape(1), high, low, back, so_far)
+
+
 def student_kernel(
-    part_ref,
+    place_ref,
     kept_ref,
     taken_ref,
     experts_ref,
@@ -100,20 +195,21 @@
     tower_in_ref,
     tower_out_ref,
     labels_ref,
-    pre_grad_ref,
-    gate_grad_ref,
-    tower_in_grad_ref,
-    tower_out_grad_ref,
+    mine_ref,
+    theirs_ref,
+    tower_mine_ref,
+    tower_theirs_ref,
     act_ref,
     slope_ref,
     *,
     loss_scale,
 ):
-    tasks, width, _ = tower_in_ref.shape
+    tasks, width, tower_width = tower_in_ref.shape
     columns = gates_ref.shape[0]
     experts = columns // tasks
     half = kept_ref.shape[1]
-    first = part_ref[0] == 0
+    first = place_ref[0] == 0
+    group = place_ref[1]
     left = jnp.where(first, kept_ref[...], taken_ref[...])
     right = jnp.where(first, taken_ref[...], kept_ref[...])
     across = (((1,), (1,)), ((), ()))
@@ -134,10 +230,13 @@
     share = sig / gate_sum
 
     scale = math.sqrt(2.0 / math.pi)
+    per_piece = PIECE
     for k in range(experts):
-        at = slice(k * width, (k + 1) * width)
-        pre = jnp.dot(left, experts_ref[:half, at], preferred_element_type=F32)
-        pre += jnp.dot(right, experts_ref[half:, at], preferred_element_type=F32)
+        if k % per_piece == 0:
+            at = slice(k * width, (k + per_piece) * width)
+            wide = jnp.dot(left, experts_ref[:half, at], preferred_element_type=F32)
+            wide += jnp.dot(right, experts_ref[half:, at], preferred_element_type=F32)
+        pre = wide[:, k % per_piece * width : (k % per_piece + 1) * width]
         square = pre * pre
         tanh = jnp.tanh(scale * (pre + 0.044715 * (square * pre)))
         cdf = 0.5 * (1.0 + tanh)
@@ -146,9 +245,13 @@
             1.0 + (3 * 0.044715) * square
         )
 
-    mix_grads = []
+    mix_grads, tower_in_grads = [], []
     lane = lax.broadcasted_iota(jnp.int32, share.shape, 1)
     share_grad = jnp.zeros(share.shape, F32)
+    per_group = tasks // 2
+    vector_rows = tower_mine_ref.shape[0] - per_group * width
+    vector_row = lax.broadcasted_iota(jnp.int32, (vector_rows, tower_width), 0)
+    vectors = [jnp.zeros((vector_rows, tower_width), F32)] * 2
     for t in range(tasks):
         mixture = jnp.zeros(act_ref.shape[1:], F32)
         for k in range(experts):
@@ -164,51 +267,173 @@
         mask = labels_ref[:, tasks + t : tasks + t + 1]
         error = jax.nn.sigmoid(task_logit) - labels_ref[:, t : t + 1]
         logit_grad = mask * error * loss_scale
-        tower_out_grad_ref[t : t + 1, :] = jnp.sum(logit_grad * tower_hid, 0, keepdims=True)
+        owner, local = t // per_group, t % per_group
+        vectors[owner] = jnp.where(
+            vector_row == local,
+            jnp.sum(logit_grad * tower_hid, 0, keepdims=True),
+            vectors[owner],
+        )
         tower_grad = (
             (logit_grad * tower_vec) * tower_sig * (1.0 + tower_pre * (1.0 - tower_sig))
         ).astype(BF16)
-        tower_in_grad_ref[t] = lax.dot_general(
-            mixture, tower_grad, down, preferred_element_type=F32
-        ).astype(BF16)
+        tower_in_grads.append(
+            lax.dot_general(mixture, tower_grad, down, preferred_element_type=F32)
+        )
         mix_grad = lax.dot_general(tower_grad, tower_w, across, preferred_element_type=F32)
         mix_grads.append(mix_grad)
         for k in range(experts):
             value = jnp.sum(mix_grad * act_ref[k], 1, keepdims=True)
             share_grad = jnp.where(lane == t * experts + k, value, share_grad)
 
-    for k in range(experts):
+    low_group = group == 0
+    for local in range(per_group):
+        at = slice(local * width, (local + 1) * width)
+        low, high = tower_in_grads[local], tower_in_grads[local + per_group]
+        tower_mine_ref[at] = jnp.where(low_group, low, high).astype(BF16)
+        tower_theirs_ref[at] = jnp.where(low_group, high, low).astype(BF16)
+    tower_mine_ref[per_group * width :] = jnp.where(low_group, vectors[0], vectors[1]).astype(BF16)
+    tower_theirs_ref[per_group * width :] = jnp.where(low_group, vectors[1], vectors[0]).astype(
+        BF16
+    )
+
+    def pre_grad(k):
         act_grad = jnp.zeros(act_ref.shape[1:], F32)
         for t in range(tasks):
             column = t * experts + k
             act_grad += share[:, column : column + 1] * mix_grads[t]
-        pre_grad_ref[:, k * width : (k + 1) * width] = (act_grad * slope_ref[k]).astype(BF16)
+        return act_grad * slope_ref[k]
+
+    for k in range(experts // 2):
+        at = slice(k * width, (k + 1) * width)
+        low, high = pre_grad(k), pre_grad(k + experts // 2)
+        mine_ref[:, at] = jnp.where(low_group, low, high).astype(BF16)
+        theirs_ref[:, at] = jnp.where(low_group, high, low).astype(BF16)
 
     sig_grad = (share_grad - task_sum(share * share_grad)) / gate_sum
-    gate_grad_ref[...] = (sig_grad * sig * (1.0 - sig)).astype(BF16)
-
-
-def student_grads(part, kept, taken, experts_w, gates_w, tower_w, tower_v, labels, loss_scale):
+    gate_grad = (sig_grad * sig * (1.0 - sig)).astype(BF16)
+    end = experts // 2 * width
+    lanes = mine_ref.shape[1] - end
+    source = lax.broadcasted_iota(jnp.int32, (columns, lanes), 0)
+    lane_at = lax.broadcasted_iota(jnp.int32, (columns, lanes), 1)
+    for ref, owner in ((mine_ref, group), (theirs_ref, 1 - group)):
+        wanted = (source == lane_at + owner * (columns // 2)) & (lane_at < columns // 2)
+        move = jnp.where(wanted, 1.0, 0.0).astype(BF16)
+        ref[:, end:] = jnp.dot(gate_grad, move, preferred_element_type=F32).astype(BF16)
+
+
+def student_grads(part, group, kept, taken, experts_w, gates_w, tower_w, tower_v, labels, loss_scale):
     rows = kept.shape[0]
-    width = tower_w.shape[1]
+    tasks, width, tower_width = tower_w.shape
     experts = experts_w.shape[1] // width
     vmem = pl.BlockSpec(memory_space=pltpu.VMEM)
+    factor = jax.ShapeDtypeStruct((rows, experts_w.shape[1] // 2 + 128), BF16)
+    tower = jax.ShapeDtypeStruct((tasks // 2 * width + 16, tower_width), BF16)
     return pl.pallas_call(
         functools.partial(student_kernel, loss_scale=loss_scale),
         in_specs=[pl.BlockSpec(memory_space=pltpu.SMEM)] + [vmem] * 7,
         out_specs=[vmem] * 4,
-        out_shape=[
-            jax.ShapeDtypeStruct((rows, experts_w.shape[1]), BF16),
-            jax.ShapeDtypeStruct((rows, gates_w.shape[1]), BF16),
-            jax.ShapeDtypeStruct(tower_w.shape, BF16),
-            jax.ShapeDtypeStruct(tower_v.shape, F32),
-        ],
+        out_shape=[factor, factor, tower, tower],
         scratch_shapes=[pltpu.VMEM((experts, rows, width), F32)] * 2,
         cost_estimate=pl.CostEstimate(
             flops=2 * rows * experts_w.size, bytes_accessed=2 * experts_w.size, transcendentals=0
         ),
-        compiler_params=pltpu.CompilerParams(vmem_limit_bytes=32 * 1024 * 1024),
-    )(part.reshape(1), kept, taken, experts_w, gates_w.T, tower_w, tower_v, labels)
+        compiler_params=pltpu.CompilerParams(vmem_limit_bytes=24 * 1024 * 1024),
+    )(
+        jnp.stack([part, group]).astype(jnp.int32),
+        kept,
+        taken,
+        experts_w,
+        gates_w.T,
+        tower_w,
+        tower_v,
+        labels,
+    )
+
+
+def pack_kernel(
+    own_rows_ref,
+    other_rows_ref,
+    mine_ref,
+    theirs_ref,
+    from_other_ref,
+    tower_mine_ref,
+    tower_theirs_ref,
+    out_ref,
+    rows_ref,
+    factor_ref,
+    tower_ref,
+    block_ref,
+):
+    blocks, each, width = out_ref.shape
+    count = mine_ref.shape[0]
+    main_rows = each - 8
+    down = (((0,), (0,)), ((), ()))
+    rows_ref[: 2 * count] = own_rows_ref[...]
+    rows_ref[2 * count :] = other_rows_ref[...]
+    factor_ref[:count] = mine_ref[...]
+    factor_ref[count : 2 * count] = from_other_ref[:count]
+    factor_ref[2 * count : 3 * count] = theirs_ref[...]
+    factor_ref[3 * count :] = from_other_ref[count:]
+    tower_ref[...] = tower_mine_ref[...].astype(F32) + tower_theirs_ref[...].astype(F32)
+    tower_rows = tower_ref.shape[0] - 16
+    window = tower_rows // 2 // blocks
+    gates = lax.dot_general(
+        factor_ref[:, width:], rows_ref[...], down, preferred_element_type=F32
+    )
+    gate_count = GATE_STEPS * 8
+    per_step = 8
+    for step in range(blocks // per_step):
+        at = step * per_step * main_rows
+        main = lax.dot_general(
+            rows_ref[:, at : at + per_step * main_rows],
+            factor_ref[:, :width],
+            down,
+            preferred_element_type=F32,
+        )
+        for local in range(per_step):
+            block = step * per_step + local
+            block_ref[:main_rows] = main[local * main_rows : (local + 1) * main_rows]
+            if block < gate_count:
+                block_ref[main_rows : main_rows + 1] = gates[block : block + 1, :width]
+                block_ref[main_rows + 1 : main_rows + 2] = gates[block : block + 1, width:]
+            else:
+                block_ref[main_rows : main_rows + 2] = jnp.zeros((2, width), F32)
+            if block == gate_count:
+                vectors = tower_ref[tower_rows:]
+                half = width // 2
+                block_ref[main_rows : main_rows + 1, :half] = vectors[0:1]
+                block_ref[main_rows : main_rows + 1, half:] = vectors[1:2]
+                block_ref[main_rows + 1 : main_rows + 2, :half] = vectors[2:3]
+            low = tower_ref[block * window : (block + 1) * window]
+            high = tower_ref[tower_rows // 2 + block * window : tower_rows // 2 + (block + 1) * window]
+            block_ref[main_rows + 2 : main_rows + 2 + window, : width // 2] = low
+            block_ref[main_rows + 2 : main_rows + 2 + window, width // 2 :] = high
+            out_ref[block] = block_ref[...].astype(BF16)
+
+
+def pack(own_rows, other_rows, mine, theirs, from_other, tower_mine, tower_theirs, blocks):
+    count, features = own_rows.shape
+    width = features // 2
+    each = features // blocks + 8
+    vmem = pl.BlockSpec(memory_space=pltpu.VMEM)
+    return pl.pallas_call(
+        pack_kernel,
+        in_specs=[vmem] * 7,
+        out_specs=vmem,
+        out_shape=jax.ShapeDtypeStruct((blocks, each, width), BF16),
+        scratch_shapes=[
+            pltpu.VMEM((2 * count, features), BF16),
+            pltpu.VMEM((2 * count, mine.shape[1]), BF16),
+            pltpu.VMEM(tower_mine.shape, F32),
+            pltpu.VMEM((each, width), F32),
+        ],
+        cost_estimate=pl.CostEstimate(
+            flops=4 * count * features * width,
+            bytes_accessed=2 * blocks * each * width,
+            transcendentals=0,
+        ),
+        compiler_params=pltpu.CompilerParams(vmem_limit_bytes=24 * 1024 * 1024),
+    )(own_rows, other_rows, mine, theirs, from_other, tower_mine, tower_theirs)
 
 
 def on_device(
@@ -250,16 +475,13 @@
             found.append(jnp.where(inside, expert_ids[:, c : c + 1] * chunk_slots + local, -1))
         return found
 
-    lane = jnp.arange(expert_total * chunk_slots, dtype=jnp.int32)[None, :]
     targets = [places(chunk) for chunk in range(SLOT_CHUNKS)]
 
     received = []
-    for first, second in targets:
-        pick = ((lane == first) | (lane == second)).astype(BF16)
-        outgoing = lax.dot_general(
-            pick, teacher_rows, (((0,), (0,)), ((), ())), preferred_element_type=F32
-        ).astype(BF16)
-        outgoing = outgoing.reshape(expert_total, chunk_slots, feature_dim)
+    for chunk in range(SLOT_CHUNKS):
+        outgoing = dispatch(
+            expert_ids.T, teacher_rows, expert_total, chunk_slots, chunk * chunk_slots
+        )
         received.append(lax.all_to_all(outgoing, "ep", split_axis=0, concat_axis=0, tiled=True))
 
     logits = jnp.dot(teacher_rows, router, preferred_element_type=F32)
@@ -289,20 +511,19 @@
         )
         high = share.astype(BF16)
         low = (share - high.astype(F32)).astype(BF16)
-        mixed = mixed + jnp.dot(high, returned, preferred_element_type=F32)
-        mixed = mixed + jnp.dot(low, returned, preferred_element_type=F32)
-    mixed = mixed.astype(BF16)
-
-    half_rows = rows_dev // width_parts
-    kept = lax.dynamic_slice_in_dim(mixed, part * half_rows, half_rows, 0)
-    given = lax.dynamic_slice_in_dim(mixed, (1 - part) * half_rows, half_rows, 0)
+        if chunk < SLOT_CHUNKS - 1:
+            mixed = mixed + jnp.dot(high, returned, preferred_element_type=F32)
+            mixed = mixed + jnp.dot(low, returned, preferred_element_type=F32)
+        else:
+            kept, given, both = combine(part, high, low, returned, mixed)
+
     taken = swap(given, "mp")
-    kept_both = jnp.concatenate([kept, given], 0)
-    all_rows = jnp.concatenate([kept_both, swap(kept_both, "grp")], 0)
+    other_both = swap(both, "grp")
 
     sample_total = rows_dev * lax.axis_size("grp") * expert_total
-    pre_grad, gate_grad, grad_tower_in, grad_tower_out = student_grads(
+    mine, theirs, tower_mine, tower_theirs = student_grads(
         part,
+        group_index,
         kept,
         taken,
         student_experts,
@@ -312,44 +533,11 @@
         labels,
         1.0 / math.sqrt(sample_total),
     )
-
-    def halves(array, axis):
-        size = array.shape[axis] // 2
-        mine = lax.dynamic_slice_in_dim(array, group_index * size, size, axis)
-        theirs = lax.dynamic_slice_in_dim(array, (1 - group_index) * size, size, axis)
-        return mine, theirs
-
-    mine, theirs = halves(pre_grad, 1)
-    gate_mine, gate_theirs = halves(gate_grad, 1)
-    width, gate_width = mine.shape[1], gate_mine.shape[1]
-    mine = jnp.concatenate([mine, gate_mine], 1)
-    theirs = swap(jnp.concatenate([theirs, gate_theirs], 1), "grp")
+    theirs = swap(theirs, "grp")
+    tower_theirs = swap(tower_theirs, "grp")
     from_other = swap(jnp.concatenate([mine, theirs], 0), "mp")
-    factors = jnp.concatenate([mine, from_other[:half_rows], theirs, from_other[half_rows:]], 0)
-    contract = (((0,), (0,)), ((), ()))
-    main = lax.dot_general(all_rows, factors[:, :width], contract, preferred_element_type=F32)
-    gates = lax.dot_general(factors[:, width:], all_rows, contract, preferred_element_type=F32)
-    mine, theirs = halves(grad_tower_in, 0)
-    tower = (mine.astype(F32) + swap(theirs, "grp").astype(F32)).reshape(-1, grad_tower_in.shape[2])
-    mine, theirs = halves(grad_tower_out.astype(BF16), 0)
-    vector = (mine.astype(F32) + swap(theirs, "grp").astype(F32)).reshape(-1)
-
-    tower_half = tower.shape[0] // 2
-    tower = jnp.concatenate([tower[:tower_half], tower[tower_half:]], 1)
-    rest = jnp.concatenate(
-        [
-            gates.reshape(-1),
-            vector,
-            jnp.zeros((2 * expert_total * width - gates.size - vector.size,), F32),
-        ]
-    )
-    packed = jnp.concatenate(
-        [
-            main.astype(BF16).reshape(expert_total, -1, width),
-            rest.astype(BF16).reshape(expert_total, -1, width),
-            tower.astype(BF16).reshape(expert_total, -1, width),
-        ],
-        1,
+    packed = pack(
+        both, other_both, mine, theirs, from_other, tower_mine, tower_theirs, expert_total
     )
 
     parts = lax.all_to_all(packed, "ep", split_axis=0, concat_axis=0, tiled=True)
@@ -361,7 +549,7 @@
     main, tower, gates, vector = unpack(other_half, 1 - group_index, chips, width_parts, filled)
     return (
         main.reshape(student_experts.shape),
-        gates.reshape(2 * gate_width, feature_dim).T,
+        gates.reshape(-1, feature_dim).T,
         tower.reshape(tower_in.shape),
         vector.reshape(2, -1)[:, : tower_out.size // 2].reshape(tower_out.shape),
     )

time: 257 us -> 258 us (level)
  matrix products: 50.3 us -> 39.6 us
  Pallas kernels: 11 us -> 20.7 us
  local copies, waits for them, and re-layouts: 15.3 us -> 19.6 us
    pallas_call x0 -> x4, Pallas kernels: none -> 7.6 us  [the longest x2 4.16 us: dispatch(): pl.pallas_call(functools.partial(dispatch_kernel, experts=experts, first_...]
    dot_general x4 -> x0, matrix products: 7.5 us -> none  [the longest x2 4.4 us: on_device(): lax.dot_general(pick, teacher_rows, (((0,), (0,)), ((), ())), preferred_e...]
    unnamed x18 -> x29, local copies, waits for them, and re-layouts: 2.7 us -> 8.11 us
    reshape x4 -> x3, local copies, waits for them, and re-layouts: 10.6 us -> 8.61 us  [on_device(): partial.reshape(expert_total, chunk_slots, width_parts, half_width)]
    ppermute x8 -> x7, waiting for transfers between devices: 12.6 us -> 12.5 us  [swap(): return lax.ppermute(shard, axis, [(0, 1), (1, 0)])]
    ppermute x8 -> x7, starting transfers between devices: 17.2 us -> 17.1 us  [swap(): return lax.ppermute(shard, axis, [(0, 1), (1, 0)])]
  transfers between devices with their start and end apart: 12 -> 11, of which waited for: 8 -> 9; matrix products, arithmetic and copies ran while one was open for 20% -> 20% of each run, Pallas kernels for 3% -> 2%
where the time goes in v4:
time: 258 us; the launch traced here: 257 us
  waiting for transfers between devices  63.1 us (24%)
  blocking collectives  61.2 us (24%)
  starting transfers between devices  51 us (20%)
  matrix products  39.6 us (15%)
  Pallas kernels  20.7 us (8%)
  local copies, waits for them, and re-layouts  19.6 us (8%)
    all_to_all x1, blocking collectives, on_device(): lax.all_to_all(spread, CHIPS, split_axis=0, concat_axis=0, tiled=True)  38.5 us
    dot_general x2, matrix products, on_device(): partial = jnp.dot(inner, down_proj, preferred_element_type=F32).astype(BF16)  33.1 us
    all_to_all x2, waiting for transfers between devices, on_device(): lax.all_to_all(outgoing, 'ep', split_axis=0, concat_axis=0, tiled=True)  28 us
    all_to_all x1, blocking collectives, on_device(): lax.all_to_all(packed, 'ep', split_axis=0, concat_axis=0, tiled=True)  22.7 us
    all_to_all x2, waiting for transfers between devices, on_device(): lax.all_to_all(outgoing, CHIPS, split_axis=0, concat_axis=0, tiled=True)  22.6 us
    all_to_all x2, starting transfers between devices, on_device(): lax.all_to_all(outgoing, CHIPS, split_axis=0, concat_axis=0, tiled=True)  17.9 us
    ppermute x7, starting transfers between devices, swap(): return lax.ppermute(shard, axis, [(0, 1), (1, 0)])  17.1 us
    all_to_all x2, starting transfers between devices, on_device(): lax.all_to_all(outgoing, 'ep', split_axis=0, concat_axis=0, tiled=True)  16 us
  transfers between devices with their start and end apart: 11, of which 9 were waited for; matrix products, arithmetic and copies ran while one was open for 20% of the time, Pallas kernels for 2%

profile of v4, /device:TPU:1, one launch (start us, length us, event | category | flops | bytes accessed | tf_op | source)
XLA Modules:
  0.0 256.6 jit_solution(14096364855729693210)
XLA Ops:
  0.7 1.3 copy-done.1
  2.6 2.1 shard_map.139
  4.7 9.4 %all-to-all-start.2 = ((bf16[32,16,2048]{2,1,0:T(8,128)(2,1)}), bf16[32,16,2048]{2,1,0:T(8,128)(2,1)}, u32[]{:S(2)}, u32[]{:S(2)}) async-start(bf16[32,16,2048]{2,1,0:T(8,128)(2,1)} %shard_map.139), calls=%async_computation.2 | async-start | bytes 4194304 | tf_op jit(solution)/shard_map/all_to_all | solution.py:485
  14.0 2.1 shard_map.138
  16.2 24.4 %all-to-all-done.2 = bf16[32,16,2048]{2,1,0:T(8,128)(2,1)} async-done(((bf16[32,16,2048]{2,1,0:T(8,128)(2,1)}), bf16[32,16,2048]{2,1,0:T(8,128)(2,1)}, u32[]{:S(2)}, u32[]{:S(2)}) %all-to-all-start.2) | async-done | bytes 2097184 | tf_op jit(solution)/shard_map/all_to_all | solution.py:485
  40.5 6.6 %all-to-all-start = ((bf16[32,16,2048]{2,1,0:T(8,128)(2,1)}), bf16[32,16,2048]{2,1,0:T(8,128)(2,1)}, u32[]{:S(2)}, u32[]{:S(2)}) async-start(bf16[32,16,2048]{2,1,0:T(8,128)(2,1)} %shard_map.138), calls=%async_computation | async-start | bytes 4194304 | tf_op jit(solution)/shard_map/all_to_all | solution.py:485
  47.2 16.6 %fusion.27 = bf16[512,2048]{1,0:T(8,128)(2,1)} fusion(bf16[1,2048,2048]{2,1,0:T(8,128)(2,1)} %param.15, bf16[512,2048]{1,0:T(8,128)(2,1)} %bitcast.17, bf16[1,2048,2048]{2,1,0:T(8,128)(2,1)} %param.14), kind=kOutput, calls=%fused_computation.27 | convolution fusion | flops 8600420352 | bytes 20971520 | tf_op jit(solution)/shard_map/dot_general | solution.py:503
  63.7 3.3 %reshape.255 = bf16[32,16,2,1024]{3,2,1,0:T(2,128)(2,1)S(1)} reshape(bf16[512,2048]{1,0:T(8,128)(2,1)} %fusion.27) | data formatting | bytes 4194304 | tf_op jit(solution)/shard_map/reshape | solution.py:504
  67.0 2.0 copy.27
  69.0 3.7 %all-to-all-done = bf16[32,16,2048]{2,1,0:T(8,128)(2,1)} async-done(((bf16[32,16,2048]{2,1,0:T(8,128)(2,1)}), bf16[32,16,2048]{2,1,0:T(8,128)(2,1)}, u32[]{:S(2)}, u32[]{:S(2)}) %all-to-all-start) | async-done | bytes 2097184 | tf_op jit(solution)/shard_map/all_to_all | solution.py:485
  72.7 9.9 %all-to-all-start.3 = ((bf16[64,16,1024]{2,1,0:T(8,128)(2,1)}), bf16[64,16,1024]{2,1,0:T(8,128)(2,1)}, u32[]{:S(2)}, u32[]{:S(2)}) async-start(bf16[64,16,1024]{2,1,0:T(8,128)(2,1)} %bitcast.19), calls=%async_computation.3 | async-start | bytes 4194304 | tf_op jit(solution)/shard_map/all_to_all | solution.py:506
  82.6 16.5 %fusion.24 = bf16[512,2048]{1,0:T(8,128)(2,1)} fusion(bf16[1,2048,2048]{2,1,0:T(8,128)(2,1)} %param.15, bf16[512,2048]{1,0:T(8,128)(2,1)} %bitcast.9, bf16[1,2048,2048]{2,1,0:T(8,128)(2,1)} %param.14), kind=kOutput, calls=%fused_computation.26 | convolution fusion | flops 8600420352 | bytes 20971520 | tf_op jit(solution)/shard_map/dot_general | solution.py:503
  99.1 3.3 %reshape.251 = bf16[32,16,2,1024]{3,2,1,0:T(2,128)(2,1)S(1)} reshape(bf16[512,2048]{1,0:T(8,128)(2,1)} %fusion.24) | data formatting | bytes 4194304 | tf_op jit(solution)/shard_map/reshape | solution.py:504
  102.4 2.0 copy.26
  104.4 3.4 %all-to-all-done.3 = bf16[64,16,1024]{2,1,0:T(8,128)(2,1)} async-done(((bf16[64,16,1024]{2,1,0:T(8,128)(2,1)}), bf16[64,16,1024]{2,1,0:T(8,128)(2,1)}, u32[]{:S(2)}, u32[]{:S(2)}) %all-to-all-start.3) | async-done | bytes 2097184 | tf_op jit(solution)/shard_map/all_to_all | solution.py:506
  107.8 8.0 %all-to-all-start.1 = ((bf16[64,16,1024]{2,1,0:T(8,128)(2,1)}), bf16[64,16,1024]{2,1,0:T(8,128)(2,1)S(1)}, u32[]{:S(2)}, u32[]{:S(2)}) async-start(bf16[64,16,1024]{2,1,0:T(8,128)(2,1)} %bitcast.66), calls=%async_computation.1 | async-start | bytes 4194304 | tf_op jit(solution)/shard_map/all_to_all | solution.py:506
  116.9 2.4 fusion.55
  119.3 3.5 %convolution_add_fusion.so_far_ref = f32[256,1024]{1,0:T(8,128)} fusion(f32[256,1024]{1,0:T(8,128)S(1)} %fusion.55, bf16[1024,1024]{1,0:T(8,128)(2,1)} %bitcast.20, f32[256]{0:T(256)S(1)} %multiply_divide_fusion, f32[256]{0:T(256)S(1)} %get-tuple-element.40, s32[1024]{0:T(1024)S(1)} %fusion.67, s32[256]{0:T(256)S(1)} %bitcast.82, s32[256]{0:T(256)S(1)} %bitcast.80), kind=kOutput, calls=%fused_computation.36 | convolution fusion | flops 539492352 | bytes 4202496 | tf_op jit(solution)/shard_map/dot_general | solution.py:516
  122.8 19.2 %all-to-all-done.1 = bf16[64,16,1024]{2,1,0:T(8,128)(2,1)S(1)} async-done(((bf16[64,16,1024]{2,1,0:T(8,128)(2,1)}), bf16[64,16,1024]{2,1,0:T(8,128)(2,1)S(1)}, u32[]{:S(2)}, u32[]{:S(2)}) %all-to-all-start.1) | async-done | bytes 2097184 | tf_op jit(solution)/shard_map/all_to_all | solution.py:506
  143.2 2.4 shard_map.140
  146.5 2.6 %collective-permute-start.1 = (bf16[128,1024]{1,0:T(8,128)(2,1)}, bf16[128,1024]{1,0:T(8,128)(2,1)S(1)}, u32[]{:S(2)}, u32[]{:S(2)}) collective-permute-start(bf16[128,1024]{1,0:T(8,128)(2,1)} %get-tuple-element.21), channel_id=1, source_target_pairs={{0,1},{1,0},{2,3},{3,2},{4,5},{5,4},{6,7},{7,6},{8,9},{9,8},{10,11... | collective-permute-start | bytes 786440 | tf_op jit(solution)/shard_map/ppermute | solution.py:20
  149.2 3.4 %collective-permute-start.2 = (f32[128,12]{1,0:T(8,128)S(1)}, f32[128,12]{1,0:T(8,128)S(1)}, u32[]{:S(2)}, u32[]{:S(2)}) collective-permute-start(f32[128,12]{1,0:T(8,128)S(1)} %copy.28), channel_id=1, source_target_pairs={{0,64},{64,0},{1,65},{65,1},{2,66},{66,2},{3,67},{67,3},{4,68},{68... | collective-permute-start | bytes 18440 | tf_op jit(solution)/shard_map/ppermute | solution.py:20
  153.5 2.2 copy-done.3
  157.6 5.9 %shard_map.141 = (bf16[128,640]{1,0:T(8,128)(2,1)S(1)}, bf16[128,640]{1,0:T(8,128)(2,1)S(1)}, bf16[400,256]{1,0:T(8,128)(2,1)S(1)}, bf16[400,256]{1,0:T(8,128)(2,1)S(1)}) custom-call(s32[2]{0:T(128)S(1)} %pad_add_fusion.place_ref, bf16[128,1024]{1,0:T(8,128)(2,1)S(1)} %get-tuple-element.20.kept_ref, bf16[128,1024]{1,0:T(8,128)(2,1)S(1)} %collective-permute-done.1.taken_ref, ...), custom_call_target="tpu_custom_call" | custom-call | flops 536870912 | bytes 4194304 | tf_op jit(solution)/shard_map/pallas_call | solution.py:331
  163.5 5.4 %collective-permute-start.3 = (bf16[128,640]{1,0:T(8,128)(2,1)S(1)}, bf16[128,640]{1,0:T(8,128)(2,1)S(1)}, u32[]{:S(2)}, u32[]{:S(2)}) collective-permute-start(bf16[128,640]{1,0:T(8,128)(2,1)S(1)} %get-tuple-element.23), channel_id=1, source_target_pairs={{0,64},{64,0},{1,65},{65,1},{2,66},{66,2},{3,67},{67,3},{4,68},{68... | collective-permute-start | bytes 491528 | tf_op jit(solution)/shard_map/ppermute | solution.py:20
  173.0 7.6 %collective-permute-done.4.from_other_ref = bf16[256,640]{1,0:T(8,128)(2,1)S(1)} collective-permute-done((bf16[256,640]{1,0:T(8,128)(2,1)S(1)}, bf16[256,640]{1,0:T(8,128)(2,1)S(1)}, u32[]{:S(2)}, u32[]{:S(2)}) %collective-permute-start.4) | collective-permute-done | bytes 327712 | tf_op jit(solution)/shard_map/ppermute | solution.py:20
  181.6 22.7 %all_to_all.30 = bf16[32,40,512]{2,1,0:T(8,128)(2,1)S(1)} all-to-all(bf16[32,40,512]{2,1,0:T(8,128)(2,1)S(1)} %shard_map.142), channel_id=1, replica_groups=mesh['grp'=2,'ep'=32,'mp'=2] {'ep'}, dimensions={0} | all-to-all | bytes 2621440 | tf_op jit(solution)/shard_map/all_to_all | solution.py:543
  204.6 38.5 %all_to_all.31 = bf16[64,40,512]{2,1,0:T(8,128)(2,1)S(1)} all-to-all(bf16[64,40,512]{2,1,0:T(8,128)(2,1)S(1)} %broadcast_in_dim.60), channel_id=1, replica_groups=mesh['grp'=2,'ep'=32,'mp'=2] {'ep','mp'}, dimensions={0} | all-to-all | bytes 5242880 | tf_op jit(solution)/shard_map/all_to_all | solution.py:546
  243.1 3.7 %collective-permute-start.6 = (bf16[64,40,512]{2,1,0:T(8,128)(2,1)S(1)}, bf16[64,40,512]{2,1,0:T(8,128)(2,1)}, u32[]{:S(2)}, u32[]{:S(2)}) collective-permute-start(bf16[64,40,512]{2,1,0:T(8,128)(2,1)S(1)} %all_to_all.31), channel_id=1, source_target_pairs={{0,64},{64,0},{1,65},{65,1},{2,66},{66,2},{3,67},{67,3},{4,68},{68... | collective-permute-start | bytes 7864328 | tf_op jit(solution)/shard_map/ppermute | solution.py:20
  246.8 2.6 %shard_map.143 = (f32[2,1024,1024]{2,1,0:T(8,128)}, f32[2,2,192,256]{3,2,1,0:T(8,128)}, f32[2,24,2048]{2,1,0:T(8,128)}, f32[2,2,512]{2,1,0:T(2,128)S(1)}) custom-call(s32[1]{0:T(128)} %bitcast.21.place_ref, bf16[32,2,40,512]{3,2,1,0:T(8,128)(2,1)S(1)} %bitcast.59), custom_call_target="tpu_custom_call" | custom-call | flops 1310720 | bytes 7409664 | tf_op jit(solution)/shard_map/pallas_call | solution.py:69
  249.4 2.0 collective-permute-done.6
  251.5 4.5 %shard_map.144 = (f32[2,1024,1024]{2,1,0:T(8,128)}, f32[2,2,192,256]{3,2,1,0:T(8,128)}, f32[2,24,2048]{2,1,0:T(8,128)}, f32[2,2,512]{2,1,0:T(2,128)S(1)}) custom-call(s32[1]{0:T(128)} %bitcast.place_ref, bf16[32,2,40,512]{3,2,1,0:T(8,128)(2,1)} %bitcast.23.half_ref, ...), custom_call_target="tpu_custom_call", output_to_operand_aliasing={{0}: (2, {}), {1}: (3, {}), {2}: (4, {}), {3}: (5, {})} | custom-call | flops 1310720 | bytes 7409664 | tf_op jit(solution)/shard_map/pallas_call | solution.py:69
  (55 shorter events, 12.6 us)
Async XLA Ops:
  0.6 115.4 %copy-start = (bf16[2048,32]{0,1:T(8,128)(2,1)S(1)}, bf16[2048,32]{0,1:T(8,128)(2,1)}, u32[]{:S(2)}) copy-start(bf16[2048,32]{0,1:T(8,128)(2,1)} %param.13) | copy-start | bytes 393220
  0.6 1.3 copy-start.1
  1.9 0.7 copy-start.9
  2.6 11.4 %copy-start.2 = (bf16[256,2048]{1,0:T(8,128)(2,1)S(1)}, bf16[256,2048]{1,0:T(8,128)(2,1)}, u32[]{:S(2)}) copy-start(bf16[256,2048]{1,0:T(8,128)(2,1)} %rows_ref.3) | copy-start | bytes 3145732
  2.6 11.4 %copy-start.10 = (s32[256,2]{0,1:T(2,128)S(1)}, s32[256,2]{0,1:T(2,128)}, u32[]{:S(2)}) copy-start(s32[256,2]{0,1:T(2,128)} %param.12) | copy-start | bytes 6148
  4.7 35.9 %all-to-all-start.2 = ((bf16[32,16,2048]{2,1,0:T(8,128)(2,1)}), bf16[32,16,2048]{2,1,0:T(8,128)(2,1)}, u32[]{:S(2)}, u32[]{:S(2)}) async-start(bf16[32,16,2048]{2,1,0:T(8,128)(2,1)} %shard_map.139), calls=%async_computation.2 | async-start | bytes 4194304 | tf_op jit(solution)/shard_map/all_to_all | solution.py:485
  40.5 32.2 %all-to-all-start = ((bf16[32,16,2048]{2,1,0:T(8,128)(2,1)}), bf16[32,16,2048]{2,1,0:T(8,128)(2,1)}, u32[]{:S(2)}, u32[]{:S(2)}) async-start(bf16[32,16,2048]{2,1,0:T(8,128)(2,1)} %shard_map.138), calls=%async_computation | async-start | bytes 4194304 | tf_op jit(solution)/shard_map/all_to_all | solution.py:485
  72.7 35.1 %all-to-all-start.3 = ((bf16[64,16,1024]{2,1,0:T(8,128)(2,1)}), bf16[64,16,1024]{2,1,0:T(8,128)(2,1)}, u32[]{:S(2)}, u32[]{:S(2)}) async-start(bf16[64,16,1024]{2,1,0:T(8,128)(2,1)} %bitcast.19), calls=%async_computation.3 | async-start | bytes 4194304 | tf_op jit(solution)/shard_map/all_to_all | solution.py:506
  107.8 34.2 %all-to-all-start.1 = ((bf16[64,16,1024]{2,1,0:T(8,128)(2,1)}), bf16[64,16,1024]{2,1,0:T(8,128)(2,1)S(1)}, u32[]{:S(2)}, u32[]{:S(2)}) async-start(bf16[64,16,1024]{2,1,0:T(8,128)(2,1)} %bitcast.66), calls=%async_computation.1 | async-start | bytes 4194304 | tf_op jit(solution)/shard_map/all_to_all | solution.py:506
  119.3 29.8 %copy-start.12 = (s32[128,6]{0,1:T(8,128)S(1)}, s32[128,6]{0,1:T(8,128)}, u32[]{:S(2)}) copy-start(s32[128,6]{0,1:T(8,128)} %param.21) | copy-start | bytes 9220
  119.3 29.8 %copy-start.13 = (f32[128,6]{0,1:T(8,128)S(1)}, f32[128,6]{0,1:T(8,128)}, u32[]{:S(2)}) copy-start(f32[128,6]{0,1:T(8,128)} %param.20) | copy-start | bytes 9220
  119.3 34.2 %copy-start.11 = (bf16[6,256]{1,0:T(8,128)(2,1)S(1)}, bf16[6,256]{1,0:T(8,128)(2,1)}, u32[]{:S(2)}) copy-start(bf16[6,256]{1,0:T(8,128)(2,1)} %tower_out_ref.1) | copy-start | bytes 9220
  142.0 1.2 copy-start.4
  145.7 0.8 copy-start.5
  146.5 7.0 %collective-permute-start.1 = (bf16[128,1024]{1,0:T(8,128)(2,1)}, bf16[128,1024]{1,0:T(8,128)(2,1)S(1)}, u32[]{:S(2)}, u32[]{:S(2)}) collective-permute-start(bf16[128,1024]{1,0:T(8,128)(2,1)} %get-tuple-element.21), channel_id=1, source_target_pairs={{0,1},{1,0},{2,3},{3,2},{4,5},{5,4},{6,7},{7,6},{8,9},{9,8},{10,11... | collective-permute-start | bytes 786440 | tf_op jit(solution)/shard_map/ppermute | solution.py:20
  149.2 4.3 %collective-permute-start.2 = (f32[128,12]{1,0:T(8,128)S(1)}, f32[128,12]{1,0:T(8,128)S(1)}, u32[]{:S(2)}, u32[]{:S(2)}) collective-permute-start(f32[128,12]{1,0:T(8,128)S(1)} %copy.28), channel_id=1, source_target_pairs={{0,64},{64,0},{1,65},{65,1},{2,66},{66,2},{3,67},{67,3},{4,68},{68... | collective-permute-start | bytes 18440 | tf_op jit(solution)/shard_map/ppermute | solution.py:20
  153.5 2.2 copy-start.3
  155.7 1.0 copy-start.7
  156.7 0.9 copy-start.8
  157.6 11.4 %copy-start.6 = (bf16[256,1024]{1,0:T(8,128)(2,1)S(1)}, bf16[256,1024]{1,0:T(8,128)(2,1)}, u32[]{:S(2)}) copy-start(bf16[256,1024]{1,0:T(8,128)(2,1)} %copy-done.5) | copy-start | bytes 1572868
  163.5 6.5 %collective-permute-start.3 = (bf16[128,640]{1,0:T(8,128)(2,1)S(1)}, bf16[128,640]{1,0:T(8,128)(2,1)S(1)}, u32[]{:S(2)}, u32[]{:S(2)}) collective-permute-start(bf16[128,640]{1,0:T(8,128)(2,1)S(1)} %get-tuple-element.23), channel_id=1, source_target_pairs={{0,64},{64,0},{1,65},{65,1},{2,66},{66,2},{3,67},{67,3},{4,68},{68... | collective-permute-start | bytes 491528 | tf_op jit(solution)/shard_map/ppermute | solution.py:20
  169.0 4.0 %collective-permute-start = (bf16[256,1024]{1,0:T(8,128)(2,1)S(1)}, bf16[256,1024]{1,0:T(8,128)(2,1)S(1)}, u32[]{:S(2)}, u32[]{:S(2)}) collective-permute-start(bf16[256,1024]{1,0:T(8,128)(2,1)S(1)} %copy-done.6), channel_id=1, source_target_pairs={{0,64},{64,0},{1,65},{65,1},{2,66},{66,2},{3,67},{67,3},{4,68},{68... | collective-permute-start | bytes 1572872 | tf_op jit(solution)/shard_map/ppermute | solution.py:20
  170.0 10.5 %collective-permute-start.4 = (bf16[256,640]{1,0:T(8,128)(2,1)S(1)}, bf16[256,640]{1,0:T(8,128)(2,1)S(1)}, u32[]{:S(2)}, u32[]{:S(2)}) collective-permute-start(bf16[256,640]{1,0:T(8,128)(2,1)S(1)} %pad_maximum_fusion), channel_id=1, source_target_pairs={{0,1},{1,0},{2,3},{3,2},{4,5},{5,4},{6,7},{7,6},{8,9},{9,8},{10,11... | collective-permute-start | bytes 983048 | tf_op jit(solution)/shard_map/ppermute | solution.py:20
  171.2 1.7 collective-permute-start.5
  243.1 8.4 %collective-permute-start.6 = (bf16[64,40,512]{2,1,0:T(8,128)(2,1)S(1)}, bf16[64,40,512]{2,1,0:T(8,128)(2,1)}, u32[]{:S(2)}, u32[]{:S(2)}) collective-permute-start(bf16[64,40,512]{2,1,0:T(8,128)(2,1)S(1)} %all_to_all.31), channel_id=1, source_target_pairs={{0,64},{64,0},{1,65},{65,1},{2,66},{66,2},{3,67},{67,3},{4,68},{68... | collective-permute-start | bytes 7864328 | tf_op jit(solution)/shard_map/ppermute | solution.py:20

commit v5 on v4

--- a/solution.py
+++ b/solution.py
@@ -12,7 +12,6 @@
 BF16 = jnp.bfloat16
 SLOT_CHUNKS = 2
 CHIPS = ("ep", "mp")
-PIECE = 2
 GATE_STEPS = 3
 
 
@@ -22,6 +21,7 @@
 
 def unpack_kernel(place_ref, half_ref, *refs):
     main_ref, tower_ref, gate_ref, vector_ref = refs[-4:]
+    earlier_ref = refs[0] if len(refs) > 4 else None
     blocks, parts, _, width = half_ref.shape
     main_rows = main_ref.shape[1] // blocks
     tower_rows = tower_ref.shape[2] // blocks
@@ -50,7 +50,20 @@
 
             @pl.when(step == GATE_STEPS)
             def _(rests=rests):
-                vector_ref[0] = sum(rests)
+                vectors = sum(rests)
+                pieces = [
+                    vectors[0:1, : width // 2],
+                    vectors[0:1, width // 2 :],
+                    vectors[1:2, : width // 2],
+                ]
+                low = place_ref[0] == 0
+                for i, value in enumerate(pieces):
+                    for own, row in ((low, i), (jnp.logical_not(low), i + len(pieces))):
+                        if earlier_ref is None:
+                            vector_ref[row : row + 1] = value
+                        else:
+                            kept = earlier_ref[row : row + 1]
+                            vector_ref[row : row + 1] = jnp.where(own, value, kept)
 
 
 def unpack(half, place, chips, parts, filled):
@@ -63,7 +76,7 @@
         jax.ShapeDtypeStruct((parts, outer * main_rows, 2 * width), F32),
         jax.ShapeDtypeStruct((2, 2, outer * tower_rows, tower_width), F32),
         jax.ShapeDtypeStruct((2, GATE_STEPS * step_blocks, 2 * parts * width), F32),
-        jax.ShapeDtypeStruct((2, 2, width), F32),
+        jax.ShapeDtypeStruct((6, tower_width), F32),
     ]
     size = sum(4 * math.prod(shape.shape) for shape in out_shape) // 2 + 2 * half.size
     return pl.pallas_call(
@@ -72,7 +85,8 @@
             num_scalar_prefetch=1,
             grid=(outer // step_blocks,),
             in_specs=[pl.BlockSpec((step_blocks, parts, each, width), lambda i, g: (i, 0, 0, 0))]
-            + [pl.BlockSpec(memory_space=pl.ANY)] * len(filled),
+            + ([pl.BlockSpec((6, tower_width), lambda i, g: (0, 0))] if filled else [])
+            + [pl.BlockSpec(memory_space=pl.ANY)] * (len(filled) - 1),
             out_specs=[
                 pl.BlockSpec((parts, step_blocks * main_rows, width), lambda i, g: (0, i, g[0])),
                 pl.BlockSpec(
@@ -82,14 +96,14 @@
                     (1, step_blocks, 2 * parts * width),
                     lambda i, g: (g[0], jnp.minimum(i, GATE_STEPS - 1), 0),
                 ),
-                pl.BlockSpec((1, 2, width), lambda i, g: (g[0], 0, 0)),
+                pl.BlockSpec((6, tower_width), lambda i, g: (0, 0)),
             ],
         ),
         out_shape=out_shape,
-        input_output_aliases={2 + i: i for i in range(len(filled))},
+        input_output_aliases={3 + i: i for i in range(len(filled) - 1)},
         cost_estimate=pl.CostEstimate(flops=half.size, bytes_accessed=size, transcendentals=0),
-        compiler_params=pltpu.CompilerParams(vmem_limit_bytes=32 * 1024 * 1024),
-    )(place.astype(jnp.int32).reshape(1), half.reshape(outer, parts, each, width), *filled)
+        compiler_params=pltpu.CompilerParams(vmem_limit_bytes=14 * 1024 * 1024),
+    )(place.astype(jnp.int32).reshape(1), half.reshape(outer, parts, each, width), *filled[3:], *filled[:3])
 
 
 def dispatch_kernel(ids_ref, rows_ref, out_ref, target_ref, *, experts, first_slot):
@@ -138,58 +152,83 @@
             bytes_accessed=2 * rows.size + 2 * experts * slots * feature_dim,
             transcendentals=0,
         ),
-        compiler_params=pltpu.CompilerParams(vmem_limit_bytes=48 * 1024 * 1024),
+        compiler_params=pltpu.CompilerParams(vmem_limit_bytes=56 * 1024 * 1024),
     )(ids_by_choice, rows)
 
 
-def combine_kernel(part_ref, high_ref, low_ref, back_ref, so_far_ref, kept_ref, given_ref, both_ref):
-    back = back_ref[...]
-    mixed = so_far_ref[...] + jnp.dot(high_ref[...], back, preferred_element_type=F32)
-    mixed += jnp.dot(low_ref[...], back, preferred_element_type=F32)
-    half = kept_ref.shape[0]
-    first = part_ref[0] == 0
-    top, bottom = mixed[:half], mixed[half:]
-    kept = jnp.where(first, top, bottom).astype(BF16)
-    given = jnp.where(first, bottom, top).astype(BF16)
-    kept_ref[...] = kept
-    given_ref[...] = given
-    both_ref[:half] = kept
-    both_ref[half:] = given
-
-
-def combine(part, high, low, back, so_far):
-    rows, width = so_far.shape
-    slots = back.shape[0]
-    block = width // 2
-    whole = pl.BlockSpec((rows, slots), lambda i: (0, 0))
-    half = pl.BlockSpec((rows // 2, block), lambda i: (0, i))
+def student_first_kernel(
+    part_ref,
+    kept_ref,
+    experts_ref,
+    gates_ref,
+    tower_ref,
+    pre_ref,
+    logit_ref,
+    experts_out_ref,
+    gates_out_ref,
+    tower_out_ref,
+    own_ref,
+    gates_own_ref,
+    sems,
+):
+    half = kept_ref.shape[1]
+    part = part_ref[0]
+    own = pl.ds(pl.multiple_of(part * half, half), half)
+    other = pl.ds(pl.multiple_of((1 - part) * half, half), half)
+    copies = [
+        pltpu.make_async_copy(experts_ref.at[own], own_ref, sems.at[0]),
+        pltpu.make_async_copy(gates_ref.at[:, own], gates_own_ref, sems.at[1]),
+        pltpu.make_async_copy(experts_ref.at[other], experts_out_ref, sems.at[2]),
+        pltpu.make_async_copy(gates_ref.at[:, other], gates_out_ref, sems.at[3]),
+        pltpu.make_async_copy(tower_ref, tower_out_ref, sems.at[4]),
+    ]
+    for copy in copies:
+        copy.start()
+    kept = kept_ref[...]
+    copies[0].wait()
+    pre_ref[...] = jnp.dot(kept, own_ref[...], preferred_element_type=F32)
+    copies[1].wait()
+    logit_ref[...] = lax.dot_general(
+        kept, gates_own_ref[...], (((1,), (1,)), ((), ())), preferred_element_type=F32
+    )
+    for copy in copies[2:]:
+        copy.wait()
+
+
+def student_first(part, kept, experts_w, gates_t, tower_w):
+    rows, half = kept.shape
+    vmem = pl.BlockSpec(memory_space=pltpu.VMEM)
+    anywhere = pl.BlockSpec(memory_space=pl.ANY)
+    experts_half = (half, experts_w.shape[1])
+    gates_half = (gates_t.shape[0], half)
     return pl.pallas_call(
-        combine_kernel,
-        grid=(width // block,),
-        in_specs=[
-            pl.BlockSpec(memory_space=pltpu.SMEM),
-            whole,
-            whole,
-            pl.BlockSpec((slots, block), lambda i: (0, i)),
-            pl.BlockSpec((rows, block), lambda i: (0, i)),
+        student_first_kernel,
+        in_specs=[pl.BlockSpec(memory_space=pltpu.SMEM), vmem, anywhere, anywhere, anywhere],
+        out_specs=[vmem] * 5,
+        out_shape=[
+            jax.ShapeDtypeStruct((rows, experts_w.shape[1]), F32),
+            jax.ShapeDtypeStruct((rows, gates_t.shape[0]), F32),
+            jax.ShapeDtypeStruct(experts_half, BF16),
+            jax.ShapeDtypeStruct(gates_half, BF16),
+            jax.ShapeDtypeStruct(tower_w.shape, BF16),
         ],
-        out_specs=[half, half, pl.BlockSpec((rows, block), lambda i: (0, i))],
-        out_shape=[
-            jax.ShapeDtypeStruct((rows // 2, width), BF16),
-            jax.ShapeDtypeStruct((rows // 2, width), BF16),
-            jax.ShapeDtypeStruct((rows, width), BF16),
+        scratch_shapes=[
+            pltpu.VMEM(experts_half, BF16),
+            pltpu.VMEM(gates_half, BF16),
+            pltpu.SemaphoreType.DMA((5,)),
         ],
         cost_estimate=pl.CostEstimate(
-            flops=4 * rows * back.size, bytes_accessed=2 * back.size, transcendentals=0
+            flops=rows * experts_w.size, bytes_accessed=2 * experts_w.size, transcendentals=0
         ),
-        compiler_params=pltpu.CompilerParams(vmem_limit_bytes=24 * 1024 * 1024),
-    )(part.reshape(1), high, low, back, so_far)
+        compiler_params=pltpu.CompilerParams(vmem_limit_bytes=14 * 1024 * 1024),
+    )(part.reshape(1), kept, experts_w, gates_t, tower_w)
 
 
 def student_kernel(
-    place_ref,
-    kept_ref,
+    group_ref,
     taken_ref,
+    first_pre_ref,
+    first_logit_ref,
     experts_ref,
     gates_ref,
     tower_in_ref,
@@ -207,16 +246,14 @@
     tasks, width, tower_width = tower_in_ref.shape
     columns = gates_ref.shape[0]
     experts = columns // tasks
-    half = kept_ref.shape[1]
-    first = place_ref[0] == 0
-    group = place_ref[1]
-    left = jnp.where(first, kept_ref[...], taken_ref[...])
-    right = jnp.where(first, taken_ref[...], kept_ref[...])
+    group = group_ref[0]
+    taken = taken_ref[...]
     across = (((1,), (1,)), ((), ()))
     down = (((0,), (0,)), ((), ()))
 
-    logit = lax.dot_general(left, gates_ref[:, :half], across, preferred_element_type=F32)
-    logit += lax.dot_general(right, gates_ref[:, half:], across, preferred_element_type=F32)
+    logit = first_logit_ref[...] + lax.dot_general(
+        taken, gates_ref[...], across, preferred_element_type=F32
+    )
     sig = jax.nn.sigmoid(logit)
     task_of = [lax.broadcasted_iota(jnp.int32, (columns, columns), d) // experts for d in (0, 1)]
     same_task = jnp.where(task_of[0] == task_of[1], 1.0, 0.0)
@@ -230,12 +267,12 @@
     share = sig / gate_sum
 
     scale = math.sqrt(2.0 / math.pi)
-    per_piece = PIECE
+    per_piece = 2
     for k in range(experts):
         if k % per_piece == 0:
             at = slice(k * width, (k + per_piece) * width)
-            wide = jnp.dot(left, experts_ref[:half, at], preferred_element_type=F32)
-            wide += jnp.dot(right, experts_ref[half:, at], preferred_element_type=F32)
+            wide = first_pre_ref[:, at]
+            wide += jnp.dot(taken, experts_ref[:, at], preferred_element_type=F32)
         pre = wide[:, k % per_piece * width : (k % per_piece + 1) * width]
         square = pre * pre
         tanh = jnp.tanh(scale * (pre + 0.044715 * (square * pre)))
@@ -321,41 +358,34 @@
         ref[:, end:] = jnp.dot(gate_grad, move, preferred_element_type=F32).astype(BF16)
 
 
-def student_grads(part, group, kept, taken, experts_w, gates_w, tower_w, tower_v, labels, loss_scale):
-    rows = kept.shape[0]
+def student_grads(group, taken, first_part, tower_v, labels, loss_scale):
+    pre, _, _, _, tower_w = first_part
+    rows, columns = pre.shape
     tasks, width, tower_width = tower_w.shape
-    experts = experts_w.shape[1] // width
+    experts = columns // width
     vmem = pl.BlockSpec(memory_space=pltpu.VMEM)
-    factor = jax.ShapeDtypeStruct((rows, experts_w.shape[1] // 2 + 128), BF16)
+    factor = jax.ShapeDtypeStruct((rows, columns // 2 + 128), BF16)
     tower = jax.ShapeDtypeStruct((tasks // 2 * width + 16, tower_width), BF16)
     return pl.pallas_call(
         functools.partial(student_kernel, loss_scale=loss_scale),
-        in_specs=[pl.BlockSpec(memory_space=pltpu.SMEM)] + [vmem] * 7,
+        in_specs=[pl.BlockSpec(memory_space=pltpu.SMEM)] + [vmem] * 8,
         out_specs=[vmem] * 4,
         out_shape=[factor, factor, tower, tower],
         scratch_shapes=[pltpu.VMEM((experts, rows, width), F32)] * 2,
         cost_estimate=pl.CostEstimate(
-            flops=2 * rows * experts_w.size, bytes_accessed=2 * experts_w.size, transcendentals=0
+            flops=rows * taken.shape[1] * columns, bytes_accessed=4 * pre.size, transcendentals=0
         ),
-        compiler_params=pltpu.CompilerParams(vmem_limit_bytes=24 * 1024 * 1024),
-    )(
-        jnp.stack([part, group]).astype(jnp.int32),
-        kept,
-        taken,
-        experts_w,
-        gates_w.T,
-        tower_w,
-        tower_v,
-        labels,
-    )
+        compiler_params=pltpu.CompilerParams(vmem_limit_bytes=14 * 1024 * 1024),
+    )(group.reshape(1), taken, *first_part, tower_v, labels)
 
 
 def pack_kernel(
     own_rows_ref,
     other_rows_ref,
     mine_ref,
+    from_part_ref,
     theirs_ref,
-    from_other_ref,
+    from_far_ref,
     tower_mine_ref,
     tower_theirs_ref,
     out_ref,
@@ -371,9 +401,9 @@
     rows_ref[: 2 * count] = own_rows_ref[...]
     rows_ref[2 * count :] = other_rows_ref[...]
     factor_ref[:count] = mine_ref[...]
-    factor_ref[count : 2 * count] = from_other_ref[:count]
+    factor_ref[count : 2 * count] = from_part_ref[...]
     factor_ref[2 * count : 3 * count] = theirs_ref[...]
-    factor_ref[3 * count :] = from_other_ref[count:]
+    factor_ref[3 * count :] = from_far_ref[...]
     tower_ref[...] = tower_mine_ref[...].astype(F32) + tower_theirs_ref[...].astype(F32)
     tower_rows = tower_ref.shape[0] - 16
     window = tower_rows // 2 // blocks
@@ -411,14 +441,14 @@
             out_ref[block] = block_ref[...].astype(BF16)
 
 
-def pack(own_rows, other_rows, mine, theirs, from_other, tower_mine, tower_theirs, blocks):
+def pack(own_rows, other_rows, mine, from_part, theirs, from_far, tower_mine, tower_theirs, blocks):
     count, features = own_rows.shape
     width = features // 2
     each = features // blocks + 8
     vmem = pl.BlockSpec(memory_space=pltpu.VMEM)
     return pl.pallas_call(
         pack_kernel,
-        in_specs=[vmem] * 7,
+        in_specs=[vmem] * 8,
         out_specs=vmem,
         out_shape=jax.ShapeDtypeStruct((blocks, each, width), BF16),
         scratch_shapes=[
@@ -432,8 +462,8 @@
             bytes_accessed=2 * blocks * each * width,
             transcendentals=0,
         ),
-        compiler_params=pltpu.CompilerParams(vmem_limit_bytes=24 * 1024 * 1024),
-    )(own_rows, other_rows, mine, theirs, from_other, tower_mine, tower_theirs)
+        compiler_params=pltpu.CompilerParams(vmem_limit_bytes=14 * 1024 * 1024),
+    )(own_rows, other_rows, mine, from_part, theirs, from_far, tower_mine, tower_theirs)
 
 
 def on_device(
@@ -511,33 +541,28 @@
         )
         high = share.astype(BF16)
         low = (share - high.astype(F32)).astype(BF16)
-        if chunk < SLOT_CHUNKS - 1:
-            mixed = mixed + jnp.dot(high, returned, preferred_element_type=F32)
-            mixed = mixed + jnp.dot(low, returned, preferred_element_type=F32)
-        else:
-            kept, given, both = combine(part, high, low, returned, mixed)
-
+        mixed = mixed + jnp.dot(high, returned, preferred_element_type=F32)
+        mixed = mixed + jnp.dot(low, returned, preferred_element_type=F32)
+    mixed = mixed.astype(BF16)
+
+    half_rows = rows_dev // width_parts
+    kept = lax.dynamic_slice_in_dim(mixed, part * half_rows, half_rows, 0)
+    given = lax.dynamic_slice_in_dim(mixed, (1 - part) * half_rows, half_rows, 0)
     taken = swap(given, "mp")
-    other_both = swap(both, "grp")
-
+    first_part = student_first(part, kept, student_experts, student_gates.T, tower_in)
     sample_total = rows_dev * lax.axis_size("grp") * expert_total
     mine, theirs, tower_mine, tower_theirs = student_grads(
-        part,
-        group_index,
-        kept,
-        taken,
-        student_experts,
-        student_gates,
-        tower_in,
-        tower_out,
-        labels,
-        1.0 / math.sqrt(sample_total),
-    )
+        group_index, taken, first_part, tower_out, labels, 1.0 / math.sqrt(sample_total)
+    )
+    from_part = swap(mine, "mp")
+    from_far = lax.ppermute(theirs, ("grp", "mp"), [(i, 3 - i) for i in range(4)])
     theirs = swap(theirs, "grp")
     tower_theirs = swap(tower_theirs, "grp")
-    from_other = swap(jnp.concatenate([mine, theirs], 0), "mp")
+    own_kept, own_given, mine = lax.optimization_barrier((kept, given, mine))
+    both = jnp.concatenate([own_kept, own_given], 0)
+    other_both = swap(both, "grp")
     packed = pack(
-        both, other_both, mine, theirs, from_other, tower_mine, tower_theirs, expert_total
+        both, other_both, mine, from_part, theirs, from_far, tower_mine, tower_theirs, expert_total
     )
 
     parts = lax.all_to_all(packed, "ep", split_axis=0, concat_axis=0, tiled=True)
@@ -551,7 +576,7 @@
         main.reshape(student_experts.shape),
         gates.reshape(-1, feature_dim).T,
         tower.reshape(tower_in.shape),
-        vector.reshape(2, -1)[:, : tower_out.size // 2].reshape(tower_out.shape),
+        vector,
     )
 
 

time: 258 us -> 250 us (0.969)
  local copies, waits for them, and re-layouts: 19.6 us -> 13.2 us
  starting transfers between devices: 51 us -> 47.8 us
  waiting for transfers between devices: 63.1 us -> 60.3 us
    ppermute x7, waiting for transfers between devices: 12.5 us -> 5.37 us  [swap(): return lax.ppermute(shard, axis, [(0, 1), (1, 0)])]
    unnamed x29 -> x19, local copies, waits for them, and re-layouts: 8.11 us -> 2.26 us
    ppermute x7, starting transfers between devices: 17.1 us -> 12.8 us  [swap(): return lax.ppermute(shard, axis, [(0, 1), (1, 0)])]
    ppermute x0 -> x1, waiting for transfers between devices: none -> 4.07 us  [on_device(): lax.ppermute(theirs, ('grp', 'mp'), [(i, 3 - i) for i in range(4)])]
    reshape x3 -> x4, local copies, waits for them, and re-layouts: 8.61 us -> 10.6 us  [on_device(): partial.reshape(expert_total, chunk_slots, width_parts, half_width)]
  transfers between devices with their start and end apart: 11 -> 12, of which waited for: 9 -> 7; matrix products, arithmetic and copies ran while one was open for 20% -> 20% of each run, Pallas kernels for 2% -> 3%
where the time goes in v5:
time: 250 us; the launch traced here: 249 us
  blocking collectives  63.3 us (25%)
  waiting for transfers between devices  60.3 us (24%)
  starting transfers between devices  47.8 us (19%)
  matrix products  41.8 us (17%)
  Pallas kernels  21.3 us (9%)
  local copies, waits for them, and re-layouts  13.2 us (5%)
    all_to_all x1, blocking collectives, on_device(): lax.all_to_all(spread, CHIPS, split_axis=0, concat_axis=0, tiled=True)  38.8 us
    dot_general x2, matrix products, on_device(): partial = jnp.dot(inner, down_proj, preferred_element_type=F32).astype(BF16)  32.5 us
    all_to_all x2, waiting for transfers between devices, on_device(): lax.all_to_all(outgoing, 'ep', split_axis=0, concat_axis=0, tiled=True)  27.7 us
    all_to_all x1, blocking collectives, on_device(): lax.all_to_all(packed, 'ep', split_axis=0, concat_axis=0, tiled=True)  24.5 us
    all_to_all x2, waiting for transfers between devices, on_device(): lax.all_to_all(outgoing, CHIPS, split_axis=0, concat_axis=0, tiled=True)  23.2 us
    all_to_all x2, starting transfers between devices, on_device(): lax.all_to_all(outgoing, CHIPS, split_axis=0, concat_axis=0, tiled=True)  16.7 us
    all_to_all x2, starting transfers between devices, on_device(): lax.all_to_all(outgoing, 'ep', split_axis=0, concat_axis=0, tiled=True)  15.9 us
    ppermute x7, starting transfers between devices, swap(): return lax.ppermute(shard, axis, [(0, 1), (1, 0)])  12.8 us
  transfers between devices with their start and end apart: 12, of which 7 were waited for; matrix products, arithmetic and copies ran while one was open for 20% of the time, Pallas kernels for 3%

profile of v5, /device:TPU:1, one launch (start us, length us, event | category | flops | bytes accessed | tf_op | source)
XLA Modules:
  0.0 249.2 jit_solution(17758532794379044088)
XLA Ops:
  0.6 3.4 %shard_map.138 = bf16[32,16,2048]{2,1,0:T(8,128)(2,1)} custom-call(s32[2,256]{1,0:T(2,128)} %bitcast.68, bf16[256,2048]{1,0:T(8,128)(2,1)} %rows_ref.3), custom_call_target="tpu_custom_call" | custom-call | flops 536870912 | bytes 3145728 | tf_op jit(solution)/shard_map/pallas_call | solution.py:140
  4.0 9.2 %all-to-all-start = ((bf16[32,16,2048]{2,1,0:T(8,128)(2,1)}), bf16[32,16,2048]{2,1,0:T(8,128)(2,1)S(1)}, u32[]{:S(2)}, u32[]{:S(2)}) async-start(bf16[32,16,2048]{2,1,0:T(8,128)(2,1)} %shard_map.138), calls=%async_computation | async-start | bytes 4194304 | tf_op jit(solution)/shard_map/all_to_all | solution.py:515
  13.2 3.4 %shard_map.139 = bf16[32,16,2048]{2,1,0:T(8,128)(2,1)} custom-call(s32[2,256]{1,0:T(2,128)} %bitcast.69, bf16[256,2048]{1,0:T(8,128)(2,1)} %rows_ref.3), custom_call_target="tpu_custom_call" | custom-call | flops 536870912 | bytes 3145728 | tf_op jit(solution)/shard_map/pallas_call | solution.py:140
  16.6 23.1 %all-to-all-done = bf16[32,16,2048]{2,1,0:T(8,128)(2,1)S(1)} async-done(((bf16[32,16,2048]{2,1,0:T(8,128)(2,1)}), bf16[32,16,2048]{2,1,0:T(8,128)(2,1)S(1)}, u32[]{:S(2)}, u32[]{:S(2)}) %all-to-all-start) | async-done | bytes 2097184 | tf_op jit(solution)/shard_map/all_to_all | solution.py:515
  39.8 6.7 %all-to-all-start.2 = ((bf16[32,16,2048]{2,1,0:T(8,128)(2,1)}), bf16[32,16,2048]{2,1,0:T(8,128)(2,1)}, u32[]{:S(2)}, u32[]{:S(2)}) async-start(bf16[32,16,2048]{2,1,0:T(8,128)(2,1)} %shard_map.139), calls=%async_computation.2 | async-start | bytes 4194304 | tf_op jit(solution)/shard_map/all_to_all | solution.py:515
  46.4 15.9 %fusion.24 = bf16[512,2048]{1,0:T(8,128)(2,1)} fusion(bf16[1,2048,2048]{2,1,0:T(8,128)(2,1)} %param.15, bf16[512,2048]{1,0:T(8,128)(2,1)S(1)} %bitcast.65, bf16[1,2048,2048]{2,1,0:T(8,128)(2,1)} %param.14), kind=kOutput, calls=%fused_computation.26 | convolution fusion | flops 8600420352 | bytes 20971520 | tf_op jit(solution)/shard_map/dot_general | solution.py:533
  62.4 3.3 %reshape.247 = bf16[32,16,2,1024]{3,2,1,0:T(2,128)(2,1)S(1)} reshape(bf16[512,2048]{1,0:T(8,128)(2,1)} %fusion.24) | data formatting | bytes 4194304 | tf_op jit(solution)/shard_map/reshape | solution.py:534
  67.7 4.6 %all-to-all-done.2 = bf16[32,16,2048]{2,1,0:T(8,128)(2,1)} async-done(((bf16[32,16,2048]{2,1,0:T(8,128)(2,1)}), bf16[32,16,2048]{2,1,0:T(8,128)(2,1)}, u32[]{:S(2)}, u32[]{:S(2)}) %all-to-all-start.2) | async-done | bytes 2097184 | tf_op jit(solution)/shard_map/all_to_all | solution.py:515
  72.2 8.7 %all-to-all-start.1 = ((bf16[64,16,1024]{2,1,0:T(8,128)(2,1)}), bf16[64,16,1024]{2,1,0:T(8,128)(2,1)}, u32[]{:S(2)}, u32[]{:S(2)}) async-start(bf16[64,16,1024]{2,1,0:T(8,128)(2,1)} %bitcast.12), calls=%async_computation.1 | async-start | bytes 4194304 | tf_op jit(solution)/shard_map/all_to_all | solution.py:536
  80.9 16.6 %fusion.27 = bf16[512,2048]{1,0:T(8,128)(2,1)} fusion(bf16[1,2048,2048]{2,1,0:T(8,128)(2,1)} %param.15, bf16[512,2048]{1,0:T(8,128)(2,1)} %bitcast.16, bf16[1,2048,2048]{2,1,0:T(8,128)(2,1)} %param.14), kind=kOutput, calls=%fused_computation.27 | convolution fusion | flops 8600420352 | bytes 20971520 | tf_op jit(solution)/shard_map/dot_general | solution.py:533
  97.5 3.3 %reshape.251 = bf16[32,16,2,1024]{3,2,1,0:T(2,128)(2,1)S(1)} reshape(bf16[512,2048]{1,0:T(8,128)(2,1)} %fusion.27) | data formatting | bytes 4194304 | tf_op jit(solution)/shard_map/reshape | solution.py:534
  100.8 2.0 copy.25
  102.8 3.5 %all-to-all-done.1 = bf16[64,16,1024]{2,1,0:T(8,128)(2,1)} async-done(((bf16[64,16,1024]{2,1,0:T(8,128)(2,1)}), bf16[64,16,1024]{2,1,0:T(8,128)(2,1)}, u32[]{:S(2)}, u32[]{:S(2)}) %all-to-all-start.1) | async-done | bytes 2097184 | tf_op jit(solution)/shard_map/all_to_all | solution.py:536
  106.4 8.0 %all-to-all-start.3 = ((bf16[64,16,1024]{2,1,0:T(8,128)(2,1)}), bf16[64,16,1024]{2,1,0:T(8,128)(2,1)S(1)}, u32[]{:S(2)}, u32[]{:S(2)}) async-start(bf16[64,16,1024]{2,1,0:T(8,128)(2,1)} %bitcast.18), calls=%async_computation.3 | async-start | bytes 4194304 | tf_op jit(solution)/shard_map/all_to_all | solution.py:536
  115.2 2.4 fusion.62
  117.6 3.4 %convolution_add_fusion.2 = f32[256,1024]{1,0:T(8,128)} fusion(f32[256,1024]{1,0:T(8,128)S(1)} %fusion.62, bf16[1024,1024]{1,0:T(8,128)(2,1)} %bitcast.13, f32[256]{0:T(256)S(1)} %multiply_divide_fusion, f32[256]{0:T(256)S(1)} %get-tuple-element.50, s32[1024]{0:T(1024)S(1)} %fusion.76, s32[256]{0:T(256)S(1)} %bitcast.83, s32[256]{0:T(256)S(1)} %bitcast.81), kind=kOutput, calls=%fused_computation.38 | convolution fusion | flops 539492352 | bytes 4202496 | tf_op jit(solution)/shard_map/dot_general | solution.py:545
  121.0 19.7 %all-to-all-done.3 = bf16[64,16,1024]{2,1,0:T(8,128)(2,1)S(1)} async-done(((bf16[64,16,1024]{2,1,0:T(8,128)(2,1)}), bf16[64,16,1024]{2,1,0:T(8,128)(2,1)S(1)}, u32[]{:S(2)}, u32[]{:S(2)}) %all-to-all-start.3) | async-done | bytes 2097184 | tf_op jit(solution)/shard_map/all_to_all | solution.py:536
  140.7 2.1 convolution_add_fusion.1
  143.7 2.6 %collective-permute-start = (bf16[128,1024]{1,0:T(8,128)(2,1)S(1)}, bf16[128,1024]{1,0:T(8,128)(2,1)S(1)}, u32[]{:S(2)}, u32[]{:S(2)}) collective-permute-start(bf16[128,1024]{1,0:T(8,128)(2,1)S(1)} %get-tuple-element.31), channel_id=1, source_target_pairs={{0,1},{1,0},{2,3},{3,2},{4,5},{5,4},{6,7},{7,6},{8,9},{9,8},{10,11... | collective-permute-start | bytes 786440 | tf_op jit(solution)/shard_map/ppermute | solution.py:19
  146.4 3.4 %collective-permute-start.1 = (f32[128,12]{1,0:T(8,128)S(1)}, f32[128,12]{1,0:T(8,128)S(1)}, u32[]{:S(2)}, u32[]{:S(2)}) collective-permute-start(f32[128,12]{1,0:T(8,128)S(1)} %copy.26), channel_id=1, source_target_pairs={{0,64},{64,0},{1,65},{65,1},{2,66},{66,2},{3,67},{67,3},{4,68},{68... | collective-permute-start | bytes 18440 | tf_op jit(solution)/shard_map/ppermute | solution.py:19
  149.8 2.2 copy-done.1
  153.4 5.1 %shard_map.141 = (bf16[128,640]{1,0:T(8,128)(2,1)S(1)}, bf16[128,640]{1,0:T(8,128)(2,1)S(1)}, bf16[400,256]{1,0:T(8,128)(2,1)S(1)}, bf16[400,256]{1,0:T(8,128)(2,1)S(1)}) custom-call(s32[1]{0:T(128)} %bitcast.20.group_ref.place_ref, bf16[128,1024]{1,0:T(8,128)(2,1)S(1)} %collective-permute-done.taken_ref, f32[128,1024]{1,0:T(8,128)S(1)} %get-tuple-element.24.first_pre_ref, ...), custom_call_target="tpu_custom_call" | custom-call | flops 134217728 | bytes 524288 | tf_op jit(solution)/shard_map/pallas_call | solution.py:369
  158.6 2.6 %collective-permute-start.2 = (bf16[256,1024]{1,0:T(8,128)(2,1)S(1)}, bf16[256,1024]{1,0:T(8,128)(2,1)S(1)}, u32[]{:S(2)}, u32[]{:S(2)}) collective-permute-start(bf16[256,1024]{1,0:T(8,128)(2,1)S(1)} %constant_dynamic-update-slice_fusion.own_rows_ref), channel_id=1, source_target_pairs={{0,64},{64,0},{1,65},{65,1},{2,66},{66,2},{3,67},{67,3},{4,68},{68... | collective-permute-start | bytes 1572872 | tf_op jit(solution)/shard_map/ppermute | solution.py:19
  162.3 2.4 collective-permute-start.5
  164.8 3.3 %collective-permute-done.3.from_part_ref = bf16[128,640]{1,0:T(8,128)(2,1)S(1)} collective-permute-done((bf16[128,640]{1,0:T(8,128)(2,1)S(1)}, bf16[128,640]{1,0:T(8,128)(2,1)S(1)}, u32[]{:S(2)}, u32[]{:S(2)}) %collective-permute-start.3) | collective-permute-done | bytes 163872 | tf_op jit(solution)/shard_map/ppermute | solution.py:19
  168.1 4.1 %collective-permute-done.5.from_far_ref = bf16[128,640]{1,0:T(8,128)(2,1)S(1)} collective-permute-done((bf16[128,640]{1,0:T(8,128)(2,1)S(1)}, bf16[128,640]{1,0:T(8,128)(2,1)S(1)}, u32[]{:S(2)}, u32[]{:S(2)}) %collective-permute-start.5) | collective-permute-done | bytes 163872 | tf_op jit(solution)/shard_map/ppermute | solution.py:558
  173.2 24.5 %all_to_all.30 = bf16[32,40,512]{2,1,0:T(8,128)(2,1)S(1)} all-to-all(bf16[32,40,512]{2,1,0:T(8,128)(2,1)S(1)} %shard_map.142), channel_id=1, replica_groups=mesh['grp'=2,'ep'=32,'mp'=2] {'ep'}, dimensions={0} | all-to-all | bytes 2621440 | tf_op jit(solution)/shard_map/all_to_all | solution.py:568
  198.1 38.8 %all_to_all.31 = bf16[64,40,512]{2,1,0:T(8,128)(2,1)S(1)} all-to-all(bf16[64,40,512]{2,1,0:T(8,128)(2,1)S(1)} %broadcast_in_dim.60), channel_id=1, replica_groups=mesh['grp'=2,'ep'=32,'mp'=2] {'ep','mp'}, dimensions={0} | all-to-all | bytes 5242880 | tf_op jit(solution)/shard_map/all_to_all | solution.py:571
  236.8 3.0 %collective-permute-start.7 = (bf16[64,40,512]{2,1,0:T(8,128)(2,1)S(1)}, bf16[64,40,512]{2,1,0:T(8,128)(2,1)}, u32[]{:S(2)}, u32[]{:S(2)}) collective-permute-start(bf16[64,40,512]{2,1,0:T(8,128)(2,1)S(1)} %all_to_all.31), channel_id=1, source_target_pairs={{0,64},{64,0},{1,65},{65,1},{2,66},{66,2},{3,67},{67,3},{4,68},{68... | collective-permute-start | bytes 7864328 | tf_op jit(solution)/shard_map/ppermute | solution.py:19
  239.8 2.6 %shard_map.143 = (f32[2,1024,1024]{2,1,0:T(8,128)}, f32[2,2,192,256]{3,2,1,0:T(8,128)}, f32[2,24,2048]{2,1,0:T(8,128)}, f32[6,256]{1,0:T(8,128)S(1)}) custom-call(s32[1]{0:T(128)} %bitcast.20.group_ref.place_ref, bf16[32,2,40,512]{3,2,1,0:T(8,128)(2,1)S(1)} %bitcast.60), custom_call_target="tpu_custom_call" | custom-call | flops 1310720 | bytes 7408640 | tf_op jit(solution)/shard_map/pallas_call | solution.py:82
  242.5 2.0 collective-permute-done.7
  244.5 4.5 %shard_map.144 = (f32[2,1024,1024]{2,1,0:T(8,128)}, f32[2,2,192,256]{3,2,1,0:T(8,128)}, f32[2,24,2048]{2,1,0:T(8,128)}, f32[6,256]{1,0:T(8,128)}) custom-call(s32[1]{0:T(128)} %bitcast.place_ref, bf16[32,2,40,512]{3,2,1,0:T(8,128)(2,1)} %bitcast.23.half_ref, ...), custom_call_target="tpu_custom_call", output_to_operand_aliasing={{0}: (3, {}), {1}: (4, {}), {2}: (5, {})} | custom-call | flops 1310720 | bytes 7408640 | tf_op jit(solution)/shard_map/pallas_call | solution.py:82
  (46 shorter events, 7.7 us)
Async XLA Ops:
  0.6 114.0 %copy-start = (bf16[2048,32]{0,1:T(8,128)(2,1)S(1)}, bf16[2048,32]{0,1:T(8,128)(2,1)}, u32[]{:S(2)}) copy-start(bf16[2048,32]{0,1:T(8,128)(2,1)} %param.13) | copy-start | bytes 393220
  4.0 35.7 %all-to-all-start = ((bf16[32,16,2048]{2,1,0:T(8,128)(2,1)}), bf16[32,16,2048]{2,1,0:T(8,128)(2,1)S(1)}, u32[]{:S(2)}, u32[]{:S(2)}) async-start(bf16[32,16,2048]{2,1,0:T(8,128)(2,1)} %shard_map.138), calls=%async_computation | async-start | bytes 4194304 | tf_op jit(solution)/shard_map/all_to_all | solution.py:515
  39.8 32.5 %all-to-all-start.2 = ((bf16[32,16,2048]{2,1,0:T(8,128)(2,1)}), bf16[32,16,2048]{2,1,0:T(8,128)(2,1)}, u32[]{:S(2)}, u32[]{:S(2)}) async-start(bf16[32,16,2048]{2,1,0:T(8,128)(2,1)} %shard_map.139), calls=%async_computation.2 | async-start | bytes 4194304 | tf_op jit(solution)/shard_map/all_to_all | solution.py:515
  72.2 34.1 %all-to-all-start.1 = ((bf16[64,16,1024]{2,1,0:T(8,128)(2,1)}), bf16[64,16,1024]{2,1,0:T(8,128)(2,1)}, u32[]{:S(2)}, u32[]{:S(2)}) async-start(bf16[64,16,1024]{2,1,0:T(8,128)(2,1)} %bitcast.12), calls=%async_computation.1 | async-start | bytes 4194304 | tf_op jit(solution)/shard_map/all_to_all | solution.py:536
  100.8 13.6 %copy-start.6 = (s32[256,2]{0,1:T(2,128)S(1)}, s32[256,2]{0,1:T(2,128)}, u32[]{:S(2)}) copy-start(s32[256,2]{0,1:T(2,128)} %param.12) | copy-start | bytes 6148
  100.8 13.8 %copy-start.5 = (bf16[256,2048]{1,0:T(8,128)(2,1)S(1)}, bf16[256,2048]{1,0:T(8,128)(2,1)}, u32[]{:S(2)}) copy-start(bf16[256,2048]{1,0:T(8,128)(2,1)} %rows_ref.3) | copy-start | bytes 3145732
  106.4 34.3 %all-to-all-start.3 = ((bf16[64,16,1024]{2,1,0:T(8,128)(2,1)}), bf16[64,16,1024]{2,1,0:T(8,128)(2,1)S(1)}, u32[]{:S(2)}, u32[]{:S(2)}) async-start(bf16[64,16,1024]{2,1,0:T(8,128)(2,1)} %bitcast.18), calls=%async_computation.3 | async-start | bytes 4194304 | tf_op jit(solution)/shard_map/all_to_all | solution.py:536
  142.7 3.6 %copy-start.7 = (s32[128,6]{0,1:T(8,128)S(1)}, s32[128,6]{0,1:T(8,128)}, u32[]{:S(2)}) copy-start(s32[128,6]{0,1:T(8,128)} %param.21) | copy-start | bytes 9220
  142.7 3.6 %copy-start.8 = (f32[128,6]{0,1:T(8,128)S(1)}, f32[128,6]{0,1:T(8,128)}, u32[]{:S(2)}) copy-start(f32[128,6]{0,1:T(8,128)} %param.20) | copy-start | bytes 9220
  142.7 7.1 %copy-start.2 = (bf16[6,128,256]{2,1,0:T(8,128)(2,1)S(1)}, bf16[6,128,256]{2,1,0:T(8,128)(2,1)}, u32[]{:S(2)}) copy-start(bf16[6,128,256]{2,1,0:T(8,128)(2,1)} %tower_ref.1) | copy-start | bytes 1179652
  142.8 7.1 %copy-start.3 = (bf16[2048,48]{0,1:T(8,128)(2,1)S(1)}, bf16[2048,48]{0,1:T(8,128)(2,1)}, u32[]{:S(2)}) copy-start(bf16[2048,48]{0,1:T(8,128)(2,1)} %param.17) | copy-start | bytes 589828
  143.6 9.8 %copy-start.4 = (bf16[6,256]{1,0:T(8,128)(2,1)S(1)}, bf16[6,256]{1,0:T(8,128)(2,1)}, u32[]{:S(2)}) copy-start(bf16[6,256]{1,0:T(8,128)(2,1)} %tower_out_ref.1) | copy-start | bytes 9220
  143.7 9.7 %collective-permute-start = (bf16[128,1024]{1,0:T(8,128)(2,1)S(1)}, bf16[128,1024]{1,0:T(8,128)(2,1)S(1)}, u32[]{:S(2)}, u32[]{:S(2)}) collective-permute-start(bf16[128,1024]{1,0:T(8,128)(2,1)S(1)} %get-tuple-element.31), channel_id=1, source_target_pairs={{0,1},{1,0},{2,3},{3,2},{4,5},{5,4},{6,7},{7,6},{8,9},{9,8},{10,11... | collective-permute-start | bytes 786440 | tf_op jit(solution)/shard_map/ppermute | solution.py:19
  146.4 6.9 %collective-permute-start.1 = (f32[128,12]{1,0:T(8,128)S(1)}, f32[128,12]{1,0:T(8,128)S(1)}, u32[]{:S(2)}, u32[]{:S(2)}) collective-permute-start(f32[128,12]{1,0:T(8,128)S(1)} %copy.26), channel_id=1, source_target_pairs={{0,64},{64,0},{1,65},{65,1},{2,66},{66,2},{3,67},{67,3},{4,68},{68... | collective-permute-start | bytes 18440 | tf_op jit(solution)/shard_map/ppermute | solution.py:19
  149.8 2.2 copy-start.1
  158.6 13.6 %collective-permute-start.2 = (bf16[256,1024]{1,0:T(8,128)(2,1)S(1)}, bf16[256,1024]{1,0:T(8,128)(2,1)S(1)}, u32[]{:S(2)}, u32[]{:S(2)}) collective-permute-start(bf16[256,1024]{1,0:T(8,128)(2,1)S(1)} %constant_dynamic-update-slice_fusion.own_rows_ref), channel_id=1, source_target_pairs={{0,64},{64,0},{1,65},{65,1},{2,66},{66,2},{3,67},{67,3},{4,68},{68... | collective-permute-start | bytes 1572872 | tf_op jit(solution)/shard_map/ppermute | solution.py:19
  161.1 11.0 %collective-permute-start.6 = (bf16[400,256]{1,0:T(8,128)(2,1)S(1)}, bf16[400,256]{1,0:T(8,128)(2,1)S(1)}, u32[]{:S(2)}, u32[]{:S(2)}) collective-permute-start(bf16[400,256]{1,0:T(8,128)(2,1)S(1)} %get-tuple-element.35), channel_id=1, source_target_pairs={{0,64},{64,0},{1,65},{65,1},{2,66},{66,2},{3,67},{67,3},{4,68},{68... | collective-permute-start | bytes 614408 | tf_op jit(solution)/shard_map/ppermute | solution.py:19
  161.2 6.9 %collective-permute-start.3 = (bf16[128,640]{1,0:T(8,128)(2,1)S(1)}, bf16[128,640]{1,0:T(8,128)(2,1)S(1)}, u32[]{:S(2)}, u32[]{:S(2)}) collective-permute-start(bf16[128,640]{1,0:T(8,128)(2,1)S(1)} %get-tuple-element.32.mine_ref), channel_id=1, source_target_pairs={{0,1},{1,0},{2,3},{3,2},{4,5},{5,4},{6,7},{7,6},{8,9},{9,8},{10,11... | collective-permute-start | bytes 491528 | tf_op jit(solution)/shard_map/ppermute | solution.py:19
  162.3 9.8 %collective-permute-start.5 = (bf16[128,640]{1,0:T(8,128)(2,1)S(1)}, bf16[128,640]{1,0:T(8,128)(2,1)S(1)}, u32[]{:S(2)}, u32[]{:S(2)}) collective-permute-start(bf16[128,640]{1,0:T(8,128)(2,1)S(1)} %get-tuple-element.33), channel_id=1, source_target_pairs={{0,65},{1,64},{64,1},{65,0},{2,67},{3,66},{66,3},{67,2},{4,69},{5,... | collective-permute-start | bytes 491528 | tf_op jit(solution)/shard_map/ppermute | solution.py:558
  164.8 7.4 %collective-permute-start.4 = (bf16[128,640]{1,0:T(8,128)(2,1)S(1)}, bf16[128,640]{1,0:T(8,128)(2,1)S(1)}, u32[]{:S(2)}, u32[]{:S(2)}) collective-permute-start(bf16[128,640]{1,0:T(8,128)(2,1)S(1)} %get-tuple-element.33), channel_id=1, source_target_pairs={{0,64},{64,0},{1,65},{65,1},{2,66},{66,2},{3,67},{67,3},{4,68},{68... | collective-permute-start | bytes 491528 | tf_op jit(solution)/shard_map/ppermute | solution.py:19
  236.8 7.7 %collective-permute-start.7 = (bf16[64,40,512]{2,1,0:T(8,128)(2,1)S(1)}, bf16[64,40,512]{2,1,0:T(8,128)(2,1)}, u32[]{:S(2)}, u32[]{:S(2)}) collective-permute-start(bf16[64,40,512]{2,1,0:T(8,128)(2,1)S(1)} %all_to_all.31), channel_id=1, source_target_pairs={{0,64},{64,0},{1,65},{65,1},{2,66},{66,2},{3,67},{67,3},{4,68},{68... | collective-permute-start | bytes 7864328 | tf_op jit(solution)/shard_map/ppermute | solution.py:19

commit v6 on v5

--- a/solution.py
+++ b/solution.py
@@ -22,13 +22,14 @@
 def unpack_kernel(place_ref, half_ref, *refs):
     main_ref, tower_ref, gate_ref, vector_ref = refs[-4:]
     earlier_ref = refs[0] if len(refs) > 4 else None
-    blocks, parts, _, width = half_ref.shape
+    _, parts, _, width = half_ref.shape
+    blocks = gate_ref.shape[1]
     main_rows = main_ref.shape[1] // blocks
     tower_rows = tower_ref.shape[2] // blocks
     tower_width = tower_ref.shape[3]
     step = pl.program_id(0)
     for block in range(blocks):
-        values = [half_ref[block, part].astype(F32) for part in range(parts)]
+        values = [half_ref[step * blocks + block, part].astype(F32) for part in range(parts)]
         for part in range(parts):
             main_ref[part, block * main_rows : (block + 1) * main_rows, :] = values[part][
                 :main_rows
@@ -84,7 +85,7 @@
         grid_spec=pltpu.PrefetchScalarGridSpec(
             num_scalar_prefetch=1,
             grid=(outer // step_blocks,),
-            in_specs=[pl.BlockSpec((step_blocks, parts, each, width), lambda i, g: (i, 0, 0, 0))]
+            in_specs=[pl.BlockSpec(memory_space=pltpu.VMEM)]
             + ([pl.BlockSpec((6, tower_width), lambda i, g: (0, 0))] if filled else [])
             + [pl.BlockSpec(memory_space=pl.ANY)] * (len(filled) - 1),
             out_specs=[
@@ -539,10 +540,7 @@
         share = jnp.where(wide_place == first, weights[0], 0.0) + jnp.where(
             wide_place == second, weights[1], 0.0
         )
-        high = share.astype(BF16)
-        low = (share - high.astype(F32)).astype(BF16)
-        mixed = mixed + jnp.dot(high, returned, preferred_element_type=F32)
-        mixed = mixed + jnp.dot(low, returned, preferred_element_type=F32)
+        mixed = mixed + jnp.dot(share.astype(BF16), returned, preferred_element_type=F32)
     mixed = mixed.astype(BF16)
 
     half_rows = rows_dev // width_parts

time: 250 us -> 249 us (level)
  matrix products: 41.8 us -> 38.6 us
    dot_general x4 -> x2, matrix products: 8.7 us -> 5.44 us  [on_device(): jnp.dot(share.astype(BF16), returned, preferred_element_type=F32)]
  transfers between devices with their start and end apart: 12 -> 12, of which waited for: 7 -> 7; matrix products, arithmetic and copies ran while one was open for 20% -> 19% of each run, Pallas kernels for 3% -> 3%
where the time goes in v6:
time: 249 us; the launch traced here: 248 us
  blocking collectives  63.3 us (25%)
  waiting for transfers between devices  62.7 us (25%)
  starting transfers between devices  47.8 us (19%)
  matrix products  38.6 us (16%)
  Pallas kernels  21.2 us (9%)
  local copies, waits for them, and re-layouts  13.2 us (5%)
    all_to_all x1, blocking collectives, on_device(): lax.all_to_all(spread, CHIPS, split_axis=0, concat_axis=0, tiled=True)  38.8 us
    dot_general x2, matrix products, on_device(): partial = jnp.dot(inner, down_proj, preferred_element_type=F32).astype(BF16)  32.5 us
    all_to_all x2, waiting for transfers between devices, on_device(): lax.all_to_all(outgoing, 'ep', split_axis=0, concat_axis=0, tiled=True)  27.7 us
    all_to_all x2, waiting for transfers between devices, on_device(): lax.all_to_all(outgoing, CHIPS, split_axis=0, concat_axis=0, tiled=True)  25.6 us
    all_to_all x1, blocking collectives, on_device(): lax.all_to_all(packed, 'ep', split_axis=0, concat_axis=0, tiled=True)  24.5 us
    all_to_all x2, starting transfers between devices, on_device(): lax.all_to_all(outgoing, CHIPS, split_axis=0, concat_axis=0, tiled=True)  16.7 us
    all_to_all x2, starting transfers between devices, on_device(): lax.all_to_all(outgoing, 'ep', split_axis=0, concat_axis=0, tiled=True)  15.9 us
    ppermute x7, starting transfers between devices, swap(): return lax.ppermute(shard, axis, [(0, 1), (1, 0)])  12.7 us
  transfers between devices with their start and end apart: 12, of which 7 were waited for; matrix products, arithmetic and copies ran while one was open for 19% of the time, Pallas kernels for 3%

profile of v6, /device:TPU:1, one launch (start us, length us, event | category | flops | bytes accessed | tf_op | source)
XLA Modules:
  0.0 248.0 jit_solution(15261740948256216721)
XLA Ops:
  0.6 3.4 %shard_map.138 = bf16[32,16,2048]{2,1,0:T(8,128)(2,1)} custom-call(s32[2,256]{1,0:T(2,128)} %bitcast.65, bf16[256,2048]{1,0:T(8,128)(2,1)} %rows_ref.3), custom_call_target="tpu_custom_call" | custom-call | flops 536870912 | bytes 3145728 | tf_op jit(solution)/shard_map/pallas_call | solution.py:141
  4.0 9.2 %all-to-all-start = ((bf16[32,16,2048]{2,1,0:T(8,128)(2,1)}), bf16[32,16,2048]{2,1,0:T(8,128)(2,1)S(1)}, u32[]{:S(2)}, u32[]{:S(2)}) async-start(bf16[32,16,2048]{2,1,0:T(8,128)(2,1)} %shard_map.138), calls=%async_computation | async-start | bytes 4194304 | tf_op jit(solution)/shard_map/all_to_all | solution.py:516
  13.2 3.4 %shard_map.139 = bf16[32,16,2048]{2,1,0:T(8,128)(2,1)} custom-call(s32[2,256]{1,0:T(2,128)} %bitcast.66, bf16[256,2048]{1,0:T(8,128)(2,1)} %rows_ref.3), custom_call_target="tpu_custom_call" | custom-call | flops 536870912 | bytes 3145728 | tf_op jit(solution)/shard_map/pallas_call | solution.py:141
  16.6 23.1 %all-to-all-done = bf16[32,16,2048]{2,1,0:T(8,128)(2,1)S(1)} async-done(((bf16[32,16,2048]{2,1,0:T(8,128)(2,1)}), bf16[32,16,2048]{2,1,0:T(8,128)(2,1)S(1)}, u32[]{:S(2)}, u32[]{:S(2)}) %all-to-all-start) | async-done | bytes 2097184 | tf_op jit(solution)/shard_map/all_to_all | solution.py:516
  39.8 6.7 %all-to-all-start.2 = ((bf16[32,16,2048]{2,1,0:T(8,128)(2,1)}), bf16[32,16,2048]{2,1,0:T(8,128)(2,1)}, u32[]{:S(2)}, u32[]{:S(2)}) async-start(bf16[32,16,2048]{2,1,0:T(8,128)(2,1)} %shard_map.139), calls=%async_computation.2 | async-start | bytes 4194304 | tf_op jit(solution)/shard_map/all_to_all | solution.py:516
  46.4 15.9 %fusion.24 = bf16[512,2048]{1,0:T(8,128)(2,1)} fusion(bf16[1,2048,2048]{2,1,0:T(8,128)(2,1)} %param.15, bf16[512,2048]{1,0:T(8,128)(2,1)S(1)} %bitcast.62, bf16[1,2048,2048]{2,1,0:T(8,128)(2,1)} %param.14), kind=kOutput, calls=%fused_computation.26 | convolution fusion | flops 8600420352 | bytes 20971520 | tf_op jit(solution)/shard_map/dot_general | solution.py:534
  62.4 3.3 %reshape.247 = bf16[32,16,2,1024]{3,2,1,0:T(2,128)(2,1)S(1)} reshape(bf16[512,2048]{1,0:T(8,128)(2,1)} %fusion.24) | data formatting | bytes 4194304 | tf_op jit(solution)/shard_map/reshape | solution.py:535
  65.7 2.0 copy.24
  67.7 4.6 %all-to-all-done.2 = bf16[32,16,2048]{2,1,0:T(8,128)(2,1)} async-done(((bf16[32,16,2048]{2,1,0:T(8,128)(2,1)}), bf16[32,16,2048]{2,1,0:T(8,128)(2,1)}, u32[]{:S(2)}, u32[]{:S(2)}) %all-to-all-start.2) | async-done | bytes 2097184 | tf_op jit(solution)/shard_map/all_to_all | solution.py:516
  72.2 8.7 %all-to-all-start.1 = ((bf16[64,16,1024]{2,1,0:T(8,128)(2,1)}), bf16[64,16,1024]{2,1,0:T(8,128)(2,1)}, u32[]{:S(2)}, u32[]{:S(2)}) async-start(bf16[64,16,1024]{2,1,0:T(8,128)(2,1)} %bitcast.12), calls=%async_computation.1 | async-start | bytes 4194304 | tf_op jit(solution)/shard_map/all_to_all | solution.py:537
  80.9 16.6 %fusion.27 = bf16[512,2048]{1,0:T(8,128)(2,1)} fusion(bf16[1,2048,2048]{2,1,0:T(8,128)(2,1)} %param.15, bf16[512,2048]{1,0:T(8,128)(2,1)} %bitcast.16, bf16[1,2048,2048]{2,1,0:T(8,128)(2,1)} %param.14), kind=kOutput, calls=%fused_computation.27 | convolution fusion | flops 8600420352 | bytes 20971520 | tf_op jit(solution)/shard_map/dot_general | solution.py:534
  97.5 3.3 %reshape.251 = bf16[32,16,2,1024]{3,2,1,0:T(2,128)(2,1)S(1)} reshape(bf16[512,2048]{1,0:T(8,128)(2,1)} %fusion.27) | data formatting | bytes 4194304 | tf_op jit(solution)/shard_map/reshape | solution.py:535
  100.8 2.0 copy.25
  102.8 3.5 %all-to-all-done.1 = bf16[64,16,1024]{2,1,0:T(8,128)(2,1)} async-done(((bf16[64,16,1024]{2,1,0:T(8,128)(2,1)}), bf16[64,16,1024]{2,1,0:T(8,128)(2,1)}, u32[]{:S(2)}, u32[]{:S(2)}) %all-to-all-start.1) | async-done | bytes 2097184 | tf_op jit(solution)/shard_map/all_to_all | solution.py:537
  106.4 8.0 %all-to-all-start.3 = ((bf16[64,16,1024]{2,1,0:T(8,128)(2,1)}), bf16[64,16,1024]{2,1,0:T(8,128)(2,1)S(1)}, u32[]{:S(2)}, u32[]{:S(2)}) async-start(bf16[64,16,1024]{2,1,0:T(8,128)(2,1)} %bitcast.18), calls=%async_computation.3 | async-start | bytes 4194304 | tf_op jit(solution)/shard_map/all_to_all | solution.py:537
  115.2 3.4 %fusion.47 = f32[256,1024]{1,0:T(8,128)} fusion(bf16[1024,1024]{1,0:T(8,128)(2,1)} %bitcast.13, f32[256]{0:T(256)S(1)} %multiply_divide_fusion, f32[256]{0:T(256)S(1)} %get-tuple-element.50, s32[1024]{0:T(1024)S(1)} %fusion.70, s32[256]{0:T(256)S(1)} %bitcast.76, s32[256]{0:T(256)S(1)} %bitcast.75), kind=kOutput, calls=%fused_computation.40 | convolution fusion | flops 538443776 | bytes 3153920 | tf_op jit(solution)/shard_map/dot_general | solution.py:543
  118.6 22.1 %all-to-all-done.3 = bf16[64,16,1024]{2,1,0:T(8,128)(2,1)S(1)} async-done(((bf16[64,16,1024]{2,1,0:T(8,128)(2,1)}), bf16[64,16,1024]{2,1,0:T(8,128)(2,1)S(1)}, u32[]{:S(2)}, u32[]{:S(2)}) %all-to-all-start.3) | async-done | bytes 2097184 | tf_op jit(solution)/shard_map/all_to_all | solution.py:537
  140.7 2.1 fusion.46
  142.8 2.6 %collective-permute-start = (bf16[128,1024]{1,0:T(8,128)(2,1)S(1)}, bf16[128,1024]{1,0:T(8,128)(2,1)S(1)}, u32[]{:S(2)}, u32[]{:S(2)}) collective-permute-start(bf16[128,1024]{1,0:T(8,128)(2,1)S(1)} %get-tuple-element.31), channel_id=1, source_target_pairs={{0,1},{1,0},{2,3},{3,2},{4,5},{5,4},{6,7},{7,6},{8,9},{9,8},{10,11... | collective-permute-start | bytes 786440 | tf_op jit(solution)/shard_map/ppermute | solution.py:19
  145.5 3.4 %collective-permute-start.1 = (f32[128,12]{1,0:T(8,128)S(1)}, f32[128,12]{1,0:T(8,128)S(1)}, u32[]{:S(2)}, u32[]{:S(2)}) collective-permute-start(f32[128,12]{1,0:T(8,128)S(1)} %copy.26), channel_id=1, source_target_pairs={{0,64},{64,0},{1,65},{65,1},{2,66},{66,2},{3,67},{67,3},{4,68},{68... | collective-permute-start | bytes 18440 | tf_op jit(solution)/shard_map/ppermute | solution.py:19
  148.9 2.2 copy-done.1
  152.5 5.1 %shard_map.141 = (bf16[128,640]{1,0:T(8,128)(2,1)S(1)}, bf16[128,640]{1,0:T(8,128)(2,1)S(1)}, bf16[400,256]{1,0:T(8,128)(2,1)S(1)}, bf16[400,256]{1,0:T(8,128)(2,1)S(1)}) custom-call(s32[1]{0:T(128)} %bitcast.20.group_ref.place_ref, bf16[128,1024]{1,0:T(8,128)(2,1)S(1)} %collective-permute-done.taken_ref, f32[128,1024]{1,0:T(8,128)S(1)} %get-tuple-element.24.first_pre_ref, ...), custom_call_target="tpu_custom_call" | custom-call | flops 134217728 | bytes 524288 | tf_op jit(solution)/shard_map/pallas_call | solution.py:370
  157.7 2.6 %collective-permute-start.2 = (bf16[256,1024]{1,0:T(8,128)(2,1)S(1)}, bf16[256,1024]{1,0:T(8,128)(2,1)S(1)}, u32[]{:S(2)}, u32[]{:S(2)}) collective-permute-start(bf16[256,1024]{1,0:T(8,128)(2,1)S(1)} %constant_dynamic-update-slice_fusion.own_rows_ref), channel_id=1, source_target_pairs={{0,64},{64,0},{1,65},{65,1},{2,66},{66,2},{3,67},{67,3},{4,68},{68... | collective-permute-start | bytes 1572872 | tf_op jit(solution)/shard_map/ppermute | solution.py:19
  161.4 2.4 collective-permute-start.5
  163.9 3.3 %collective-permute-done.3.from_part_ref = bf16[128,640]{1,0:T(8,128)(2,1)S(1)} collective-permute-done((bf16[128,640]{1,0:T(8,128)(2,1)S(1)}, bf16[128,640]{1,0:T(8,128)(2,1)S(1)}, u32[]{:S(2)}, u32[]{:S(2)}) %collective-permute-start.3) | collective-permute-done | bytes 163872 | tf_op jit(solution)/shard_map/ppermute | solution.py:19
  167.2 4.1 %collective-permute-done.5.from_far_ref = bf16[128,640]{1,0:T(8,128)(2,1)S(1)} collective-permute-done((bf16[128,640]{1,0:T(8,128)(2,1)S(1)}, bf16[128,640]{1,0:T(8,128)(2,1)S(1)}, u32[]{:S(2)}, u32[]{:S(2)}) %collective-permute-start.5) | collective-permute-done | bytes 163872 | tf_op jit(solution)/shard_map/ppermute | solution.py:556
  172.3 24.5 %all_to_all.30 = bf16[32,40,512]{2,1,0:T(8,128)(2,1)S(1)} all-to-all(bf16[32,40,512]{2,1,0:T(8,128)(2,1)S(1)} %shard_map.142), channel_id=1, replica_groups=mesh['grp'=2,'ep'=32,'mp'=2] {'ep'}, dimensions={0} | all-to-all | bytes 2621440 | tf_op jit(solution)/shard_map/all_to_all | solution.py:566
  197.2 38.8 %all_to_all.31 = bf16[64,40,512]{2,1,0:T(8,128)(2,1)S(1)} all-to-all(bf16[64,40,512]{2,1,0:T(8,128)(2,1)S(1)} %broadcast_in_dim.60), channel_id=1, replica_groups=mesh['grp'=2,'ep'=32,'mp'=2] {'ep','mp'}, dimensions={0} | all-to-all | bytes 5242880 | tf_op jit(solution)/shard_map/all_to_all | solution.py:569
  236.0 3.0 %collective-permute-start.7 = (bf16[64,40,512]{2,1,0:T(8,128)(2,1)S(1)}, bf16[64,40,512]{2,1,0:T(8,128)(2,1)}, u32[]{:S(2)}, u32[]{:S(2)}) collective-permute-start(bf16[64,40,512]{2,1,0:T(8,128)(2,1)S(1)} %all_to_all.31), channel_id=1, source_target_pairs={{0,64},{64,0},{1,65},{65,1},{2,66},{66,2},{3,67},{67,3},{4,68},{68... | collective-permute-start | bytes 7864328 | tf_op jit(solution)/shard_map/ppermute | solution.py:19
  238.9 2.6 %shard_map.143 = (f32[2,1024,1024]{2,1,0:T(8,128)}, f32[2,2,192,256]{3,2,1,0:T(8,128)}, f32[2,24,2048]{2,1,0:T(8,128)}, f32[6,256]{1,0:T(8,128)S(1)}) custom-call(s32[1]{0:T(128)} %bitcast.20.group_ref.place_ref, bf16[32,2,40,512]{3,2,1,0:T(8,128)(2,1)S(1)} %bitcast.58), custom_call_target="tpu_custom_call" | custom-call | flops 1310720 | bytes 7408640 | tf_op jit(solution)/shard_map/pallas_call | solution.py:83
  241.6 2.0 collective-permute-done.7
  243.6 4.4 %shard_map.144 = (f32[2,1024,1024]{2,1,0:T(8,128)}, f32[2,2,192,256]{3,2,1,0:T(8,128)}, f32[2,24,2048]{2,1,0:T(8,128)}, f32[6,256]{1,0:T(8,128)}) custom-call(s32[1]{0:T(128)} %bitcast.place_ref, bf16[32,2,40,512]{3,2,1,0:T(8,128)(2,1)} %bitcast.23.half_ref, ...), custom_call_target="tpu_custom_call", output_to_operand_aliasing={{0}: (3, {}), {1}: (4, {}), {2}: (5, {})} | custom-call | flops 1310720 | bytes 7408640 | tf_op jit(solution)/shard_map/pallas_call | solution.py:83
  (44 shorter events, 4.8 us)
Async XLA Ops:
  0.6 114.0 %copy-start = (bf16[2048,32]{0,1:T(8,128)(2,1)S(1)}, bf16[2048,32]{0,1:T(8,128)(2,1)}, u32[]{:S(2)}) copy-start(bf16[2048,32]{0,1:T(8,128)(2,1)} %param.13) | copy-start | bytes 393220
  4.0 35.7 %all-to-all-start = ((bf16[32,16,2048]{2,1,0:T(8,128)(2,1)}), bf16[32,16,2048]{2,1,0:T(8,128)(2,1)S(1)}, u32[]{:S(2)}, u32[]{:S(2)}) async-start(bf16[32,16,2048]{2,1,0:T(8,128)(2,1)} %shard_map.138), calls=%async_computation | async-start | bytes 4194304 | tf_op jit(solution)/shard_map/all_to_all | solution.py:516
  39.8 32.5 %all-to-all-start.2 = ((bf16[32,16,2048]{2,1,0:T(8,128)(2,1)}), bf16[32,16,2048]{2,1,0:T(8,128)(2,1)}, u32[]{:S(2)}, u32[]{:S(2)}) async-start(bf16[32,16,2048]{2,1,0:T(8,128)(2,1)} %shard_map.139), calls=%async_computation.2 | async-start | bytes 4194304 | tf_op jit(solution)/shard_map/all_to_all | solution.py:516
  72.2 34.1 %all-to-all-start.1 = ((bf16[64,16,1024]{2,1,0:T(8,128)(2,1)}), bf16[64,16,1024]{2,1,0:T(8,128)(2,1)}, u32[]{:S(2)}, u32[]{:S(2)}) async-start(bf16[64,16,1024]{2,1,0:T(8,128)(2,1)} %bitcast.12), calls=%async_computation.1 | async-start | bytes 4194304 | tf_op jit(solution)/shard_map/all_to_all | solution.py:537
  100.8 13.6 %copy-start.6 = (s32[256,2]{0,1:T(2,128)S(1)}, s32[256,2]{0,1:T(2,128)}, u32[]{:S(2)}) copy-start(s32[256,2]{0,1:T(2,128)} %param.12) | copy-start | bytes 6148
  100.8 13.8 %copy-start.5 = (bf16[256,2048]{1,0:T(8,128)(2,1)S(1)}, bf16[256,2048]{1,0:T(8,128)(2,1)}, u32[]{:S(2)}) copy-start(bf16[256,2048]{1,0:T(8,128)(2,1)} %rows_ref.3) | copy-start | bytes 3145732
  106.4 34.3 %all-to-all-start.3 = ((bf16[64,16,1024]{2,1,0:T(8,128)(2,1)}), bf16[64,16,1024]{2,1,0:T(8,128)(2,1)S(1)}, u32[]{:S(2)}, u32[]{:S(2)}) async-start(bf16[64,16,1024]{2,1,0:T(8,128)(2,1)} %bitcast.18), calls=%async_computation.3 | async-start | bytes 4194304 | tf_op jit(solution)/shard_map/all_to_all | solution.py:537
  118.6 26.8 %copy-start.7 = (s32[128,6]{0,1:T(8,128)S(1)}, s32[128,6]{0,1:T(8,128)}, u32[]{:S(2)}) copy-start(s32[128,6]{0,1:T(8,128)} %param.21) | copy-start | bytes 9220
  118.6 26.8 %copy-start.8 = (f32[128,6]{0,1:T(8,128)S(1)}, f32[128,6]{0,1:T(8,128)}, u32[]{:S(2)}) copy-start(f32[128,6]{0,1:T(8,128)} %param.20) | copy-start | bytes 9220
  118.6 30.3 %copy-start.2 = (bf16[6,128,256]{2,1,0:T(8,128)(2,1)S(1)}, bf16[6,128,256]{2,1,0:T(8,128)(2,1)}, u32[]{:S(2)}) copy-start(bf16[6,128,256]{2,1,0:T(8,128)(2,1)} %tower_ref.1) | copy-start | bytes 1179652
  118.6 30.3 %copy-start.3 = (bf16[2048,48]{0,1:T(8,128)(2,1)S(1)}, bf16[2048,48]{0,1:T(8,128)(2,1)}, u32[]{:S(2)}) copy-start(bf16[2048,48]{0,1:T(8,128)(2,1)} %param.17) | copy-start | bytes 589828
  142.7 9.8 %copy-start.4 = (bf16[6,256]{1,0:T(8,128)(2,1)S(1)}, bf16[6,256]{1,0:T(8,128)(2,1)}, u32[]{:S(2)}) copy-start(bf16[6,256]{1,0:T(8,128)(2,1)} %tower_out_ref.1) | copy-start | bytes 9220
  142.8 9.7 %collective-permute-start = (bf16[128,1024]{1,0:T(8,128)(2,1)S(1)}, bf16[128,1024]{1,0:T(8,128)(2,1)S(1)}, u32[]{:S(2)}, u32[]{:S(2)}) collective-permute-start(bf16[128,1024]{1,0:T(8,128)(2,1)S(1)} %get-tuple-element.31), channel_id=1, source_target_pairs={{0,1},{1,0},{2,3},{3,2},{4,5},{5,4},{6,7},{7,6},{8,9},{9,8},{10,11... | collective-permute-start | bytes 786440 | tf_op jit(solution)/shard_map/ppermute | solution.py:19
  145.5 6.9 %collective-permute-start.1 = (f32[128,12]{1,0:T(8,128)S(1)}, f32[128,12]{1,0:T(8,128)S(1)}, u32[]{:S(2)}, u32[]{:S(2)}) collective-permute-start(f32[128,12]{1,0:T(8,128)S(1)} %copy.26), channel_id=1, source_target_pairs={{0,64},{64,0},{1,65},{65,1},{2,66},{66,2},{3,67},{67,3},{4,68},{68... | collective-permute-start | bytes 18440 | tf_op jit(solution)/shard_map/ppermute | solution.py:19
  148.9 2.2 copy-start.1
  157.7 13.6 %collective-permute-start.2 = (bf16[256,1024]{1,0:T(8,128)(2,1)S(1)}, bf16[256,1024]{1,0:T(8,128)(2,1)S(1)}, u32[]{:S(2)}, u32[]{:S(2)}) collective-permute-start(bf16[256,1024]{1,0:T(8,128)(2,1)S(1)} %constant_dynamic-update-slice_fusion.own_rows_ref), channel_id=1, source_target_pairs={{0,64},{64,0},{1,65},{65,1},{2,66},{66,2},{3,67},{67,3},{4,68},{68... | collective-permute-start | bytes 1572872 | tf_op jit(solution)/shard_map/ppermute | solution.py:19
  160.2 11.0 %collective-permute-start.6 = (bf16[400,256]{1,0:T(8,128)(2,1)S(1)}, bf16[400,256]{1,0:T(8,128)(2,1)S(1)}, u32[]{:S(2)}, u32[]{:S(2)}) collective-permute-start(bf16[400,256]{1,0:T(8,128)(2,1)S(1)} %get-tuple-element.35), channel_id=1, source_target_pairs={{0,64},{64,0},{1,65},{65,1},{2,66},{66,2},{3,67},{67,3},{4,68},{68... | collective-permute-start | bytes 614408 | tf_op jit(solution)/shard_map/ppermute | solution.py:19
  160.3 6.9 %collective-permute-start.3 = (bf16[128,640]{1,0:T(8,128)(2,1)S(1)}, bf16[128,640]{1,0:T(8,128)(2,1)S(1)}, u32[]{:S(2)}, u32[]{:S(2)}) collective-permute-start(bf16[128,640]{1,0:T(8,128)(2,1)S(1)} %get-tuple-element.32.mine_ref), channel_id=1, source_target_pairs={{0,1},{1,0},{2,3},{3,2},{4,5},{5,4},{6,7},{7,6},{8,9},{9,8},{10,11... | collective-permute-start | bytes 491528 | tf_op jit(solution)/shard_map/ppermute | solution.py:19
  161.4 9.8 %collective-permute-start.5 = (bf16[128,640]{1,0:T(8,128)(2,1)S(1)}, bf16[128,640]{1,0:T(8,128)(2,1)S(1)}, u32[]{:S(2)}, u32[]{:S(2)}) collective-permute-start(bf16[128,640]{1,0:T(8,128)(2,1)S(1)} %get-tuple-element.33), channel_id=1, source_target_pairs={{0,65},{1,64},{64,1},{65,0},{2,67},{3,66},{66,3},{67,2},{4,69},{5,... | collective-permute-start | bytes 491528 | tf_op jit(solution)/shard_map/ppermute | solution.py:556
  163.9 7.4 %collective-permute-start.4 = (bf16[128,640]{1,0:T(8,128)(2,1)S(1)}, bf16[128,640]{1,0:T(8,128)(2,1)S(1)}, u32[]{:S(2)}, u32[]{:S(2)}) collective-permute-start(bf16[128,640]{1,0:T(8,128)(2,1)S(1)} %get-tuple-element.33), channel_id=1, source_target_pairs={{0,64},{64,0},{1,65},{65,1},{2,66},{66,2},{3,67},{67,3},{4,68},{68... | collective-permute-start | bytes 491528 | tf_op jit(solution)/shard_map/ppermute | solution.py:19
  236.0 7.6 %collective-permute-start.7 = (bf16[64,40,512]{2,1,0:T(8,128)(2,1)S(1)}, bf16[64,40,512]{2,1,0:T(8,128)(2,1)}, u32[]{:S(2)}, u32[]{:S(2)}) collective-permute-start(bf16[64,40,512]{2,1,0:T(8,128)(2,1)S(1)} %all_to_all.31), channel_id=1, source_target_pairs={{0,64},{64,0},{1,65},{65,1},{2,66},{66,2},{3,67},{67,3},{4,68},{68... | collective-permute-start | bytes 7864328 | tf_op jit(solution)/shard_map/ppermute | solution.py:19

commit v7 on v6

--- a/solution.py
+++ b/solution.py
@@ -11,7 +11,7 @@
 F32 = jnp.float32
 BF16 = jnp.bfloat16
 SLOT_CHUNKS = 2
-CHIPS = ("ep", "mp")
+CHIPS = ("mp", "ep")
 GATE_STEPS = 3
 
 
@@ -22,14 +22,14 @@
 def unpack_kernel(place_ref, half_ref, *refs):
     main_ref, tower_ref, gate_ref, vector_ref = refs[-4:]
     earlier_ref = refs[0] if len(refs) > 4 else None
-    _, parts, _, width = half_ref.shape
+    parts, _, _, width = half_ref.shape
     blocks = gate_ref.shape[1]
     main_rows = main_ref.shape[1] // blocks
     tower_rows = tower_ref.shape[2] // blocks
     tower_width = tower_ref.shape[3]
     step = pl.program_id(0)
     for block in range(blocks):
-        values = [half_ref[step * blocks + block, part].astype(F32) for part in range(parts)]
+        values = [half_ref[part, step * blocks + block].astype(F32) for part in range(parts)]
         for part in range(parts):
             main_ref[part, block * main_rows : (block + 1) * main_rows, :] = values[part][
                 :main_rows
@@ -104,7 +104,7 @@
         input_output_aliases={3 + i: i for i in range(len(filled) - 1)},
         cost_estimate=pl.CostEstimate(flops=half.size, bytes_accessed=size, transcendentals=0),
         compiler_params=pltpu.CompilerParams(vmem_limit_bytes=14 * 1024 * 1024),
-    )(place.astype(jnp.int32).reshape(1), half.reshape(outer, parts, each, width), *filled[3:], *filled[:3])
+    )(place.astype(jnp.int32).reshape(1), half.reshape(parts, outer, each, width), *filled[3:], *filled[:3])
 
 
 def dispatch_kernel(ids_ref, rows_ref, out_ref, target_ref, *, experts, first_slot):
@@ -526,14 +526,13 @@
     half_width = feature_dim // width_parts
     mixed = jnp.zeros((rows_dev, half_width), F32)
     wide_lane = jnp.arange(chips * chunk_slots, dtype=jnp.int32)[None, :]
-    wide_expert = wide_lane // (width_parts * chunk_slots)
-    wide_place = wide_expert * chunk_slots + wide_lane % chunk_slots
+    wide_place = wide_lane % (expert_total * chunk_slots)
     for chunk in range(SLOT_CHUNKS):
         rows_in = received[chunk].reshape(expert_total * chunk_slots, feature_dim)
         inner = jax.nn.gelu(jnp.dot(rows_in, up_proj, preferred_element_type=F32)).astype(BF16)
         partial = jnp.dot(inner, down_proj, preferred_element_type=F32).astype(BF16)
         outgoing = partial.reshape(expert_total, chunk_slots, width_parts, half_width)
-        outgoing = outgoing.transpose(0, 2, 1, 3).reshape(chips, chunk_slots, half_width)
+        outgoing = outgoing.transpose(2, 0, 1, 3).reshape(chips, chunk_slots, half_width)
         returned = lax.all_to_all(outgoing, CHIPS, split_axis=0, concat_axis=0, tiled=True)
         returned = returned.reshape(chips * chunk_slots, half_width)
         first, second = targets[chunk]

time: 249 us -> 248 us (level)
  starting transfers between devices: 47.8 us -> 45.3 us
where the time goes in v7:
time: 248 us; the launch traced here: 247 us
  waiting for transfers between devices  64.9 us (26%)
  blocking collectives  62.9 us (25%)
  starting transfers between devices  45.3 us (18%)
  matrix products  38.6 us (16%)
  Pallas kernels  21.2 us (9%)
  local copies, waits for them, and re-layouts  13.1 us (5%)
    all_to_all x1, blocking collectives, on_device(): lax.all_to_all(spread, CHIPS, split_axis=0, concat_axis=0, tiled=True)  39 us
    dot_general x2, matrix products, on_device(): partial = jnp.dot(inner, down_proj, preferred_element_type=F32).astype(BF16)  32.5 us
    all_to_all x2, waiting for transfers between devices, on_device(): lax.all_to_all(outgoing, 'ep', split_axis=0, concat_axis=0, tiled=True)  27.7 us
    all_to_all x2, waiting for transfers between devices, on_device(): lax.all_to_all(outgoing, CHIPS, split_axis=0, concat_axis=0, tiled=True)  27.7 us
    all_to_all x1, blocking collectives, on_device(): lax.all_to_all(packed, 'ep', split_axis=0, concat_axis=0, tiled=True)  24 us
    all_to_all x2, starting transfers between devices, on_device(): lax.all_to_all(outgoing, 'ep', split_axis=0, concat_axis=0, tiled=True)  15.9 us
    all_to_all x2, starting transfers between devices, on_device(): lax.all_to_all(outgoing, CHIPS, split_axis=0, concat_axis=0, tiled=True)  14.9 us
    ppermute x7, starting transfers between devices, swap(): return lax.ppermute(shard, axis, [(0, 1), (1, 0)])  11.2 us
  transfers between devices with their start and end apart: 12, of which 7 were waited for; matrix products, arithmetic and copies ran while one was open for 19% of the time, Pallas kernels for 3%

profile of v7, /device:TPU:1, one launch (start us, length us, event | category | flops | bytes accessed | tf_op | source)
XLA Modules:
  0.0 247.2 jit_solution(8345423253798603947)
XLA Ops:
  0.6 3.4 %shard_map.138 = bf16[32,16,2048]{2,1,0:T(8,128)(2,1)} custom-call(s32[2,256]{1,0:T(2,128)} %bitcast.65, bf16[256,2048]{1,0:T(8,128)(2,1)} %rows_ref.3), custom_call_target="tpu_custom_call" | custom-call | flops 536870912 | bytes 3145728 | tf_op jit(solution)/shard_map/pallas_call | solution.py:141
  4.0 9.2 %all-to-all-start = ((bf16[32,16,2048]{2,1,0:T(8,128)(2,1)}), bf16[32,16,2048]{2,1,0:T(8,128)(2,1)S(1)}, u32[]{:S(2)}, u32[]{:S(2)}) async-start(bf16[32,16,2048]{2,1,0:T(8,128)(2,1)} %shard_map.138), calls=%async_computation | async-start | bytes 4194304 | tf_op jit(solution)/shard_map/all_to_all | solution.py:516
  13.2 3.4 %shard_map.139 = bf16[32,16,2048]{2,1,0:T(8,128)(2,1)} custom-call(s32[2,256]{1,0:T(2,128)} %bitcast.66, bf16[256,2048]{1,0:T(8,128)(2,1)} %rows_ref.3), custom_call_target="tpu_custom_call" | custom-call | flops 536870912 | bytes 3145728 | tf_op jit(solution)/shard_map/pallas_call | solution.py:141
  16.6 23.1 %all-to-all-done = bf16[32,16,2048]{2,1,0:T(8,128)(2,1)S(1)} async-done(((bf16[32,16,2048]{2,1,0:T(8,128)(2,1)}), bf16[32,16,2048]{2,1,0:T(8,128)(2,1)S(1)}, u32[]{:S(2)}, u32[]{:S(2)}) %all-to-all-start) | async-done | bytes 2097184 | tf_op jit(solution)/shard_map/all_to_all | solution.py:516
  39.8 6.7 %all-to-all-start.2 = ((bf16[32,16,2048]{2,1,0:T(8,128)(2,1)}), bf16[32,16,2048]{2,1,0:T(8,128)(2,1)}, u32[]{:S(2)}, u32[]{:S(2)}) async-start(bf16[32,16,2048]{2,1,0:T(8,128)(2,1)} %shard_map.139), calls=%async_computation.2 | async-start | bytes 4194304 | tf_op jit(solution)/shard_map/all_to_all | solution.py:516
  46.4 15.9 %fusion.24 = bf16[512,2048]{1,0:T(8,128)(2,1)} fusion(bf16[1,2048,2048]{2,1,0:T(8,128)(2,1)} %param.15, bf16[512,2048]{1,0:T(8,128)(2,1)S(1)} %bitcast.62, bf16[1,2048,2048]{2,1,0:T(8,128)(2,1)} %param.14), kind=kOutput, calls=%fused_computation.26 | convolution fusion | flops 8600420352 | bytes 20971520 | tf_op jit(solution)/shard_map/dot_general | solution.py:533
  62.4 3.3 %reshape.207 = bf16[32,16,2,1024]{3,2,1,0:T(2,128)(2,1)S(1)} reshape(bf16[512,2048]{1,0:T(8,128)(2,1)} %fusion.24) | data formatting | bytes 4194304 | tf_op jit(solution)/shard_map/reshape | solution.py:534
  65.7 2.0 copy.24
  67.7 4.6 %all-to-all-done.2 = bf16[32,16,2048]{2,1,0:T(8,128)(2,1)} async-done(((bf16[32,16,2048]{2,1,0:T(8,128)(2,1)}), bf16[32,16,2048]{2,1,0:T(8,128)(2,1)}, u32[]{:S(2)}, u32[]{:S(2)}) %all-to-all-start.2) | async-done | bytes 2097184 | tf_op jit(solution)/shard_map/all_to_all | solution.py:516
  72.2 8.7 %all-to-all-start.1 = ((bf16[64,16,1024]{2,1,0:T(8,128)(2,1)}), bf16[64,16,1024]{2,1,0:T(8,128)(2,1)}, u32[]{:S(2)}, u32[]{:S(2)}) async-start(bf16[64,16,1024]{2,1,0:T(8,128)(2,1)} %bitcast.12), calls=%async_computation.1 | async-start | bytes 4194304 | tf_op jit(solution)/shard_map/all_to_all | solution.py:536
  80.9 16.6 %fusion.27 = bf16[512,2048]{1,0:T(8,128)(2,1)} fusion(bf16[1,2048,2048]{2,1,0:T(8,128)(2,1)} %param.15, bf16[512,2048]{1,0:T(8,128)(2,1)} %bitcast.16, bf16[1,2048,2048]{2,1,0:T(8,128)(2,1)} %param.14), kind=kOutput, calls=%fused_computation.27 | convolution fusion | flops 8600420352 | bytes 20971520 | tf_op jit(solution)/shard_map/dot_general | solution.py:533
  97.5 3.3 %reshape.211 = bf16[32,16,2,1024]{3,2,1,0:T(2,128)(2,1)S(1)} reshape(bf16[512,2048]{1,0:T(8,128)(2,1)} %fusion.27) | data formatting | bytes 4194304 | tf_op jit(solution)/shard_map/reshape | solution.py:534
  100.8 2.0 copy.25
  102.8 4.8 %all-to-all-done.1 = bf16[64,16,1024]{2,1,0:T(8,128)(2,1)} async-done(((bf16[64,16,1024]{2,1,0:T(8,128)(2,1)}), bf16[64,16,1024]{2,1,0:T(8,128)(2,1)}, u32[]{:S(2)}, u32[]{:S(2)}) %all-to-all-start.1) | async-done | bytes 2097184 | tf_op jit(solution)/shard_map/all_to_all | solution.py:536
  107.6 6.2 %all-to-all-start.3 = ((bf16[64,16,1024]{2,1,0:T(8,128)(2,1)}), bf16[64,16,1024]{2,1,0:T(8,128)(2,1)S(1)}, u32[]{:S(2)}, u32[]{:S(2)}) async-start(bf16[64,16,1024]{2,1,0:T(8,128)(2,1)} %bitcast.18), calls=%async_computation.3 | async-start | bytes 4194304 | tf_op jit(solution)/shard_map/all_to_all | solution.py:536
  114.7 3.4 %fusion.47 = f32[256,1024]{1,0:T(8,128)} fusion(bf16[1024,1024]{1,0:T(8,128)(2,1)} %bitcast.13, f32[256]{0:T(256)S(1)} %multiply_divide_fusion, f32[256]{0:T(256)S(1)} %get-tuple-element.50, s32[1024]{0:T(1024)S(1)} %add_select_fusion, s32[256]{0:T(256)S(1)} %bitcast.76, s32[256]{0:T(256)S(1)} %bitcast.75), kind=kOutput, calls=%fused_computation.40 | convolution fusion | flops 538443776 | bytes 3153920 | tf_op jit(solution)/shard_map/dot_general | solution.py:542
  118.1 22.9 %all-to-all-done.3 = bf16[64,16,1024]{2,1,0:T(8,128)(2,1)S(1)} async-done(((bf16[64,16,1024]{2,1,0:T(8,128)(2,1)}), bf16[64,16,1024]{2,1,0:T(8,128)(2,1)S(1)}, u32[]{:S(2)}, u32[]{:S(2)}) %all-to-all-start.3) | async-done | bytes 2097184 | tf_op jit(solution)/shard_map/all_to_all | solution.py:536
  141.0 2.1 fusion.46
  143.5 4.3 %collective-permute-start.1 = (f32[128,12]{1,0:T(8,128)S(1)}, f32[128,12]{1,0:T(8,128)S(1)}, u32[]{:S(2)}, u32[]{:S(2)}) collective-permute-start(f32[128,12]{1,0:T(8,128)S(1)} %copy.26), channel_id=1, source_target_pairs={{0,64},{64,0},{1,65},{65,1},{2,66},{66,2},{3,67},{67,3},{4,68},{68... | collective-permute-start | bytes 18440 | tf_op jit(solution)/shard_map/ppermute | solution.py:19
  147.7 2.2 copy-done.1
  149.9 1.3 shard_map.140
  151.3 5.1 %shard_map.141 = (bf16[128,640]{1,0:T(8,128)(2,1)S(1)}, bf16[128,640]{1,0:T(8,128)(2,1)S(1)}, bf16[400,256]{1,0:T(8,128)(2,1)S(1)}, bf16[400,256]{1,0:T(8,128)(2,1)S(1)}) custom-call(s32[1]{0:T(128)} %bitcast.20.group_ref.place_ref, bf16[128,1024]{1,0:T(8,128)(2,1)S(1)} %collective-permute-done.taken_ref, f32[128,1024]{1,0:T(8,128)S(1)} %get-tuple-element.24.first_pre_ref, ...), custom_call_target="tpu_custom_call" | custom-call | flops 134217728 | bytes 524288 | tf_op jit(solution)/shard_map/pallas_call | solution.py:370
  156.5 3.4 %collective-permute-start.2 = (bf16[256,1024]{1,0:T(8,128)(2,1)S(1)}, bf16[256,1024]{1,0:T(8,128)(2,1)S(1)}, u32[]{:S(2)}, u32[]{:S(2)}) collective-permute-start(bf16[256,1024]{1,0:T(8,128)(2,1)S(1)} %constant_dynamic-update-slice_fusion.own_rows_ref), channel_id=1, source_target_pairs={{0,64},{64,0},{1,65},{65,1},{2,66},{66,2},{3,67},{67,3},{4,68},{68... | collective-permute-start | bytes 1572872 | tf_op jit(solution)/shard_map/ppermute | solution.py:19
  160.3 3.3 %collective-permute-start.5 = (bf16[128,640]{1,0:T(8,128)(2,1)S(1)}, bf16[128,640]{1,0:T(8,128)(2,1)S(1)}, u32[]{:S(2)}, u32[]{:S(2)}) collective-permute-start(bf16[128,640]{1,0:T(8,128)(2,1)S(1)} %get-tuple-element.33), channel_id=1, source_target_pairs={{0,65},{1,64},{64,1},{65,0},{2,67},{3,66},{66,3},{67,2},{4,69},{5,... | collective-permute-start | bytes 491528 | tf_op jit(solution)/shard_map/ppermute | solution.py:555
  163.6 3.2 %collective-permute-done.3.from_part_ref = bf16[128,640]{1,0:T(8,128)(2,1)S(1)} collective-permute-done((bf16[128,640]{1,0:T(8,128)(2,1)S(1)}, bf16[128,640]{1,0:T(8,128)(2,1)S(1)}, u32[]{:S(2)}, u32[]{:S(2)}) %collective-permute-start.3) | collective-permute-done | bytes 163872 | tf_op jit(solution)/shard_map/ppermute | solution.py:19
  166.8 4.1 %collective-permute-done.5.from_far_ref = bf16[128,640]{1,0:T(8,128)(2,1)S(1)} collective-permute-done((bf16[128,640]{1,0:T(8,128)(2,1)S(1)}, bf16[128,640]{1,0:T(8,128)(2,1)S(1)}, u32[]{:S(2)}, u32[]{:S(2)}) %collective-permute-start.5) | collective-permute-done | bytes 163872 | tf_op jit(solution)/shard_map/ppermute | solution.py:555
  171.9 24.0 %all_to_all.30 = bf16[32,40,512]{2,1,0:T(8,128)(2,1)S(1)} all-to-all(bf16[32,40,512]{2,1,0:T(8,128)(2,1)S(1)} %shard_map.142), channel_id=1, replica_groups=mesh['grp'=2,'ep'=32,'mp'=2] {'ep'}, dimensions={0} | all-to-all | bytes 2621440 | tf_op jit(solution)/shard_map/all_to_all | solution.py:565
  196.2 39.0 %all_to_all.31 = bf16[64,40,512]{2,1,0:T(8,128)(2,1)S(1)} all-to-all(bf16[64,40,512]{2,1,0:T(8,128)(2,1)S(1)} %broadcast_in_dim.60), channel_id=1, replica_groups=mesh['grp'=2,'ep'=32,'mp'=2] {'mp','ep'}, dimensions={0} | all-to-all | bytes 5242880 | tf_op jit(solution)/shard_map/all_to_all | solution.py:568
  235.2 2.9 %collective-permute-start.7 = (bf16[64,40,512]{2,1,0:T(8,128)(2,1)S(1)}, bf16[64,40,512]{2,1,0:T(8,128)(2,1)}, u32[]{:S(2)}, u32[]{:S(2)}) collective-permute-start(bf16[64,40,512]{2,1,0:T(8,128)(2,1)S(1)} %all_to_all.31), channel_id=1, source_target_pairs={{0,64},{64,0},{1,65},{65,1},{2,66},{66,2},{3,67},{67,3},{4,68},{68... | collective-permute-start | bytes 7864328 | tf_op jit(solution)/shard_map/ppermute | solution.py:19
  238.1 2.6 %shard_map.143 = (f32[2,1024,1024]{2,1,0:T(8,128)}, f32[2,2,192,256]{3,2,1,0:T(8,128)}, f32[2,24,2048]{2,1,0:T(8,128)}, f32[6,256]{1,0:T(8,128)S(1)}) custom-call(s32[1]{0:T(128)} %bitcast.20.group_ref.place_ref, bf16[2,32,40,512]{3,2,1,0:T(8,128)(2,1)S(1)} %bitcast.58), custom_call_target="tpu_custom_call" | custom-call | flops 1310720 | bytes 7408640 | tf_op jit(solution)/shard_map/pallas_call | solution.py:83
  240.7 2.0 collective-permute-done.7
  242.8 4.4 %shard_map.144 = (f32[2,1024,1024]{2,1,0:T(8,128)}, f32[2,2,192,256]{3,2,1,0:T(8,128)}, f32[2,24,2048]{2,1,0:T(8,128)}, f32[6,256]{1,0:T(8,128)}) custom-call(s32[1]{0:T(128)} %bitcast.place_ref, bf16[2,32,40,512]{3,2,1,0:T(8,128)(2,1)} %bitcast.23.half_ref, ...), custom_call_target="tpu_custom_call", output_to_operand_aliasing={{0}: (3, {}), {1}: (4, {}), {2}: (5, {})} | custom-call | flops 1310720 | bytes 7408640 | tf_op jit(solution)/shard_map/pallas_call | solution.py:83
  (44 shorter events, 2.9 us)
Async XLA Ops:
  0.6 113.5 %copy-start = (bf16[2048,32]{0,1:T(8,128)(2,1)S(1)}, bf16[2048,32]{0,1:T(8,128)(2,1)}, u32[]{:S(2)}) copy-start(bf16[2048,32]{0,1:T(8,128)(2,1)} %param.13) | copy-start | bytes 393220
  4.0 35.7 %all-to-all-start = ((bf16[32,16,2048]{2,1,0:T(8,128)(2,1)}), bf16[32,16,2048]{2,1,0:T(8,128)(2,1)S(1)}, u32[]{:S(2)}, u32[]{:S(2)}) async-start(bf16[32,16,2048]{2,1,0:T(8,128)(2,1)} %shard_map.138), calls=%async_computation | async-start | bytes 4194304 | tf_op jit(solution)/shard_map/all_to_all | solution.py:516
  39.8 32.5 %all-to-all-start.2 = ((bf16[32,16,2048]{2,1,0:T(8,128)(2,1)}), bf16[32,16,2048]{2,1,0:T(8,128)(2,1)}, u32[]{:S(2)}, u32[]{:S(2)}) async-start(bf16[32,16,2048]{2,1,0:T(8,128)(2,1)} %shard_map.139), calls=%async_computation.2 | async-start | bytes 4194304 | tf_op jit(solution)/shard_map/all_to_all | solution.py:516
  72.2 35.4 %all-to-all-start.1 = ((bf16[64,16,1024]{2,1,0:T(8,128)(2,1)}), bf16[64,16,1024]{2,1,0:T(8,128)(2,1)}, u32[]{:S(2)}, u32[]{:S(2)}) async-start(bf16[64,16,1024]{2,1,0:T(8,128)(2,1)} %bitcast.12), calls=%async_computation.1 | async-start | bytes 4194304 | tf_op jit(solution)/shard_map/all_to_all | solution.py:536
  100.8 13.1 %copy-start.6 = (s32[256,2]{0,1:T(2,128)S(1)}, s32[256,2]{0,1:T(2,128)}, u32[]{:S(2)}) copy-start(s32[256,2]{0,1:T(2,128)} %param.12) | copy-start | bytes 6148
  100.8 13.3 %copy-start.5 = (bf16[256,2048]{1,0:T(8,128)(2,1)S(1)}, bf16[256,2048]{1,0:T(8,128)(2,1)}, u32[]{:S(2)}) copy-start(bf16[256,2048]{1,0:T(8,128)(2,1)} %rows_ref.3) | copy-start | bytes 3145732
  107.6 33.3 %all-to-all-start.3 = ((bf16[64,16,1024]{2,1,0:T(8,128)(2,1)}), bf16[64,16,1024]{2,1,0:T(8,128)(2,1)S(1)}, u32[]{:S(2)}, u32[]{:S(2)}) async-start(bf16[64,16,1024]{2,1,0:T(8,128)(2,1)} %bitcast.18), calls=%async_computation.3 | async-start | bytes 4194304 | tf_op jit(solution)/shard_map/all_to_all | solution.py:536
  118.1 25.3 %copy-start.7 = (s32[128,6]{0,1:T(8,128)S(1)}, s32[128,6]{0,1:T(8,128)}, u32[]{:S(2)}) copy-start(s32[128,6]{0,1:T(8,128)} %param.21) | copy-start | bytes 9220
  118.1 25.3 %copy-start.8 = (f32[128,6]{0,1:T(8,128)S(1)}, f32[128,6]{0,1:T(8,128)}, u32[]{:S(2)}) copy-start(f32[128,6]{0,1:T(8,128)} %param.20) | copy-start | bytes 9220
  118.1 29.7 %copy-start.2 = (bf16[6,128,256]{2,1,0:T(8,128)(2,1)S(1)}, bf16[6,128,256]{2,1,0:T(8,128)(2,1)}, u32[]{:S(2)}) copy-start(bf16[6,128,256]{2,1,0:T(8,128)(2,1)} %tower_ref.1) | copy-start | bytes 1179652
  118.1 29.7 %copy-start.3 = (bf16[2048,48]{0,1:T(8,128)(2,1)S(1)}, bf16[2048,48]{0,1:T(8,128)(2,1)}, u32[]{:S(2)}) copy-start(bf16[2048,48]{0,1:T(8,128)(2,1)} %param.17) | copy-start | bytes 589828
  143.0 8.3 %copy-start.4 = (bf16[6,256]{1,0:T(8,128)(2,1)S(1)}, bf16[6,256]{1,0:T(8,128)(2,1)}, u32[]{:S(2)}) copy-start(bf16[6,256]{1,0:T(8,128)(2,1)} %tower_out_ref.1) | copy-start | bytes 9220
  143.1 8.2 %collective-permute-start = (bf16[128,1024]{1,0:T(8,128)(2,1)S(1)}, bf16[128,1024]{1,0:T(8,128)(2,1)S(1)}, u32[]{:S(2)}, u32[]{:S(2)}) collective-permute-start(bf16[128,1024]{1,0:T(8,128)(2,1)S(1)} %get-tuple-element.31), channel_id=1, source_target_pairs={{0,1},{1,0},{2,3},{3,2},{4,5},{5,4},{6,7},{7,6},{8,9},{9,8},{10,11... | collective-permute-start | bytes 786440 | tf_op jit(solution)/shard_map/ppermute | solution.py:19
  143.5 7.8 %collective-permute-start.1 = (f32[128,12]{1,0:T(8,128)S(1)}, f32[128,12]{1,0:T(8,128)S(1)}, u32[]{:S(2)}, u32[]{:S(2)}) collective-permute-start(f32[128,12]{1,0:T(8,128)S(1)} %copy.26), channel_id=1, source_target_pairs={{0,64},{64,0},{1,65},{65,1},{2,66},{66,2},{3,67},{67,3},{4,68},{68... | collective-permute-start | bytes 18440 | tf_op jit(solution)/shard_map/ppermute | solution.py:19
  147.7 2.2 copy-start.1
  156.5 14.4 %collective-permute-start.2 = (bf16[256,1024]{1,0:T(8,128)(2,1)S(1)}, bf16[256,1024]{1,0:T(8,128)(2,1)S(1)}, u32[]{:S(2)}, u32[]{:S(2)}) collective-permute-start(bf16[256,1024]{1,0:T(8,128)(2,1)S(1)} %constant_dynamic-update-slice_fusion.own_rows_ref), channel_id=1, source_target_pairs={{0,64},{64,0},{1,65},{65,1},{2,66},{66,2},{3,67},{67,3},{4,68},{68... | collective-permute-start | bytes 1572872 | tf_op jit(solution)/shard_map/ppermute | solution.py:19
  159.9 11.0 %collective-permute-start.6 = (bf16[400,256]{1,0:T(8,128)(2,1)S(1)}, bf16[400,256]{1,0:T(8,128)(2,1)S(1)}, u32[]{:S(2)}, u32[]{:S(2)}) collective-permute-start(bf16[400,256]{1,0:T(8,128)(2,1)S(1)} %get-tuple-element.35), channel_id=1, source_target_pairs={{0,64},{64,0},{1,65},{65,1},{2,66},{66,2},{3,67},{67,3},{4,68},{68... | collective-permute-start | bytes 614408 | tf_op jit(solution)/shard_map/ppermute | solution.py:19
  160.0 6.8 %collective-permute-start.3 = (bf16[128,640]{1,0:T(8,128)(2,1)S(1)}, bf16[128,640]{1,0:T(8,128)(2,1)S(1)}, u32[]{:S(2)}, u32[]{:S(2)}) collective-permute-start(bf16[128,640]{1,0:T(8,128)(2,1)S(1)} %get-tuple-element.32.mine_ref), channel_id=1, source_target_pairs={{0,1},{1,0},{2,3},{3,2},{4,5},{5,4},{6,7},{7,6},{8,9},{9,8},{10,11... | collective-permute-start | bytes 491528 | tf_op jit(solution)/shard_map/ppermute | solution.py:19
  160.3 10.6 %collective-permute-start.5 = (bf16[128,640]{1,0:T(8,128)(2,1)S(1)}, bf16[128,640]{1,0:T(8,128)(2,1)S(1)}, u32[]{:S(2)}, u32[]{:S(2)}) collective-permute-start(bf16[128,640]{1,0:T(8,128)(2,1)S(1)} %get-tuple-element.33), channel_id=1, source_target_pairs={{0,65},{1,64},{64,1},{65,0},{2,67},{3,66},{66,3},{67,2},{4,69},{5,... | collective-permute-start | bytes 491528 | tf_op jit(solution)/shard_map/ppermute | solution.py:555
  163.5 7.4 %collective-permute-start.4 = (bf16[128,640]{1,0:T(8,128)(2,1)S(1)}, bf16[128,640]{1,0:T(8,128)(2,1)S(1)}, u32[]{:S(2)}, u32[]{:S(2)}) collective-permute-start(bf16[128,640]{1,0:T(8,128)(2,1)S(1)} %get-tuple-element.33), channel_id=1, source_target_pairs={{0,64},{64,0},{1,65},{65,1},{2,66},{66,2},{3,67},{67,3},{4,68},{68... | collective-permute-start | bytes 491528 | tf_op jit(solution)/shard_map/ppermute | solution.py:19
  235.2 7.6 %collective-permute-start.7 = (bf16[64,40,512]{2,1,0:T(8,128)(2,1)S(1)}, bf16[64,40,512]{2,1,0:T(8,128)(2,1)}, u32[]{:S(2)}, u32[]{:S(2)}) collective-permute-start(bf16[64,40,512]{2,1,0:T(8,128)(2,1)S(1)} %all_to_all.31), channel_id=1, source_target_pairs={{0,64},{64,0},{1,65},{65,1},{2,66},{66,2},{3,67},{67,3},{4,68},{68... | collective-permute-start | bytes 7864328 | tf_op jit(solution)/shard_map/ppermute | solution.py:19
